TPU v7x, 256 devices: a whole 4x4x8 slice. The times are simulated.
256 devices in a mesh: dom: 256 (over y, x, z, core).
Axes of the slice: x: 4, y: 4, z: 8, core: 2. Of those that a mesh axis runs over, the one named last changes fastest.
Arguments:
- features: bfloat16 [1048576, 128], P('dom'), may hold values from -6 to 6
- local_tiles: bfloat16 [8192, 3, 128, 128], P('dom'), may hold values from 0 to 0.06982422
- local_src: int32 [8192, 3], P('dom'), may hold values from 0 to 31
- remote_tiles: bfloat16 [8192, 3, 128, 128], P('dom'), may hold values from 0 to 0.06982422
- remote_src: int32 [8192, 3], P('dom'), may hold values from 0 to 23, as said below
- send_blocks: int32 [1024, 4], P('dom'), may hold values from 0 to 31
- hub_rows: int32 [1024], P('dom'), may hold values from 0 to 4095
- w_self: bfloat16 [128, 256], replicated, may hold values from -0.5 to 0.5
- w_neigh: bfloat16 [128, 256], replicated, may hold values from -0.5 to 0.5
- bias: float32 [256], replicated, may hold values from -3 to 3
- d_hidden: bfloat16 [1048576, 256], P('dom'), may hold values from -24 to 24
Outputs:
- hidden: bfloat16 [1048576, 256], P('dom')
- grad_features: bfloat16 [1048576, 128], P('dom')
- grad_w_self: float32 [128, 256], P(None, 'dom')
- grad_w_neigh: float32 [128, 256], P(None, 'dom')
- grad_bias: float32 [256], P('dom')
Inputs may be any that keep to these rules, and one draw needn't show every extreme that they name: `local_src`: local tile sources index the partition's own row blocks. `remote_src`: remote tile sources index the partition's remote table; in each partition every halo block of the table is the source of at least one remote tile. `send_blocks`: blocks may repeat in a list. `hub_rows`: two hubs may name the same row.
All inputs are finite; a program needn't handle non-finite values.
Results may differ from a plain program's by a relative error of at most 0.0065.
Values may be sent and summed in bfloat16 or wider, within the bound.
No kernel may reach another device: no remote copies, remote signals or barrier semaphores. Data moves between devices by JAX's collectives and lax.ppermute only.
A program may use at most 128 MiB of HBM per device.

v0:
```python
import jax
import jax.numpy as jnp
from jax import lax
from jax.sharding import PartitionSpec as P

OFFSETS = (1, -1, 2, -2)


def shifted(block, axis, distance):
    devices = range(lax.axis_size(axis))
    route = [((i - distance) % len(devices), i) for i in devices]
    return lax.ppermute(block, axis, route)


def add_into(grid, index, update):
    return grid.at[index].add(update)


def shards(
    features,
    local_tiles,
    local_src,
    remote_tiles,
    remote_src,
    send_blocks,
    hub_rows,
    w_self,
    w_neigh,
    bias,
    d_hidden,
):
    node_count, width = features.shape
    tile = local_tiles.shape[-1]
    block_count = node_count // tile
    blocks = features.reshape(block_count, tile, width)
    hub_all = lax.all_gather(features[hub_rows], "dom", axis=0, tiled=True)
    received = []
    for j, step in enumerate(OFFSETS):
        received.append(shifted(blocks[send_blocks[j]], "dom", step))
    halo_count = len(received) * received[0].shape[0]
    remote = jnp.concatenate(received + [hub_all.reshape(-1, tile, width)], 0)
    agg = jnp.einsum(
        "bkij,bkjf->bif", local_tiles, blocks[local_src], preferred_element_type=jnp.float32
    )
    agg = agg + jnp.einsum(
        "bkij,bkjf->bif", remote_tiles, remote[remote_src], preferred_element_type=jnp.float32
    )
    agg_b = agg.reshape(node_count, width).astype(jnp.bfloat16)
    pre = (
        jnp.dot(features, w_self, preferred_element_type=jnp.float32)
        + jnp.dot(agg_b, w_neigh, preferred_element_type=jnp.float32)
        + bias
    )
    sig = jax.nn.sigmoid(pre)
    hidden = (pre * sig).astype(jnp.bfloat16)
    d_pre = d_hidden.astype(jnp.float32) * sig * (1.0 + pre * (1.0 - sig))
    d_pre_b = d_pre.astype(jnp.bfloat16)
    part_self = jnp.dot(features.T, d_pre_b, preferred_element_type=jnp.float32)
    part_neigh = jnp.dot(agg_b.T, d_pre_b, preferred_element_type=jnp.float32)
    part_bias = jnp.sum(d_pre, 0)
    grad_w_self, grad_w_neigh, grad_bias = (
        lax.psum_scatter(part_self, "dom", scatter_dimension=1, tiled=True),
        lax.psum_scatter(part_neigh, "dom", scatter_dimension=1, tiled=True),
        lax.psum_scatter(part_bias, "dom", scatter_dimension=0, tiled=True),
    )
    d_self = jnp.dot(d_pre_b, w_self.T, preferred_element_type=jnp.float32)
    d_agg = jnp.dot(d_pre_b, w_neigh.T, preferred_element_type=jnp.float32).astype(jnp.bfloat16)
    d_agg = d_agg.reshape(block_count, tile, width)
    local_terms = jnp.einsum(
        "bkij,bif->bkjf", local_tiles, d_agg, preferred_element_type=jnp.float32
    )
    remote_terms = jnp.einsum(
        "bkij,bif->bkjf", remote_tiles, d_agg, preferred_element_type=jnp.float32
    )
    d_loc = jnp.zeros((block_count, tile, width), jnp.float32).at[local_src].add(local_terms)
    d_rem = jnp.zeros((remote.shape[0], tile, width), jnp.float32).at[remote_src].add(remote_terms)
    grad_blocks = d_self.reshape(block_count, tile, width) + d_loc
    per_list = halo_count // 4
    halo_grad = d_rem[:halo_count].reshape(4, per_list, tile, width)
    for j, step in enumerate(OFFSETS):
        returned = shifted(halo_grad[j].astype(jnp.bfloat16), "dom", -step).astype(jnp.float32)
        grad_blocks = add_into(grad_blocks, send_blocks[j], returned)
    hub_part = d_rem[halo_count:].reshape(-1, width)
    hub_mine = lax.psum_scatter(hub_part, "dom", scatter_dimension=0, tiled=True)
    grad_flat = grad_blocks.reshape(node_count, width).at[hub_rows].add(hub_mine)
    return (hidden, grad_flat.astype(jnp.bfloat16), grad_w_self, grad_w_neigh, grad_bias)


def solution(mesh):
    in_specs = (
        P("dom", None),
        P("dom", None, None, None),
        P("dom", None),
        P("dom", None, None, None),
        P("dom", None),
        P("dom", None),
        P("dom"),
        P(),
        P(),
        P(),
        P("dom", None),
    )
    out_specs = (P("dom", None), P("dom", None), P(None, "dom"), P(None, "dom"), P("dom"))
    return jax.shard_map(shards, mesh=mesh, in_specs=in_specs, out_specs=out_specs, check_vma=False)
```

profile of v0, /device:TPU:1, one launch (start us, length us, event | category | flops | bytes accessed | tf_op | source)
XLA Modules:
  0.0 436.5 jit_solution(14368515429748615657)
XLA Ops:
  8.1 2.5 gather_fusion.1
  10.6 3.0 collective-permute-start
  13.7 2.4 gather_fusion.2
  20.2 2.4 gather_fusion.4
  22.6 7.1 %collective-permute-start.3 = (bf16[4,128,128]{2,1,0:T(8,128)(2,1)}, bf16[4,128,128]{2,1,0:T(8,128)(2,1)}, u32[]{:S(2)}, u32[]{:S(2)}) collective-permute-start(bf16[4,128,128]{2,1,0:T(8,128)(2,1)} %gather_fusion.4), channel_id=1, source_target_pairs={{2,0},{3,1},{4,2},{5,3},{6,4},{7,5},{8,6},{9,7},{10,8},{11,9},{12,... | collective-permute-start | bytes 393224 | tf_op jit(solution)/shard_map/ppermute | solution.py:12
  33.8 4.0 gather_fusion
  37.8 4.0 fusion.10
  44.1 65.1 %all-gather.1 = bf16[256,4,128]{2,1,0:T(4,128)(2,1)S(1)} all-gather(bf16[1,4,128]{2,1,0:T(4,128)(2,1)S(1)} %bitcast.88), channel_id=2, replica_groups=mesh['dom'=256] {'dom'}, dimensions={0}, use_global_device_ids=true | all-gather | bytes 263168 | tf_op jit(solution)/shard_map/all_gather | solution.py:36
  116.4 3.9 gather_fusion.6
  120.3 3.7 fusion.1
  124.8 3.4 fusion.8
  132.4 3.6 fusion.13
  136.0 3.7 fusion.12
  139.7 6.5 %copy.33 = f32[96,128,128]{2,1,0:T(8,128)} copy(f32[96,128,128]{1,2,0:T(8,128)} %bitcast.79) | data formatting | bytes 12582912 | tf_op jit(solution)/shard_map/bkij,bif->bkjf/dot_general | solution.py:72
  147.6 20.0 %scatter_fusion.1 = f32[24,128,128]{2,1,0:T(8,128)} fusion(f32[24,128,128]{2,1,0:T(8,128)} %broadcast_in_dim.11, s32[96]{0:T(128)S(1)} %reshape.208, f32[96,128,128]{2,1,0:T(8,128)} %copy.33), kind=kCustom, calls=%fused_computation.8 | custom fusion | flops 1572864 | bytes 18874752 | tf_op jit(solution)/shard_map/scatter-add | solution.py:76
  169.4 2.4 convert.6
  175.5 8.7 %collective-permute-start.6 = (bf16[4,128,128]{2,1,0:T(8,128)(2,1)}, bf16[4,128,128]{2,1,0:T(8,128)(2,1)}, u32[]{:S(2)}, u32[]{:S(2)}) collective-permute-start(bf16[4,128,128]{2,1,0:T(8,128)(2,1)} %get-tuple-element.12), channel_id=1, source_target_pairs={{2,0},{3,1},{4,2},{5,3},{6,4},{7,5},{8,6},{9,7},{10,8},{11,9},{12,... | collective-permute-start | bytes 393224 | tf_op jit(solution)/shard_map/ppermute | solution.py:12
  184.2 3.7 fusion.11
  187.9 6.5 %copy.31 = f32[96,128,128]{2,1,0:T(8,128)} copy(f32[96,128,128]{1,2,0:T(8,128)} %bitcast.78) | data formatting | bytes 12582912 | tf_op jit(solution)/shard_map/bkij,bif->bkjf/dot_general | solution.py:69
  194.4 77.8 %all-reduce.3 = f32[256]{0:T(256)S(1)} all-reduce(f32[256]{0:T(256)S(1)} %get-tuple-element.8), channel_id=6, replica_groups=mesh['dom'=256] {'dom'}, use_global_device_ids=true, to_apply=%region_11.0.clone | all-reduce | flops 256 | bytes 2048
  272.9 19.9 %scatter_fusion = f32[32,128,128]{2,1,0:T(8,128)} fusion(f32[32,128,128]{2,1,0:T(8,128)} %bitcast.71, s32[96]{0:T(128)S(1)} %reshape.160, f32[96,128,128]{2,1,0:T(8,128)} %copy.31), kind=kCustom, calls=%fused_computation.7 | custom fusion | flops 1572864 | bytes 18874752 | tf_op jit(solution)/shard_map/scatter-add | solution.py:75
  305.7 115.2 %all-reduce.7.cloned.1.call-done = (f32[1024,128]{1,0:T(8,128)}, f32[128,256]{0,1:T(8,128)}, f32[128,256]{0,1:T(8,128)}) async-done(((f32[1024,128]{1,0:T(8,128)}, f32[128,256]{0,1:T(8,128)}, f32[128,256]{0,1:T(8,128)}), (f32[1024,128]{1,0:T(8,128)}, f32[128,256]{0,1:T(8,128)}, f32[128,256]{0,1:T(8,128)})) %all-reduce.7.cloned.1.call-update) | async-done | bytes 786448
  420.9 3.7 scatter_custom_fusion.6
  424.6 2.7 convert_element_type.51
  (76 shorter events, 46.4 us)
Async XLA Ops:
  7.2 113.1 %copy-start = (bf16[32,3,128,128]{3,2,1,0:T(8,128)(2,1)S(1)}, bf16[32,3,128,128]{3,2,1,0:T(8,128)(2,1)}, u32[]{:S(2)}) copy-start(bf16[32,3,128,128]{3,2,1,0:T(8,128)(2,1)} %param.14) | copy-start | bytes 9437188
  7.2 413.7 %all-reduce.7.cloned.1.call-start = ((), (), s32[]{:S(2)}) async-start(), calls=%async_computation | async-start | bytes 1572864
  10.6 98.8 %collective-permute-start = (bf16[4,128,128]{2,1,0:T(8,128)(2,1)}, bf16[4,128,128]{2,1,0:T(8,128)(2,1)}, u32[]{:S(2)}, u32[]{:S(2)}) collective-permute-start(bf16[4,128,128]{2,1,0:T(8,128)(2,1)} %gather_fusion.1), channel_id=1, source_target_pairs={{255,0},{0,1},{1,2},{2,3},{3,4},{4,5},{5,6},{6,7},{7,8},{8,9},{9,1... | collective-permute-start | bytes 393224 | tf_op jit(solution)/shard_map/ppermute | solution.py:12
  16.1 94.9 %collective-permute-start.1 = (bf16[4,128,128]{2,1,0:T(8,128)(2,1)}, bf16[4,128,128]{2,1,0:T(8,128)(2,1)}, u32[]{:S(2)}, u32[]{:S(2)}) collective-permute-start(bf16[4,128,128]{2,1,0:T(8,128)(2,1)} %gather_fusion.2), channel_id=1, source_target_pairs={{1,0},{2,1},{3,2},{4,3},{5,4},{6,5},{7,6},{8,7},{9,8},{10,9},{11,1... | collective-permute-start | bytes 393224 | tf_op jit(solution)/shard_map/ppermute | solution.py:12
  18.7 93.8 %collective-permute-start.2 = (bf16[4,128,128]{2,1,0:T(8,128)(2,1)}, bf16[4,128,128]{2,1,0:T(8,128)(2,1)}, u32[]{:S(2)}, u32[]{:S(2)}) collective-permute-start(bf16[4,128,128]{2,1,0:T(8,128)(2,1)} %gather_fusion.3), channel_id=1, source_target_pairs={{254,0},{255,1},{0,2},{1,3},{2,4},{3,5},{4,6},{5,7},{6,8},{7,9},{8... | collective-permute-start | bytes 393224 | tf_op jit(solution)/shard_map/ppermute | solution.py:12
  22.6 91.6 %collective-permute-start.3 = (bf16[4,128,128]{2,1,0:T(8,128)(2,1)}, bf16[4,128,128]{2,1,0:T(8,128)(2,1)}, u32[]{:S(2)}, u32[]{:S(2)}) collective-permute-start(bf16[4,128,128]{2,1,0:T(8,128)(2,1)} %gather_fusion.4), channel_id=1, source_target_pairs={{2,0},{3,1},{4,2},{5,3},{6,4},{7,5},{8,6},{9,7},{10,8},{11,9},{12,... | collective-permute-start | bytes 393224 | tf_op jit(solution)/shard_map/ppermute | solution.py:12
  33.8 4.0 copy-start.7
  37.8 4.0 copy-start.4
  37.8 4.0 copy-start.5
  120.3 3.8 copy-start.3
  120.3 3.8 copy-start.8
  120.3 4.5 %copy-start.9 = (bf16[4096,256]{1,0:T(8,128)(2,1)S(1)}, bf16[4096,256]{1,0:T(8,128)(2,1)}, u32[]{:S(2)}) copy-start(bf16[4096,256]{1,0:T(8,128)(2,1)} %param.21) | copy-start | bytes 6291460
  120.3 4.4 %copy-start.10 = (f32[256]{0:T(256)S(1)}, f32[256]{0:T(256)}, u32[]{:S(2)}) copy-start(f32[256]{0:T(256)} %param.20) | copy-start | bytes 3076
  128.2 2.3 copy-start.1
  129.7 1.2 copy-start.2
  132.3 3.7 copy-start.6
  173.8 118.9 %collective-permute-start.4 = (bf16[4,128,128]{2,1,0:T(8,128)(2,1)S(1)}, bf16[4,128,128]{2,1,0:T(8,128)(2,1)}, u32[]{:S(2)}, u32[]{:S(2)}) collective-permute-start(bf16[4,128,128]{2,1,0:T(8,128)(2,1)S(1)} %get-tuple-element.14), channel_id=1, source_target_pairs={{1,0},{2,1},{3,2},{4,3},{5,4},{6,5},{7,6},{8,7},{9,8},{10,9},{11,1... | collective-permute-start | bytes 393224 | tf_op jit(solution)/shard_map/ppermute | solution.py:12
  173.8 122.2 %collective-permute-start.5 = (bf16[4,128,128]{2,1,0:T(8,128)(2,1)}, bf16[4,128,128]{2,1,0:T(8,128)(2,1)}, u32[]{:S(2)}, u32[]{:S(2)}) collective-permute-start(bf16[4,128,128]{2,1,0:T(8,128)(2,1)} %get-tuple-element.13), channel_id=1, source_target_pairs={{255,0},{0,1},{1,2},{2,3},{3,4},{4,5},{5,6},{6,7},{7,8},{8,9},{9,1... | collective-permute-start | bytes 393224 | tf_op jit(solution)/shard_map/ppermute | solution.py:12
  175.5 123.7 %collective-permute-start.6 = (bf16[4,128,128]{2,1,0:T(8,128)(2,1)}, bf16[4,128,128]{2,1,0:T(8,128)(2,1)}, u32[]{:S(2)}, u32[]{:S(2)}) collective-permute-start(bf16[4,128,128]{2,1,0:T(8,128)(2,1)} %get-tuple-element.12), channel_id=1, source_target_pairs={{2,0},{3,1},{4,2},{5,3},{6,4},{7,5},{8,6},{9,7},{10,8},{11,9},{12,... | collective-permute-start | bytes 393224 | tf_op jit(solution)/shard_map/ppermute | solution.py:12
  184.2 118.2 %collective-permute-start.7 = (bf16[4,128,128]{2,1,0:T(8,128)(2,1)}, bf16[4,128,128]{2,1,0:T(8,128)(2,1)}, u32[]{:S(2)}, u32[]{:S(2)}) collective-permute-start(bf16[4,128,128]{2,1,0:T(8,128)(2,1)} %get-tuple-element.11), channel_id=1, source_target_pairs={{254,0},{255,1},{0,2},{1,3},{2,4},{3,5},{4,6},{5,7},{6,8},{7,9},{8... | collective-permute-start | bytes 393224 | tf_op jit(solution)/shard_map/ppermute | solution.py:12
Sparse Core Ops, SparseCore 0:
  172.0 248.8 all-reduce.6
where the time goes:
time: 439 us; the launch traced here: 436 us
  blocking collectives  143 us (33%)
  waiting for transfers between devices  115 us (26%)
  other arithmetic  64.5 us (15%)
  local copies, waits for them, and re-layouts  49.3 us (11%)
  matrix products  28 us (6%)
  starting transfers between devices  22.2 us (5%)
  between operations  14.2 us (3%)
    unnamed x2, waiting for transfers between devices  115 us
    unnamed x1, blocking collectives  77.8 us
    all_gather x1, blocking collectives, shards(): hub_all = lax.all_gather(features[hub_rows], 'dom', axis=0, tiled=True)  65.1 us
    ppermute x8, starting transfers between devices, shifted(): return lax.ppermute(block, axis, route)  22.2 us
    scatter-add x1, other arithmetic, shards(): jnp.zeros((remote.shape[0], tile, width), jnp.float32).at[remote_src]  20 us
    scatter-add x1, other arithmetic, shards(): jnp.zeros((block_count, tile, width), jnp.float32).at[local_src]  19.9 us
    unnamed x29, local copies, waits for them, and re-layouts  10.5 us
    gather x4, local copies, waits for them, and re-layouts, shards(): received.append(shifted(blocks[send_blocks[j]], 'dom', step))  9.79 us
  transfers between devices with their start and end apart: 9, of which 1 were waited for; matrix products, arithmetic and copies ran while one was open for 17% of the time, Pallas kernels for 0%

commit v1 on v0

v1 whole, which is shorter than its diff:
```python
import functools

import jax
import jax.numpy as jnp
from jax import lax
from jax.experimental import pallas as pl
from jax.experimental.pallas import tpu as pltpu
from jax.sharding import PartitionSpec as P

OFFSETS = (1, -1, 2, -2)
F32 = jnp.float32
BF16 = jnp.bfloat16
NT = (((1,), (1,)), ((), ()))
TN = (((0,), (0,)), ((), ()))
GROUP = 16
CHUNK = 8
STEP = 4


def shifted(block, axis, distance):
    devices = range(lax.axis_size(axis))
    route = [((i - distance) % len(devices), i) for i in devices]
    return lax.ppermute(block, axis, route)


def params(mib, **more):
    return pltpu.CompilerParams(vmem_limit_bytes=mib << 20, **more)


def whole(shape):
    return pl.BlockSpec(shape, lambda *_: (0,) * len(shape))


def send_kernel(send, hubs, blocks, *refs):
    lists, per_list = send.shape
    outs, hub_out = refs[:lists], refs[lists]
    near, sem_a, sem_b = refs[lists + 1 :]
    owned = hubs.shape[0]
    tile = blocks.shape[1]
    copies = []
    for i in range(owned):
        row = hubs[i]
        base = pl.multiple_of(lax.rem(row, tile) // GROUP * GROUP, GROUP)
        copies.append(
            pltpu.make_async_copy(
                blocks.at[row // tile, pl.ds(base, GROUP), :], near.at[i], sem_a.at[i]
            )
        )
    for c in copies:
        c.start()
    moves = []
    for j in range(lists):
        for h in range(per_list):
            moves.append(
                pltpu.make_async_copy(
                    blocks.at[send[j, h]], outs[j].at[h], sem_b.at[j * per_list + h]
                )
            )
    for c in moves:
        c.start()
    for c in copies:
        c.wait()
    place = lax.broadcasted_iota(jnp.int32, (GROUP, near.shape[-1]), 0)
    rows = []
    for i in range(owned):
        chosen = jnp.where(place == lax.rem(hubs[i], GROUP), near[i].astype(F32), 0.0)
        rows.append(jnp.sum(chosen, 0, keepdims=True))
    rows.append(jnp.zeros((hub_out.shape[0] - owned, near.shape[-1]), F32))
    hub_out[...] = jnp.concatenate(rows, 0)
    for c in moves:
        c.wait()


def gather_sends(send, hubs, blocks):
    lists, per_list = send.shape
    _, tile, width = blocks.shape
    owned = hubs.shape[0]
    any_spec = pl.BlockSpec(memory_space=pl.ANY)
    return pl.pallas_call(
        send_kernel,
        out_shape=[jax.ShapeDtypeStruct((per_list, tile, width), blocks.dtype)] * lists
        + [jax.ShapeDtypeStruct((8, width), F32)],
        in_specs=[
            pl.BlockSpec(memory_space=pltpu.SMEM),
            pl.BlockSpec(memory_space=pltpu.SMEM),
            any_spec,
        ],
        out_specs=[any_spec] * lists + [pl.BlockSpec(memory_space=pltpu.VMEM)],
        scratch_shapes=[
            pltpu.VMEM((owned, GROUP, width), blocks.dtype),
            pltpu.SemaphoreType.DMA((owned,)),
            pltpu.SemaphoreType.DMA((lists * per_list,)),
        ],
        compiler_params=params(8),
        name="sends",
    )(send, hubs, blocks)


def local_kernel(src, tiles, blocks, agg):
    first = pl.program_id(0) * STEP
    tile = tiles.shape[-1]
    for b in range(STEP):
        taken = [blocks[src[k, first + b]] for k in range(tiles.shape[1])]
        edges = [tiles[b, k] for k in range(tiles.shape[1])]
        agg[b * tile : (b + 1) * tile, :] = jnp.dot(
            jnp.concatenate(edges, 1), jnp.concatenate(taken, 0), preferred_element_type=F32
        )


def local_aggregate(src, tiles, blocks):
    count, per_block, tile, _ = tiles.shape
    width = blocks.shape[-1]
    return pl.pallas_call(
        local_kernel,
        out_shape=jax.ShapeDtypeStruct((count * tile, width), F32),
        grid_spec=pltpu.PrefetchScalarGridSpec(
            num_scalar_prefetch=1,
            grid=(count // STEP,),
            in_specs=[
                pl.BlockSpec((STEP, per_block, tile, tile), lambda i, *_: (i, 0, 0, 0)),
                whole(blocks.shape),
            ],
            out_specs=pl.BlockSpec((STEP * tile, width), lambda i, *_: (i, 0)),
        ),
        compiler_params=params(12),
        cost_estimate=pl.CostEstimate(
            flops=2 * tiles.size * width, bytes_accessed=8 << 20, transcendentals=0
        ),
        name="local_aggregate",
    )(src, tiles, blocks)


def layer_kernel(src, tiles, rows, agg_local, *refs):
    lists = len(OFFSETS)
    halos, refs = refs[:lists], refs[lists:]
    hub, weights, bias, d_hidden, hidden, d_pre_out, d_agg_out = refs[:7]
    backs, refs = refs[7 : 7 + lists], refs[7 + lists :]
    packed, table, rem_grad, w_grad, b_grad, spread, sems = refs
    step = pl.program_id(0)
    tile = tiles.shape[-1]
    width = rows.shape[-1]
    per_list = halos[0].shape[0]
    halo_count = lists * per_list
    hub_blocks = hub.shape[0]

    @pl.when(step == 0)
    def _():
        moves = []
        for j in range(lists):
            moves.append(
                pltpu.make_async_copy(
                    halos[j], table.at[pl.ds(j * per_list, per_list)], sems.at[j]
                )
            )
        moves.append(
            pltpu.make_async_copy(hub, table.at[pl.ds(halo_count, hub_blocks)], sems.at[lists])
        )
        for c in moves:
            c.start()
        rem_grad[...] = jnp.zeros_like(rem_grad)
        w_grad[...] = jnp.zeros_like(w_grad)
        b_grad[...] = jnp.zeros_like(b_grad)
        for c in moves:
            c.wait()

    for b in range(STEP):
        block = slice(b * tile, (b + 1) * tile)
        sources = [src[k, step * STEP + b] for k in range(tiles.shape[1])]
        edges = jnp.concatenate([tiles[b, k] for k in range(tiles.shape[1])], 1)
        taken = jnp.concatenate([table[s] for s in sources], 0)
        agg = agg_local[block, :] + jnp.dot(edges, taken, preferred_element_type=F32)
        both = jnp.concatenate([rows[block, :], agg.astype(BF16)], 1)
        pre = jnp.dot(both, weights[...], preferred_element_type=F32) + bias[...]
        sig = jax.nn.sigmoid(pre)
        hidden[block, :] = (pre * sig).astype(BF16)
        d_pre = d_hidden[block, :].astype(F32) * (sig * (1.0 + pre * (1.0 - sig)))
        b_grad[...] += jnp.sum(d_pre.reshape(tile // 8, 8, d_pre.shape[-1]), 0)
        d_pre_b = d_pre.astype(BF16)
        d_pre_out[block, :] = d_pre_b
        w_grad[...] += lax.dot_general(d_pre_b, both, TN, preferred_element_type=F32)
        d_agg = lax.dot_general(weights[width:, :], d_pre_b, NT, preferred_element_type=F32)
        d_agg = d_agg.astype(BF16)
        d_agg_out[b] = d_agg
        terms = jnp.dot(d_agg, edges, preferred_element_type=F32)
        for k, s in enumerate(sources):
            rem_grad[s] += terms[:, k * tile : (k + 1) * tile]

    @pl.when(step == pl.num_programs(0) - 1)
    def _():
        for j in range(lists):
            backs[j][...] = rem_grad[j * per_list : (j + 1) * per_list].astype(BF16)
        parts, chunk, _ = packed.shape
        owned = hub_blocks * tile // parts
        hub_rows = jnp.concatenate(
            [jnp.transpose(rem_grad[halo_count + q]) for q in range(hub_blocks)], 0
        )
        spread[...] = jnp.zeros_like(spread)
        split = hub_rows.reshape(parts, owned, width)
        for i in range(owned):
            spread[pl.ds(i, parts, stride=chunk), :] = split[:, i, :]
        spread[pl.ds(owned, parts, stride=chunk), :] = w_grad[:, :width]
        spread[pl.ds(owned + 1, parts, stride=chunk), :] = w_grad[:, width:]
        total = jnp.sum(b_grad[...], 0, keepdims=True)
        high = total.astype(BF16).astype(F32)
        lane = lax.broadcasted_iota(jnp.int32, (width, parts), 0)
        two = jnp.where(lane == 0, high, jnp.where(lane == 1, total - high, 0.0))
        spread[pl.ds(owned + 2, parts, stride=chunk), :] = jnp.transpose(two)
        packed[...] = spread[...].reshape(parts, chunk, width).astype(BF16)


def layer(src, tiles, rows, agg_local, halos, hub, weights, bias, d_hidden, parts):
    count, per_block, tile, _ = tiles.shape
    nodes, width = rows.shape
    units = d_hidden.shape[-1]
    per_list = halos[0].shape[0]
    table = len(halos) * per_list + hub.shape[0]
    any_spec = pl.BlockSpec(memory_space=pl.ANY)

    def by_step(*shape):
        return pl.BlockSpec(shape, lambda i, *_: (i,) + (0,) * (len(shape) - 1))

    return pl.pallas_call(
        layer_kernel,
        out_shape=[
            jax.ShapeDtypeStruct((nodes, units), BF16),
            jax.ShapeDtypeStruct((nodes, units), BF16),
            jax.ShapeDtypeStruct((count, width, tile), BF16),
        ]
        + [jax.ShapeDtypeStruct((per_list, width, tile), BF16)] * len(halos)
        + [jax.ShapeDtypeStruct((parts, CHUNK, width), BF16)],
        grid_spec=pltpu.PrefetchScalarGridSpec(
            num_scalar_prefetch=1,
            grid=(count // STEP,),
            in_specs=[
                by_step(STEP, per_block, tile, tile),
                by_step(STEP * tile, width),
                by_step(STEP * tile, width),
            ]
            + [any_spec] * (len(halos) + 1)
            + [
                whole(weights.shape),
                whole(bias.shape),
                by_step(STEP * tile, units),
            ],
            out_specs=[
                by_step(STEP * tile, units),
                by_step(STEP * tile, units),
                by_step(STEP, width, tile),
            ]
            + [whole((per_list, width, tile))] * len(halos)
            + [whole((parts, CHUNK, width))],
            scratch_shapes=[
                pltpu.VMEM((table, tile, width), BF16),
                pltpu.VMEM((table, width, tile), F32),
                pltpu.VMEM((units, 2 * width), F32),
                pltpu.VMEM((8, units), F32),
                pltpu.VMEM((parts * CHUNK, width), F32),
                pltpu.SemaphoreType.DMA((len(halos) + 1,)),
            ],
        ),
        compiler_params=params(24),
        cost_estimate=pl.CostEstimate(
            flops=4 * tiles.size * width + 12 * nodes * width * units,
            bytes_accessed=14 << 20,
            transcendentals=nodes * units,
        ),
        name="layer",
    )(src, tiles, rows, agg_local, *halos, hub, weights, bias, d_hidden)


def back_kernel(src, tiles, d_pre, d_agg, weight, grad):
    step = pl.program_id(0)
    tile = tiles.shape[-1]

    @pl.when(step == 0)
    def _():
        grad[...] = jnp.zeros_like(grad)

    for b in range(STEP):
        own = lax.dot_general(
            weight[...], d_pre[b * tile : (b + 1) * tile, :], NT, preferred_element_type=F32
        )
        grad[step * STEP + b] += own
        edges = jnp.concatenate([tiles[b, k] for k in range(tiles.shape[1])], 1)
        terms = jnp.dot(d_agg[b], edges, preferred_element_type=F32)
        for k in range(tiles.shape[1]):
            s = src[k, step * STEP + b]
            grad[s] += terms[:, k * tile : (k + 1) * tile]


def local_backward(src, tiles, d_pre, d_agg, weight):
    count, per_block, tile, _ = tiles.shape
    width, units = weight.shape
    return pl.pallas_call(
        back_kernel,
        out_shape=jax.ShapeDtypeStruct((count, width, tile), F32),
        grid_spec=pltpu.PrefetchScalarGridSpec(
            num_scalar_prefetch=1,
            grid=(count // STEP,),
            in_specs=[
                pl.BlockSpec((STEP, per_block, tile, tile), lambda i, *_: (i, 0, 0, 0)),
                pl.BlockSpec((STEP * tile, units), lambda i, *_: (i, 0)),
                pl.BlockSpec((STEP, width, tile), lambda i, *_: (i, 0, 0)),
                whole(weight.shape),
            ],
            out_specs=whole((count, width, tile)),
        ),
        compiler_params=params(16),
        cost_estimate=pl.CostEstimate(
            flops=2 * tiles.size * width + 2 * d_pre.size * width,
            bytes_accessed=8 << 20,
            transcendentals=0,
        ),
        name="local_backward",
    )(src, tiles, d_pre, d_agg, weight)


def collect_kernel(send, hubs, grad, *refs):
    lists, per_list = send.shape
    halos = refs[:lists]
    out, near, total = refs[lists:]
    count, width, tile = grad.shape
    total[...] = grad[...]
    for j in range(lists):
        for h in range(per_list):
            total[send[j, h]] += halos[j][h].astype(F32)
    for b in range(count):
        out[b * tile : (b + 1) * tile, :] = jnp.transpose(total[b]).astype(BF16)
    for i in range(hubs.shape[0]):
        row = hubs[i]
        turned = jnp.transpose(total[row // tile])
        want = lax.rem(row, tile) // GROUP
        part = jnp.zeros((GROUP, width), F32)
        for g in range(tile // GROUP):
            part = jnp.where(want == g, turned[g * GROUP : (g + 1) * GROUP], part)
        near[i] = part


def collect(send, hubs, grad, halos):
    count, width, tile = grad.shape
    smem = pl.BlockSpec(memory_space=pltpu.SMEM)
    vmem = pl.BlockSpec(memory_space=pltpu.VMEM)
    return pl.pallas_call(
        collect_kernel,
        out_shape=[
            jax.ShapeDtypeStruct((count * tile, width), BF16),
            jax.ShapeDtypeStruct((hubs.shape[0], GROUP, width), F32),
        ],
        in_specs=[smem, smem] + [vmem] * (1 + len(halos)),
        out_specs=[vmem, vmem],
        scratch_shapes=[pltpu.VMEM((count, width, tile), F32)],
        compiler_params=params(16),
        cost_estimate=pl.CostEstimate(
            flops=grad.size * 8, bytes_accessed=4 << 20, transcendentals=0
        ),
        name="collect",
    )(send, hubs, grad, *halos)


def finish_kernel(hubs, pieces, near, _, grad, g_self, g_neigh, g_bias, rows, sems):
    owned = hubs.shape[0]
    total = jnp.sum(pieces[...].astype(F32), 0)
    g_self[...] = total[owned : owned + 1, :]
    g_neigh[...] = total[owned + 1 : owned + 2, :]
    last = total[owned + 2 : owned + 3, :]
    g_bias[...] = jnp.broadcast_to(last[:, 0:1] + last[:, 1:2], last.shape)
    place = lax.broadcasted_iota(jnp.int32, (GROUP, total.shape[-1]), 0)
    for i in range(owned):
        value = near[i]
        for m in range(owned):
            same = hubs[m] // GROUP == hubs[i] // GROUP
            hit = jnp.logical_and(place == lax.rem(hubs[m], GROUP), same)
            value = value + jnp.where(hit, total[m : m + 1, :], 0.0)
        rows[i] = value.astype(BF16)

    def fresh(i):
        new = hubs[i] >= 0
        for m in range(i):
            new = jnp.logical_and(new, hubs[m] // GROUP != hubs[i] // GROUP)
        return new

    def move(i):
        base = pl.multiple_of(hubs[i] // GROUP * GROUP, GROUP)
        return pltpu.make_async_copy(rows.at[i], grad.at[pl.ds(base, GROUP), :], sems.at[i])

    for i in range(owned):
        pl.when(fresh(i))(lambda i=i: move(i).start())
    for i in range(owned):
        pl.when(fresh(i))(lambda i=i: move(i).wait())


def finish(hubs, pieces, near, grad):
    owned, _, width = near.shape
    smem = pl.BlockSpec(memory_space=pltpu.SMEM)
    vmem = pl.BlockSpec(memory_space=pltpu.VMEM)
    any_spec = pl.BlockSpec(memory_space=pl.ANY)
    line = jax.ShapeDtypeStruct((1, width), F32)
    return pl.pallas_call(
        finish_kernel,
        out_shape=[jax.ShapeDtypeStruct(grad.shape, grad.dtype), line, line, line],
        in_specs=[smem, vmem, vmem, any_spec],
        out_specs=[any_spec, vmem, vmem, vmem],
        scratch_shapes=[
            pltpu.VMEM((owned, GROUP, width), BF16),
            pltpu.SemaphoreType.DMA((owned,)),
        ],
        input_output_aliases={3: 0},
        compiler_params=params(8),
        name="finish",
    )(hubs, pieces, near, grad)


def shards(
    features,
    local_tiles,
    local_src,
    remote_tiles,
    remote_src,
    send_blocks,
    hub_rows,
    w_self,
    w_neigh,
    bias,
    d_hidden,
):
    parts = lax.axis_size("dom")
    nodes, width = features.shape
    tile = local_tiles.shape[-1]
    owned = hub_rows.shape[0]
    blocks = features.reshape(nodes // tile, tile, width)
    *sends, hub_mine = gather_sends(send_blocks, hub_rows, blocks)
    everywhere = jnp.broadcast_to(hub_mine[:owned].astype(BF16)[None], (parts, owned, width))
    hub_all = lax.all_to_all(everywhere, "dom", 0, 0)
    halos = [shifted(b, "dom", step) for b, step in zip(sends, OFFSETS)]
    agg_local = local_aggregate(local_src.T, local_tiles, blocks)
    weights = jnp.concatenate([w_self, w_neigh], 0)
    hidden, d_pre, d_agg, *rest = layer(
        remote_src.T,
        remote_tiles,
        features,
        agg_local,
        halos,
        hub_all.reshape(parts * owned // tile, tile, width),
        weights,
        bias[None],
        d_hidden,
        parts,
    )
    *backs, packed = rest
    pieces = lax.all_to_all(packed, "dom", 0, 0)
    returned = [shifted(b, "dom", -step) for b, step in zip(backs, OFFSETS)]
    grad_t = local_backward(local_src.T, local_tiles, d_pre, d_agg, w_self)
    rough, near = collect(send_blocks, hub_rows, grad_t, returned)
    grad, g_self, g_neigh, g_bias = finish(hub_rows, pieces, near, rough)
    return (hidden, grad, g_self.reshape(width, 1), g_neigh.reshape(width, 1), g_bias[0, :1])


def solution(mesh):
    in_specs = (
        P("dom", None),
        P("dom", None, None, None),
        P("dom", None),
        P("dom", None, None, None),
        P("dom", None),
        P("dom", None),
        P("dom"),
        P(),
        P(),
        P(),
        P("dom", None),
    )
    out_specs = (P("dom", None), P("dom", None), P(None, "dom"), P(None, "dom"), P("dom"))
    return jax.shard_map(shards, mesh=mesh, in_specs=in_specs, out_specs=out_specs, check_vma=False)
```

time: 439 us -> 120 us (0.27)
  blocking collectives: 143 us -> 0 us
  waiting for transfers between devices: 115 us -> 2.29 us
  other arithmetic: 64.5 us -> 0.01 us
  starting transfers between devices: 22.2 us -> 55.3 us
  Pallas kernels: 0 us -> 31.9 us
  matrix products: 28 us -> 0 us
  local copies, waits for them, and re-layouts: 49.3 us -> 29.1 us
  between operations: 14.2 us -> 0.83 us
    unnamed x2 -> x0, waiting for transfers between devices: 115 us -> none
    unnamed x1 -> x0, blocking collectives: 77.8 us -> none
    all_gather x1 -> x0, blocking collectives: 65.1 us -> none  [shards(): hub_all = lax.all_gather(features[hub_rows], 'dom', axis=0, tiled=True)]
    scatter-add x7 -> x0, other arithmetic: 52.7 us -> none  [the longest x1 20 us: shards(): jnp.zeros((remote.shape[0], tile, width), jnp.float32).at[remote_src]]
    pallas_call x0 -> x6, Pallas kernels: none -> 31.9 us  [the longest x1 19.4 us: layer(): pl.pallas_call(layer_kernel, out_shape=[jax.ShapeDtypeStruct((nodes, unit...]
    all_to_all x0 -> x2, starting transfers between devices: none -> 29.7 us  [the longest x1 15.7 us: shards(): hub_all = lax.all_to_all(everywhere, 'dom', 0, 0)]
    dot_general x10 -> x0, matrix products: 28 us -> none  [the longest x1 3.99 us: shards(): jnp.dot(features, w_self, preferred_element_type=jnp.float32)]
    gather x7 -> x0, local copies, waits for them, and re-layouts: 19.6 us -> none  [the longest x4 9.79 us: shards(): received.append(shifted(blocks[send_blocks[j]], 'dom', step))]
  transfers between devices with their start and end apart: 9 -> 10, of which waited for: 1 -> 1; matrix products, arithmetic and copies ran while one was open for 17% -> 0% of each run, Pallas kernels for 0% -> 7%
where the time goes in v1:
time: 120 us; the launch traced here: 119 us
  starting transfers between devices  55.3 us (46%)
  Pallas kernels  31.9 us (27%)
  local copies, waits for them, and re-layouts  29.1 us (24%)
  waiting for transfers between devices  2.29 us (2%)
    unnamed x74, local copies, waits for them, and re-layouts  28.3 us
    ppermute x8, starting transfers between devices, shifted(): return lax.ppermute(block, axis, route)  25.6 us
    pallas_call x1, Pallas kernels, layer(): pl.pallas_call(layer_kernel, out_shape=[jax.ShapeDtypeStruct((nodes, unit...  19.4 us
    all_to_all x1, starting transfers between devices, shards(): hub_all = lax.all_to_all(everywhere, 'dom', 0, 0)  15.7 us
    all_to_all x1, starting transfers between devices, shards(): pieces = lax.all_to_all(packed, 'dom', 0, 0)  14.1 us
    pallas_call x1, Pallas kernels, local_backward(): pl.pallas_call(back_kernel, out_shape=jax.ShapeDtypeStruct((count, width,...  3.48 us
    pallas_call x1, Pallas kernels, local_aggregate(): pl.pallas_call(local_kernel, out_shape=jax.ShapeDtypeStruct((count * tile...  2.75 us
    pallas_call x1, Pallas kernels, finish(): pl.pallas_call(finish_kernel, out_shape=[jax.ShapeDtypeStruct(grad.shape,...  2.5 us
  transfers between devices with their start and end apart: 10, of which 1 were waited for; matrix products, arithmetic and copies ran while one was open for 0% of the time, Pallas kernels for 7%

profile of v1, /device:TPU:1, one launch (start us, length us, event | category | flops | bytes accessed | tf_op | source)
XLA Modules:
  0.0 119.4 jit_solution(9284517808785385671)
XLA Ops:
  0.6 1.2 %copy-done.2 = bf16[4096,128]{1,0:T(8,128)(2,1)S(1)} copy-done((bf16[4096,128]{1,0:T(8,128)(2,1)S(1)}, bf16[4096,128]{1,0:T(8,128)(2,1)}, u32[]{:S(2)}) %copy-start.2) | copy-done | bytes 1048600
  3.2 1.6 %sends.1 = (bf16[4,128,128]{2,1,0:T(8,128)(2,1)S(1)}, bf16[4,128,128]{2,1,0:T(8,128)(2,1)S(1)}, bf16[4,128,128]{2,1,0:T(8,128)(2,1)S(1)}, bf16[4,128,128]{2,1,0:T(8,128)(2,1)S(1)}, f32[8,128]{1,0:T(8,128)S(1)}) custom-call(s32[4,4]{1,0:T(4,128)S(1)} %copy-done.26, s32[4]{0:T(128)S(1)} %copy-done.28, bf16[32,128,128]{2,1,0:T(8,128)(2,1)S(1)} %bitcast.9), custom_call_target="tpu_custom_call" | custom-call | tf_op jit(solution)/shard_map/sends/pallas_call | solution.py:79
  5.6 15.7 %all-to-all-start = ((bf16[256,4,128]{2,1,0:T(4,128)(2,1)}), bf16[256,4,128]{2,1,0:T(4,128)(2,1)S(1)}, u32[]{:S(2)}, u32[]{:S(2)}) async-start(bf16[256,4,128]{2,1,0:T(4,128)(2,1)} %broadcast_in_dim.4), calls=%async_computation | async-start | bytes 524288 | tf_op jit(solution)/shard_map/all_to_all | solution.py:433
  21.3 1.8 %collective-permute-start = (bf16[4,128,128]{2,1,0:T(8,128)(2,1)S(1)}, bf16[4,128,128]{2,1,0:T(8,128)(2,1)S(1)}, u32[]{:S(2)}, u32[]{:S(2)}) collective-permute-start(bf16[4,128,128]{2,1,0:T(8,128)(2,1)S(1)} %get-tuple-element.24), channel_id=1, source_target_pairs={{255,0},{0,1},{1,2},{2,3},{3,4},{4,5},{5,6},{6,7},{7,8},{8,9},{9,1... | collective-permute-start | bytes 393224 | tf_op jit(solution)/shard_map/ppermute | solution.py:23
  23.6 1.0 collective-permute-start.2
  24.6 6.1 %collective-permute-start.3 = (bf16[4,128,128]{2,1,0:T(8,128)(2,1)S(1)}, bf16[4,128,128]{2,1,0:T(8,128)(2,1)S(1)}, u32[]{:S(2)}, u32[]{:S(2)}) collective-permute-start(bf16[4,128,128]{2,1,0:T(8,128)(2,1)S(1)} %get-tuple-element.27), channel_id=1, source_target_pairs={{2,0},{3,1},{4,2},{5,3},{6,4},{7,5},{8,6},{9,7},{10,8},{11,9},{12,... | collective-permute-start | bytes 393224 | tf_op jit(solution)/shard_map/ppermute | solution.py:23
  30.7 1.9 %copy-done = bf16[32,3,128,128]{3,2,1,0:T(8,128)(2,1)S(1)} copy-done((bf16[32,3,128,128]{3,2,1,0:T(8,128)(2,1)S(1)}, bf16[32,3,128,128]{3,2,1,0:T(8,128)(2,1)}, u32[]{:S(2)}) %copy-start) | copy-done | bytes 3145752
  33.2 2.7 %local_aggregate.1.agg_local = f32[4096,128]{1,0:T(8,128)S(1)} custom-call(s32[3,32]{1,0:T(4,128)S(1)} %bitcast.12, bf16[32,3,128,128]{3,2,1,0:T(8,128)(2,1)S(1)} %copy-done, bf16[32,128,128]{2,1,0:T(8,128)(2,1)S(1)} %bitcast.10), custom_call_target="tpu_custom_call" | custom-call | flops 402653184 | bytes 8388608 | tf_op jit(solution)/shard_map/local_aggregate/pallas_call | solution.py:113
  36.0 1.3 %copy-done.5 = f32[4096,128]{1,0:T(8,128)} copy-done((f32[4096,128]{1,0:T(8,128)}, f32[4096,128]{1,0:T(8,128)S(1)}, u32[]{:S(2)}) %copy-start.5) | copy-done | bytes 2097176
  40.0 1.2 %copy-done.4 = bf16[4096,128]{1,0:T(8,128)(2,1)S(1)} copy-done((bf16[4096,128]{1,0:T(8,128)(2,1)S(1)}, bf16[4096,128]{1,0:T(8,128)(2,1)}, u32[]{:S(2)}) %copy-start.4) | copy-done | bytes 1048600
  41.2 1.6 %copy-done.6 = f32[4096,128]{1,0:T(8,128)S(1)} copy-done((f32[4096,128]{1,0:T(8,128)S(1)}, f32[4096,128]{1,0:T(8,128)}, u32[]{:S(2)}) %copy-start.6) | copy-done | bytes 2097176
  42.8 1.9 %copy-done.7 = bf16[32,3,128,128]{3,2,1,0:T(8,128)(2,1)S(1)} copy-done((bf16[32,3,128,128]{3,2,1,0:T(8,128)(2,1)S(1)}, bf16[32,3,128,128]{3,2,1,0:T(8,128)(2,1)}, u32[]{:S(2)}) %copy-start.7) | copy-done | bytes 3145752
  44.7 1.6 %copy-done.10 = bf16[4096,256]{1,0:T(8,128)(2,1)S(1)} copy-done((bf16[4096,256]{1,0:T(8,128)(2,1)S(1)}, bf16[4096,256]{1,0:T(8,128)(2,1)}, u32[]{:S(2)}) %copy-start.10) | copy-done | bytes 2097176
  49.9 19.4 %layer.1 = (bf16[4096,256]{1,0:T(8,128)(2,1)}, bf16[4096,256]{1,0:T(8,128)(2,1)S(1)}, bf16[32,128,128]{2,1,0:T(8,128)(2,1)S(1)}, bf16[4,128,128]{2,1,0:T(8,128)(...) custom-call(s32[3,32]{1,0:T(4,128)S(1)} %bitcast.14, ...), custom_call_target="tpu_custom_call" | custom-call | flops 2415919104 | bytes 14680064 | tf_op jit(solution)/shard_map/layer/pallas_call | solution.py:222
  69.3 1.3 %copy-done.8 = bf16[4096,256]{1,0:T(8,128)(2,1)} copy-done((bf16[4096,256]{1,0:T(8,128)(2,1)}, bf16[4096,256]{1,0:T(8,128)(2,1)S(1)}, u32[]{:S(2)}) %copy-start.8) | copy-done | bytes 2097176
  75.1 14.1 %all-to-all-start.1 = ((bf16[256,8,128]{2,1,0:T(8,128)(2,1)}), bf16[256,8,128]{2,1,0:T(8,128)(2,1)}, u32[]{:S(2)}, u32[]{:S(2)}) async-start(bf16[256,8,128]{2,1,0:T(8,128)(2,1)} %copy-done.13), calls=%async_computation.1 | async-start | bytes 1048576 | tf_op jit(solution)/shard_map/all_to_all | solution.py:450
  89.1 2.4 %collective-permute-start.4 = (bf16[4,128,128]{2,1,0:T(8,128)(2,1)}, bf16[4,128,128]{2,1,0:T(8,128)(2,1)S(1)}, u32[]{:S(2)}, u32[]{:S(2)}) collective-permute-start(bf16[4,128,128]{2,1,0:T(8,128)(2,1)} %copy-done.35), channel_id=1, source_target_pairs={{1,0},{2,1},{3,2},{4,3},{5,4},{6,5},{7,6},{8,7},{9,8},{10,9},{11,1... | collective-permute-start | bytes 393224 | tf_op jit(solution)/shard_map/ppermute | solution.py:23
  91.6 13.8 %collective-permute-start.6 = (bf16[4,128,128]{2,1,0:T(8,128)(2,1)}, bf16[4,128,128]{2,1,0:T(8,128)(2,1)S(1)}, u32[]{:S(2)}, u32[]{:S(2)}) collective-permute-start(bf16[4,128,128]{2,1,0:T(8,128)(2,1)} %copy-done.33), channel_id=1, source_target_pairs={{2,0},{3,1},{4,2},{5,3},{6,4},{7,5},{8,6},{9,7},{10,8},{11,9},{12,... | collective-permute-start | bytes 393224 | tf_op jit(solution)/shard_map/ppermute | solution.py:23
  105.3 1.6 %copy-done.9 = bf16[4096,256]{1,0:T(8,128)(2,1)S(1)} copy-done((bf16[4096,256]{1,0:T(8,128)(2,1)S(1)}, bf16[4096,256]{1,0:T(8,128)(2,1)}, u32[]{:S(2)}) %copy-start.9) | copy-done | bytes 2097176
  106.9 1.2 %copy-done.12 = bf16[32,128,128]{2,1,0:T(8,128)(2,1)S(1)} copy-done((bf16[32,128,128]{2,1,0:T(8,128)(2,1)S(1)}, bf16[32,128,128]{2,1,0:T(8,128)(2,1)}, u32[]{:S(2)}) %copy-start.12) | copy-done | bytes 1048600
  109.0 3.5 %local_backward.1.grad = f32[32,128,128]{2,1,0:T(8,128)S(1)} custom-call(s32[3,32]{1,0:T(4,128)S(1)} %bitcast.13, bf16[32,3,128,128]{3,2,1,0:T(8,128)(2,1)S(1)} %copy-done.1, bf16[4096,256]{1,0:T(8,128)(2,1)S(1)} %copy-done.9, bf16[32,128,128]{2,1,0:T(8,128)(2,1)S(1)} %copy-done.12, bf16[128,256]{1,0:T(8,128)(2,1)S(1)} %copy-done.15), custom_call_target="tpu_custom_call" | custom-call | flops 671088640 | bytes 8388608 | tf_op jit(solution)/shard_map/local_backward/pallas_call | solution.py:294
  112.5 2.3 %collective-permute-done.7.refs_3_ = bf16[4,128,128]{2,1,0:T(8,128)(2,1)S(1)} collective-permute-done((bf16[4,128,128]{2,1,0:T(8,128)(2,1)}, bf16[4,128,128]{2,1,0:T(8,128)(2,1)S(1)}, u32[]{:S(2)}, u32[]{:S(2)}) %collective-permute-start.7) | collective-permute-done | bytes 131104 | tf_op jit(solution)/shard_map/ppermute | solution.py:23
  114.8 2.1 %collect.1 = (bf16[4096,128]{1,0:T(8,128)(2,1)}, f32[4,16,128]{2,1,0:T(8,128)S(1)}) custom-call(s32[4,4]{1,0:T(4,128)S(1)} %copy-done.27, s32[4]{0:T(128)S(1)} %copy-done.29, f32[32,128,128]{2,1,0:T(8,128)S(1)} %local_backward.1.grad, bf16[4,128,128]{2,1,0:T(8,128)(2,1)S(1)} %collective-permute-done.4.refs_0_, ...), custom_call_target="tpu_custom_call" | custom-call | flops 4194304 | bytes 4194304 | tf_op jit(solution)/shard_map/collect/pallas_call | solution.py:343
  116.9 2.5 %finish.1 = (bf16[4096,128]{1,0:T(8,128)(2,1)}, f32[1,128]{1,0:T(1,128)}, f32[1,128]{1,0:T(1,128)}, f32[1,128]{1,0:T(1,128)}) custom-call(s32[4]{0:T(128)S(1)} %copy-done.29, bf16[256,8,128]{2,1,0:T(8,128)(2,1)} %all-to-all-done.1.pieces, f32[4,16,128]{2,1,0:T(8,128)S(1)} %get-tuple-element.37.near, ...), custom_call_target="tpu_custom_call", output_to_operand_aliasing={{0}: (3, {})} | custom-call | tf_op jit(solution)/shard_map/finish/pallas_call | solution.py:398
  (80 shorter events, 14.8 us)
Async XLA Ops:
  3.2 27.5 %copy-start.3 = (bf16[4096,128]{1,0:T(8,128)(2,1)S(1)}, bf16[4096,128]{1,0:T(8,128)(2,1)}, u32[]{:S(2)}) copy-start(bf16[4096,128]{1,0:T(8,128)(2,1)} %rows.1) | copy-start | bytes 3145732
  5.6 34.4 %all-to-all-start = ((bf16[256,4,128]{2,1,0:T(4,128)(2,1)}), bf16[256,4,128]{2,1,0:T(4,128)(2,1)S(1)}, u32[]{:S(2)}, u32[]{:S(2)}) async-start(bf16[256,4,128]{2,1,0:T(4,128)(2,1)} %broadcast_in_dim.4), calls=%async_computation | async-start | bytes 524288 | tf_op jit(solution)/shard_map/all_to_all | solution.py:433
  21.3 16.1 %collective-permute-start = (bf16[4,128,128]{2,1,0:T(8,128)(2,1)S(1)}, bf16[4,128,128]{2,1,0:T(8,128)(2,1)S(1)}, u32[]{:S(2)}, u32[]{:S(2)}) collective-permute-start(bf16[4,128,128]{2,1,0:T(8,128)(2,1)S(1)} %get-tuple-element.24), channel_id=1, source_target_pairs={{255,0},{0,1},{1,2},{2,3},{3,4},{4,5},{5,6},{6,7},{7,8},{8,9},{9,1... | collective-permute-start | bytes 393224 | tf_op jit(solution)/shard_map/ppermute | solution.py:23
  23.1 14.9 %collective-permute-start.1 = (bf16[4,128,128]{2,1,0:T(8,128)(2,1)S(1)}, bf16[4,128,128]{2,1,0:T(8,128)(2,1)S(1)}, u32[]{:S(2)}, u32[]{:S(2)}) collective-permute-start(bf16[4,128,128]{2,1,0:T(8,128)(2,1)S(1)} %get-tuple-element.25), channel_id=1, source_target_pairs={{1,0},{2,1},{3,2},{4,3},{5,4},{6,5},{7,6},{8,7},{9,8},{10,9},{11,1... | collective-permute-start | bytes 393224 | tf_op jit(solution)/shard_map/ppermute | solution.py:23
  23.6 15.1 %collective-permute-start.2 = (bf16[4,128,128]{2,1,0:T(8,128)(2,1)S(1)}, bf16[4,128,128]{2,1,0:T(8,128)(2,1)S(1)}, u32[]{:S(2)}, u32[]{:S(2)}) collective-permute-start(bf16[4,128,128]{2,1,0:T(8,128)(2,1)S(1)} %get-tuple-element.26), channel_id=1, source_target_pairs={{254,0},{255,1},{0,2},{1,3},{2,4},{3,5},{4,6},{5,7},{6,8},{7,9},{8... | collective-permute-start | bytes 393224 | tf_op jit(solution)/shard_map/ppermute | solution.py:23
  24.6 14.8 %collective-permute-start.3 = (bf16[4,128,128]{2,1,0:T(8,128)(2,1)S(1)}, bf16[4,128,128]{2,1,0:T(8,128)(2,1)S(1)}, u32[]{:S(2)}, u32[]{:S(2)}) collective-permute-start(bf16[4,128,128]{2,1,0:T(8,128)(2,1)S(1)} %get-tuple-element.27), channel_id=1, source_target_pairs={{2,0},{3,1},{4,2},{5,3},{6,4},{7,5},{8,6},{9,7},{10,8},{11,9},{12,... | collective-permute-start | bytes 393224 | tf_op jit(solution)/shard_map/ppermute | solution.py:23
  30.7 1.9 %copy-start = (bf16[32,3,128,128]{3,2,1,0:T(8,128)(2,1)S(1)}, bf16[32,3,128,128]{3,2,1,0:T(8,128)(2,1)}, u32[]{:S(2)}) copy-start(bf16[32,3,128,128]{3,2,1,0:T(8,128)(2,1)} %tiles.5) | copy-start | bytes 9437188
  33.2 4.1 %copy-start.14 = (bf16[128,256]{1,0:T(8,128)(2,1)S(1)}, bf16[128,256]{1,0:T(8,128)(2,1)}, u32[]{:S(2)}) copy-start(bf16[128,256]{1,0:T(8,128)(2,1)} %weight.1) | copy-start | bytes 196612
  33.2 4.1 %copy-start.36 = (bf16[128,256]{1,0:T(8,128)(2,1)S(1)}, bf16[128,256]{1,0:T(8,128)(2,1)}, u32[]{:S(2)}) copy-start(bf16[128,256]{1,0:T(8,128)(2,1)} %param.19) | copy-start | bytes 196612
  33.2 6.7 %copy-start.30 = (s32[32,3]{0,1:T(4,128)S(1)}, s32[32,3]{0,1:T(4,128)}, u32[]{:S(2)}) copy-start(s32[32,3]{0,1:T(4,128)} %param.15) | copy-start | bytes 1156
  33.2 6.7 %copy-start.31 = (f32[256]{0:T(256)S(1)}, f32[256]{0:T(256)}, u32[]{:S(2)}) copy-start(f32[256]{0:T(256)} %param.20) | copy-start | bytes 3076
  41.2 1.6 %copy-start.6 = (f32[4096,128]{1,0:T(8,128)S(1)}, f32[4096,128]{1,0:T(8,128)}, u32[]{:S(2)}) copy-start(f32[4096,128]{1,0:T(8,128)} %copy-done.5) | copy-start | bytes 6291460
  42.8 1.9 %copy-start.7 = (bf16[32,3,128,128]{3,2,1,0:T(8,128)(2,1)S(1)}, bf16[32,3,128,128]{3,2,1,0:T(8,128)(2,1)}, u32[]{:S(2)}) copy-start(bf16[32,3,128,128]{3,2,1,0:T(8,128)(2,1)} %tiles.4) | copy-start | bytes 9437188
  44.7 1.6 %copy-start.10 = (bf16[4096,256]{1,0:T(8,128)(2,1)S(1)}, bf16[4096,256]{1,0:T(8,128)(2,1)}, u32[]{:S(2)}) copy-start(bf16[4096,256]{1,0:T(8,128)(2,1)} %refs_7_.1) | copy-start | bytes 6291460
  49.9 55.4 %copy-start.1 = (bf16[32,3,128,128]{3,2,1,0:T(8,128)(2,1)S(1)}, bf16[32,3,128,128]{3,2,1,0:T(8,128)(2,1)}, u32[]{:S(2)}) copy-start(bf16[32,3,128,128]{3,2,1,0:T(8,128)(2,1)} %tiles.5) | copy-start | bytes 9437188
  49.9 55.4 %copy-start.25 = (s32[32,3]{0,1:T(4,128)S(1)}, s32[32,3]{0,1:T(4,128)}, u32[]{:S(2)}) copy-start(s32[32,3]{0,1:T(4,128)} %param.13) | copy-start | bytes 1156
  75.1 41.9 %all-to-all-start.1 = ((bf16[256,8,128]{2,1,0:T(8,128)(2,1)}), bf16[256,8,128]{2,1,0:T(8,128)(2,1)}, u32[]{:S(2)}, u32[]{:S(2)}) async-start(bf16[256,8,128]{2,1,0:T(8,128)(2,1)} %copy-done.13), calls=%async_computation.1 | async-start | bytes 1048576 | tf_op jit(solution)/shard_map/all_to_all | solution.py:450
  89.1 23.4 %collective-permute-start.4 = (bf16[4,128,128]{2,1,0:T(8,128)(2,1)}, bf16[4,128,128]{2,1,0:T(8,128)(2,1)S(1)}, u32[]{:S(2)}, u32[]{:S(2)}) collective-permute-start(bf16[4,128,128]{2,1,0:T(8,128)(2,1)} %copy-done.35), channel_id=1, source_target_pairs={{1,0},{2,1},{3,2},{4,3},{5,4},{6,5},{7,6},{8,7},{9,8},{10,9},{11,1... | collective-permute-start | bytes 393224 | tf_op jit(solution)/shard_map/ppermute | solution.py:23
  91.6 20.9 %collective-permute-start.5 = (bf16[4,128,128]{2,1,0:T(8,128)(2,1)}, bf16[4,128,128]{2,1,0:T(8,128)(2,1)S(1)}, u32[]{:S(2)}, u32[]{:S(2)}) collective-permute-start(bf16[4,128,128]{2,1,0:T(8,128)(2,1)} %copy-done.34), channel_id=1, source_target_pairs={{255,0},{0,1},{1,2},{2,3},{3,4},{4,5},{5,6},{6,7},{7,8},{8,9},{9,1... | collective-permute-start | bytes 393224 | tf_op jit(solution)/shard_map/ppermute | solution.py:23
  91.6 20.9 %collective-permute-start.6 = (bf16[4,128,128]{2,1,0:T(8,128)(2,1)}, bf16[4,128,128]{2,1,0:T(8,128)(2,1)S(1)}, u32[]{:S(2)}, u32[]{:S(2)}) collective-permute-start(bf16[4,128,128]{2,1,0:T(8,128)(2,1)} %copy-done.33), channel_id=1, source_target_pairs={{2,0},{3,1},{4,2},{5,3},{6,4},{7,5},{8,6},{9,7},{10,8},{11,9},{12,... | collective-permute-start | bytes 393224 | tf_op jit(solution)/shard_map/ppermute | solution.py:23
  105.3 9.5 %collective-permute-start.7 = (bf16[4,128,128]{2,1,0:T(8,128)(2,1)}, bf16[4,128,128]{2,1,0:T(8,128)(2,1)S(1)}, u32[]{:S(2)}, u32[]{:S(2)}) collective-permute-start(bf16[4,128,128]{2,1,0:T(8,128)(2,1)} %copy-done.32), channel_id=1, source_target_pairs={{254,0},{255,1},{0,2},{1,3},{2,4},{3,5},{4,6},{5,7},{6,8},{7,9},{8... | collective-permute-start | bytes 393224 | tf_op jit(solution)/shard_map/ppermute | solution.py:23
  105.3 1.6 %copy-start.9 = (bf16[4096,256]{1,0:T(8,128)(2,1)S(1)}, bf16[4096,256]{1,0:T(8,128)(2,1)}, u32[]{:S(2)}) copy-start(bf16[4096,256]{1,0:T(8,128)(2,1)} %copy-done.8) | copy-start | bytes 6291460
  109.0 5.8 %copy-start.27 = (s32[4,4]{1,0:T(4,128)S(1)}, s32[4,4]{1,0:T(4,128)}, u32[]{:S(2)}) copy-start(s32[4,4]{1,0:T(4,128)} %send.3) | copy-start | bytes 196
  109.0 5.8 %copy-start.29 = (s32[4]{0:T(128)S(1)}, s32[4]{0:T(128)}, u32[]{:S(2)}) copy-start(s32[4]{0:T(128)} %hubs.5) | copy-start | bytes 52
  (23 other events, 19.8 us)

commit v2 on v0

v2 whole, which is shorter than its diff:
```python
import functools

import jax
import jax.numpy as jnp
from jax import lax
from jax.experimental import pallas as pl
from jax.experimental.pallas import tpu as pltpu
from jax.sharding import PartitionSpec as P

OFFSETS = (1, -1, 2, -2)
F32 = jnp.float32
BF16 = jnp.bfloat16
NT = (((1,), (1,)), ((), ()))
TN = (((0,), (0,)), ((), ()))
GROUP = 16
CHUNK = 8
STEP = 8


def partner(i, way, n):
    if way == 0:
        return i ^ 1
    if way == 1:
        return (i + (1 if i & 1 else -1)) % n
    ahead = (i >> 1) & 1 == way - 2
    return (i + (2 if ahead else -2)) % n


def swapped(block, way):
    n = lax.axis_size("dom")
    return lax.ppermute(block, "dom", [(i, partner(i, way, n)) for i in range(n)])


def lists_of_ways():
    me = lax.axis_index("dom")
    odd, odd_chip = me & 1, (me >> 1) & 1
    return odd, 1 - odd, 2 + odd_chip, 3 - odd_chip


def rows_of(chunk, size):
    return pl.ds(pl.multiple_of(chunk * size, size), size)


def params():
    return pltpu.CompilerParams(vmem_limit_bytes=40 << 20)


def hbm(x):
    return pltpu.with_memory_space_constraint(x, pltpu.HBM)


def vmem(x):
    return pltpu.with_memory_space_constraint(x, pltpu.VMEM)


ANY_SPEC = pl.BlockSpec(memory_space=pl.ANY)
HBM_SPEC = pl.BlockSpec(memory_space=pltpu.HBM)
VMEM_SPEC = pl.BlockSpec(memory_space=pltpu.VMEM)


def start(copies):
    for c in copies:
        c.start()


def wait(copies):
    for c in copies:
        c.wait()


def whole(shape):
    return pl.BlockSpec(shape, lambda *_: (0,) * len(shape))


def send_kernel(send_hbm, hubs_hbm, blocks_hbm, *refs):
    lists, per_list = send_hbm.shape
    outs, refs = refs[:lists], refs[lists:]
    hub_out, blocks, send, hubs, sem_in, sems = refs
    owned = hubs.shape[0]
    count, tile, width = blocks.shape
    pairs = [(send_hbm, send), (hubs_hbm, hubs)]
    half = count // 2
    for part in (pl.ds(0, half), pl.ds(half, half)):
        pairs.append((blocks_hbm.at[part], blocks.at[part]))
    loads = [pltpu.make_async_copy(*p, sem_in.at[n]) for n, p in enumerate(pairs)]
    start(loads)
    wait(loads)
    moves = []
    for way, j in enumerate(lists_of_ways()):
        for h in range(per_list):
            moves.append(
                pltpu.make_async_copy(
                    blocks.at[send[j, h]], outs[way].at[h], sems.at[way * per_list + h]
                )
            )
    start(moves)
    place = lax.broadcasted_iota(jnp.int32, (GROUP, width), 0)
    rows = []
    for i in range(owned):
        row = hubs[i]
        base = pl.multiple_of(lax.rem(row, tile) // GROUP * GROUP, GROUP)
        near = blocks[row // tile, pl.ds(base, GROUP), :].astype(F32)
        chosen = jnp.where(place == lax.rem(row, GROUP), near, 0.0)
        rows.append(jnp.sum(chosen, 0, keepdims=True))
    hub_out[...] = jnp.broadcast_to(jnp.concatenate(rows, 0).astype(BF16)[None], hub_out.shape)
    wait(moves)


def gather_sends(send, hubs, blocks, parts):
    lists, per_list = send.shape
    _, tile, width = blocks.shape
    return pl.pallas_call(
        send_kernel,
        out_shape=[jax.ShapeDtypeStruct((per_list, tile, width), BF16)] * lists
        + [
            jax.ShapeDtypeStruct((parts, hubs.shape[0], width), BF16),
            pltpu.VMEM(blocks.shape, BF16),
        ],
        in_specs=[HBM_SPEC] * 3,
        out_specs=[ANY_SPEC] * lists + [VMEM_SPEC, VMEM_SPEC],
        scratch_shapes=[
            pltpu.SMEM(send.shape, jnp.int32),
            pltpu.SMEM(hubs.shape, jnp.int32),
            pltpu.SemaphoreType.DMA((4,)),
            pltpu.SemaphoreType.DMA((lists * per_list,)),
        ],
        compiler_params=params(),
        name="sends",
    )(hbm(send), hbm(hubs), hbm(blocks))


def local_kernel(
    src_hbm, tiles_hbm, remote_hbm, d_hbm, blocks, agg, tiles, remote, d_hidden, src, sem, sem_in
):
    count, per_block, tile, _ = tiles.shape
    chunks = count // STEP

    def fetch(i):
        part = pl.ds(i * STEP, STEP)
        return pltpu.make_async_copy(tiles_hbm.at[part], tiles.at[part], sem_in.at[i])

    index = pltpu.make_async_copy(src_hbm, src, sem.at[0])
    index.start()
    for i in range(chunks):
        fetch(i).start()
    later = [
        pltpu.make_async_copy(remote_hbm, remote, sem.at[1]),
        pltpu.make_async_copy(d_hbm, d_hidden, sem.at[2]),
    ]
    start(later)
    index.wait()

    @pl.loop(0, chunks)
    def _(i):
        fetch(i).wait()
        for b in range(STEP):
            at = i * STEP + b
            taken = [blocks[src[k, at]] for k in range(per_block)]
            edges = [tiles[at, k] for k in range(per_block)]
            agg[rows_of(at, tile), :] = jnp.dot(
                jnp.concatenate(edges, 1), jnp.concatenate(taken, 0), preferred_element_type=F32
            )

    wait(later)


def local_aggregate(src, tiles, remote, d_hidden, blocks):
    count, per_block, tile, _ = tiles.shape
    width = blocks.shape[-1]
    return pl.pallas_call(
        local_kernel,
        out_shape=[
            pltpu.VMEM((count * tile, width), F32),
            pltpu.VMEM(tiles.shape, BF16),
            pltpu.VMEM(remote.shape, BF16),
            pltpu.VMEM(d_hidden.shape, BF16),
        ],
        in_specs=[HBM_SPEC] * 4 + [VMEM_SPEC],
        out_specs=[VMEM_SPEC] * 4,
        scratch_shapes=[
            pltpu.SMEM(src.shape, jnp.int32),
            pltpu.SemaphoreType.DMA((3,)),
            pltpu.SemaphoreType.DMA((count // STEP,)),
        ],
        compiler_params=params(),
        cost_estimate=pl.CostEstimate(
            flops=2 * tiles.size * width, bytes_accessed=8 << 20, transcendentals=0
        ),
        name="local_aggregate",
    )(hbm(src), hbm(tiles), hbm(remote), hbm(d_hidden), vmem(blocks))


def layer_kernel(src_hbm, *refs):
    lists = len(OFFSETS)
    tiles, rows, agg_local, d_hidden = refs[:4]
    halos, refs = refs[4 : 4 + lists], refs[4 + lists :]
    hub, self_hbm, neigh_hbm, bias_hbm, hidden, d_pre_out, d_agg_out = refs[:7]
    backs, refs = refs[7 : 7 + lists], refs[7 + lists :]
    packed, src, weights, bias, table, rem_grad, backs_out, w_grad, b_grad, spread = refs[:10]
    pack_out, sem_t, sem_back = refs[10:]
    count, per_block, tile, _ = tiles.shape
    width = rows.shape[-1]
    per_list = halos[0].shape[0]
    halo_count = lists * per_list
    hub_blocks = hub.shape[0]
    slots = [j ^ 1 for j in lists_of_ways()]
    pairs = [
        (src_hbm, src),
        (hub, table.at[pl.ds(halo_count, hub_blocks)]),
        (self_hbm, weights.at[pl.ds(0, width)]),
        (neigh_hbm, weights.at[pl.ds(width, width)]),
        (bias_hbm, bias),
    ]
    for w, s in enumerate(slots):
        pairs.append((halos[w], table.at[pl.ds(s * per_list, per_list)]))
    moves = [pltpu.make_async_copy(*p, sem_t.at[n]) for n, p in enumerate(pairs)]
    start(moves)
    rem_grad[...] = jnp.zeros_like(rem_grad)
    w_grad[...] = jnp.zeros_like(w_grad)
    b_grad[...] = jnp.zeros_like(b_grad)
    wait(moves)

    @pl.loop(0, count // STEP)
    def _(i):
        many = rows_of(i, STEP * tile)

        def edges(b):
            return jnp.concatenate([tiles[i * STEP + b, k] for k in range(per_block)], 1)

        sources = [[src[k, i * STEP + b] for k in range(per_block)] for b in range(STEP)]
        remote = [
            jnp.dot(
                edges(b),
                jnp.concatenate([table[s] for s in sources[b]], 0),
                preferred_element_type=F32,
            )
            for b in range(STEP)
        ]
        agg = agg_local[many, :] + jnp.concatenate(remote, 0)
        both = jnp.concatenate([rows[many, :], agg.astype(BF16)], 1)
        pre = jnp.dot(both, weights[...], preferred_element_type=F32) + bias[...]
        sig = jax.nn.sigmoid(pre)
        hidden[many, :] = (pre * sig).astype(BF16)
        d_pre = d_hidden[many, :].astype(F32) * (sig * (1.0 + pre * (1.0 - sig)))
        b_grad[...] += jnp.sum(d_pre.reshape(-1, 8, d_pre.shape[-1]), 0)
        d_pre_b = d_pre.astype(BF16)
        d_pre_out[many, :] = d_pre_b
        d_agg = lax.dot_general(weights[width:, :], d_pre_b, NT, preferred_element_type=F32)
        d_agg = d_agg.astype(BF16)
        for b in range(STEP):
            own = d_agg[:, b * tile : (b + 1) * tile]
            d_agg_out[i * STEP + b] = own
            terms = jnp.dot(own, edges(b), preferred_element_type=F32)
            for k, s in enumerate(sources[b]):
                rem_grad[s] += terms[:, k * tile : (k + 1) * tile]
        w_grad[...] += lax.dot_general(d_pre_b, both, TN, preferred_element_type=F32)

    sent = []
    for w, s in enumerate(slots):
        backs_out[w] = rem_grad[pl.ds(s * per_list, per_list)].astype(BF16)
        sent.append(pltpu.make_async_copy(backs_out.at[w], backs[w], sem_back.at[w]))
    start(sent)
    parts, chunk, _ = packed.shape
    owned = hub_blocks * tile // parts
    hub_rows = jnp.concatenate(
        [jnp.transpose(rem_grad[halo_count + q]) for q in range(hub_blocks)], 0
    )
    split = hub_rows.reshape(parts, owned, width)
    for i in range(owned):
        spread[pl.ds(i, parts, stride=chunk), :] = split[:, i, :]
    spread[pl.ds(owned, parts, stride=chunk), :] = w_grad[:, :width]
    spread[pl.ds(owned + 1, parts, stride=chunk), :] = w_grad[:, width:]
    total = jnp.sum(b_grad[...], 0, keepdims=True)
    high = total.astype(BF16).astype(F32)
    lane = lax.broadcasted_iota(jnp.int32, (width, parts), 0)
    two = jnp.where(lane == 0, high, jnp.where(lane == 1, total - high, 0.0))
    spread[pl.ds(owned + 2, parts, stride=chunk), :] = jnp.transpose(two)
    for i in range(owned + 3, chunk):
        spread[pl.ds(i, parts, stride=chunk), :] = jnp.zeros((parts, width), F32)
    pack_out[...] = spread[...].reshape(parts, chunk, width).astype(BF16)
    last = pltpu.make_async_copy(pack_out, packed, sem_back.at[lists])
    last.start()
    wait(sent)
    last.wait()


def layer(src, tiles, rows, agg_local, halos, hub, w_self, w_neigh, bias, d_hidden, parts):
    count, per_block, tile, _ = tiles.shape
    nodes, width = rows.shape
    units = d_hidden.shape[-1]
    lists, per_list = len(halos), halos[0].shape[0]
    table = lists * per_list + hub.shape[0]
    packed = (parts, CHUNK, width)
    return pl.pallas_call(
        layer_kernel,
        out_shape=[
            pltpu.VMEM((nodes, units), BF16),
            pltpu.VMEM((nodes, units), BF16),
            pltpu.VMEM((count, width, tile), BF16),
        ]
        + [jax.ShapeDtypeStruct((per_list, width, tile), BF16)] * lists
        + [jax.ShapeDtypeStruct(packed, BF16)],
        in_specs=[HBM_SPEC] + [VMEM_SPEC] * 4 + [HBM_SPEC] * (lists + 4),
        out_specs=[VMEM_SPEC] * 3 + [ANY_SPEC] * (lists + 1),
        scratch_shapes=[
            pltpu.SMEM(src.shape, jnp.int32),
            pltpu.VMEM((2 * width, units), BF16),
            pltpu.VMEM((1, units), F32),
            pltpu.VMEM((table, tile, width), BF16),
            pltpu.VMEM((table, width, tile), F32),
            pltpu.VMEM((lists, per_list, width, tile), BF16),
            pltpu.VMEM((units, 2 * width), F32),
            pltpu.VMEM((8, units), F32),
            pltpu.VMEM((parts * CHUNK, width), F32),
            pltpu.VMEM(packed, BF16),
            pltpu.SemaphoreType.DMA((lists + 5,)),
            pltpu.SemaphoreType.DMA((lists + 1,)),
        ],
        compiler_params=params(),
        cost_estimate=pl.CostEstimate(
            flops=4 * tiles.size * width + 12 * nodes * width * units,
            bytes_accessed=14 << 20,
            transcendentals=nodes * units,
        ),
        name="layer",
    )(
        hbm(src),
        vmem(tiles),
        vmem(rows),
        vmem(agg_local),
        vmem(d_hidden),
        *[hbm(x) for x in (*halos, hub, w_self, w_neigh, bias)],
    )


def back_kernel(src_hbm, weight_hbm, tiles, d_pre, d_agg, hidden, out, total, src, weight, sems):
    count, per_block, tile, _ = tiles.shape
    size = STEP * tile
    result = pltpu.make_async_copy(hidden, out, sems.at[0])
    result.start()
    loads = [
        pltpu.make_async_copy(src_hbm, src, sems.at[1]),
        pltpu.make_async_copy(weight_hbm, weight, sems.at[2]),
    ]
    start(loads)
    total[...] = jnp.zeros_like(total)
    wait(loads)

    @pl.loop(0, count // STEP)
    def _(i):
        own = lax.dot_general(
            weight[...], d_pre[rows_of(i, size), :], NT, preferred_element_type=F32
        )
        for b in range(STEP):
            at = i * STEP + b
            total[at] += own[:, b * tile : (b + 1) * tile]
            edges = jnp.concatenate([tiles[at, k] for k in range(per_block)], 1)
            terms = jnp.dot(d_agg[at], edges, preferred_element_type=F32)
            for k in range(per_block):
                s = src[k, at]
                total[s] += terms[:, k * tile : (k + 1) * tile]

    result.wait()


def local_backward(src, tiles, d_pre, d_agg, weight, hidden):
    count, per_block, tile, _ = tiles.shape
    width, units = weight.shape
    return pl.pallas_call(
        back_kernel,
        out_shape=[
            jax.ShapeDtypeStruct(hidden.shape, BF16),
            pltpu.VMEM((count, width, tile), F32),
        ],
        in_specs=[HBM_SPEC] * 2 + [VMEM_SPEC] * 4,
        out_specs=[ANY_SPEC, VMEM_SPEC],
        scratch_shapes=[
            pltpu.SMEM(src.shape, jnp.int32),
            pltpu.VMEM(weight.shape, BF16),
            pltpu.SemaphoreType.DMA((3,)),
        ],
        compiler_params=params(),
        cost_estimate=pl.CostEstimate(
            flops=2 * tiles.size * width + 2 * d_pre.size * width,
            bytes_accessed=8 << 20,
            transcendentals=0,
        ),
        name="local_backward",
    )(hbm(src), hbm(weight), vmem(tiles), vmem(d_pre), vmem(d_agg), vmem(hidden))


def collect_kernel(send_hbm, hubs_hbm, _, *refs):
    lists, per_list = send_hbm.shape
    halos_hbm = refs[:lists]
    total, out, near, send, hubs, halos, turned, sem_in, sem_out = refs[lists:]
    count, width, tile = total.shape
    pairs = [(send_hbm, send), (hubs_hbm, hubs)]
    pairs += [(halos_hbm[way], halos.at[way]) for way in range(lists)]
    loads = [pltpu.make_async_copy(*p, sem_in.at[n]) for n, p in enumerate(pairs)]
    start(loads)
    wait(loads)
    for way, j in enumerate(lists_of_ways()):
        for h in range(per_list):
            total[send[j, h]] += halos[way, h].astype(F32)
    chunks = sem_out.shape[0]
    each = count // chunks
    stores = []
    for c in range(chunks):
        for b in range(c * each, (c + 1) * each):
            turned[b * tile : (b + 1) * tile, :] = jnp.transpose(total[b]).astype(BF16)
        part = pl.ds(c * each * tile, each * tile)
        stores.append(pltpu.make_async_copy(turned.at[part], out.at[part], sem_out.at[c]))
        stores[-1].start()
    for i in range(hubs.shape[0]):
        row = hubs[i]
        block = jnp.transpose(total[row // tile])
        want = lax.rem(row, tile) // GROUP
        part = jnp.zeros((GROUP, width), F32)
        for g in range(tile // GROUP):
            part = jnp.where(want == g, block[g * GROUP : (g + 1) * GROUP], part)
        near[i] = part
    wait(stores)


def collect(send, hubs, grad, halos):
    count, width, tile = grad.shape
    lists = len(halos)
    near = (hubs.shape[0], GROUP, width)
    return pl.pallas_call(
        collect_kernel,
        out_shape=[
            pltpu.VMEM(grad.shape, F32),
            jax.ShapeDtypeStruct((count * tile, width), BF16),
            pltpu.VMEM(near, F32),
        ],
        in_specs=[HBM_SPEC] * 2 + [VMEM_SPEC] + [HBM_SPEC] * lists,
        out_specs=[VMEM_SPEC, ANY_SPEC, VMEM_SPEC],
        scratch_shapes=[
            pltpu.SMEM(send.shape, jnp.int32),
            pltpu.SMEM(hubs.shape, jnp.int32),
            pltpu.VMEM((lists,) + halos[0].shape, BF16),
            pltpu.VMEM((count * tile, width), BF16),
            pltpu.SemaphoreType.DMA((2 + lists,)),
            pltpu.SemaphoreType.DMA((4,)),
        ],
        input_output_aliases={2: 0},
        compiler_params=params(),
        cost_estimate=pl.CostEstimate(
            flops=grad.size * 8, bytes_accessed=4 << 20, transcendentals=0
        ),
        name="collect",
    )(hbm(send), hbm(hubs), vmem(grad), *[hbm(x) for x in halos])[1:]


def finish_kernel(
    hubs_hbm, pieces_hbm, near, _, grad, g_self, g_neigh, g_bias, hubs, pieces, rows, sem_in, sems
):
    owned = hubs.shape[0]
    chunks = sem_in.shape[0] - 1
    each = pieces.shape[0] // chunks
    index = pltpu.make_async_copy(hubs_hbm, hubs, sem_in.at[chunks])
    index.start()
    loads = []
    for c in range(chunks):
        part = pl.ds(c * each, each)
        loads.append(pltpu.make_async_copy(pieces_hbm.at[part], pieces.at[part], sem_in.at[c]))
    start(loads)
    index.wait()
    total = jnp.zeros(pieces.shape[1:], F32)
    for c in range(chunks):
        loads[c].wait()
        total += jnp.sum(pieces[c * each : (c + 1) * each].astype(F32), 0)
    g_self[...] = total[owned : owned + 1, :]
    g_neigh[...] = total[owned + 1 : owned + 2, :]
    last = total[owned + 2 : owned + 3, :]
    g_bias[...] = jnp.broadcast_to(last[:, 0:1] + last[:, 1:2], last.shape)
    place = lax.broadcasted_iota(jnp.int32, (GROUP, total.shape[-1]), 0)
    for i in range(owned):
        value = near[i]
        for m in range(owned):
            same = hubs[m] // GROUP == hubs[i] // GROUP
            hit = jnp.logical_and(place == lax.rem(hubs[m], GROUP), same)
            value = value + jnp.where(hit, total[m : m + 1, :], 0.0)
        rows[i] = value.astype(BF16)

    def fresh(i):
        new = hubs[i] >= 0
        for m in range(i):
            new = jnp.logical_and(new, hubs[m] // GROUP != hubs[i] // GROUP)
        return new

    def move(i):
        base = pl.multiple_of(hubs[i] // GROUP * GROUP, GROUP)
        return pltpu.make_async_copy(rows.at[i], grad.at[pl.ds(base, GROUP), :], sems.at[i])

    for i in range(owned):
        pl.when(fresh(i))(lambda i=i: move(i).start())
    for i in range(owned):
        pl.when(fresh(i))(lambda i=i: move(i).wait())


def finish(hubs, pieces, near, grad):
    owned, _, width = near.shape
    line = jax.ShapeDtypeStruct((1, width), F32)
    return pl.pallas_call(
        finish_kernel,
        out_shape=[jax.ShapeDtypeStruct(grad.shape, grad.dtype), line, line, line],
        in_specs=[HBM_SPEC, HBM_SPEC, VMEM_SPEC, ANY_SPEC],
        out_specs=[ANY_SPEC, VMEM_SPEC, VMEM_SPEC, VMEM_SPEC],
        scratch_shapes=[
            pltpu.SMEM(hubs.shape, jnp.int32),
            pltpu.VMEM(pieces.shape, BF16),
            pltpu.VMEM((owned, GROUP, width), BF16),
            pltpu.SemaphoreType.DMA((5,)),
            pltpu.SemaphoreType.DMA((owned,)),
        ],
        input_output_aliases={3: 0},
        compiler_params=params(),
        name="finish",
    )(hbm(hubs), hbm(pieces), vmem(near), grad)


def shards(
    features,
    local_tiles,
    local_src,
    remote_tiles,
    remote_src,
    send_blocks,
    hub_rows,
    w_self,
    w_neigh,
    bias,
    d_hidden,
):
    parts = lax.axis_size("dom")
    nodes, width = features.shape
    tile = local_tiles.shape[-1]
    owned = hub_rows.shape[0]
    blocks = features.reshape(nodes // tile, tile, width)
    *sends, hub_mine, own = gather_sends(send_blocks, hub_rows, blocks, parts)
    hub_all = lax.all_to_all(hub_mine, "dom", 0, 0)
    halos = [swapped(b, way) for way, b in enumerate(sends)]
    agg_local, tiles_l, tiles_r, d_hid = local_aggregate(
        local_src.T, local_tiles, remote_tiles, d_hidden, own
    )
    hidden, d_pre, d_agg, *rest = layer(
        remote_src.T,
        tiles_r,
        own.reshape(nodes, width),
        agg_local,
        halos,
        hub_all.reshape(parts * owned // tile, tile, width),
        w_self,
        w_neigh,
        bias[None],
        d_hid,
        parts,
    )
    *backs, packed = rest
    pieces = lax.all_to_all(packed, "dom", 0, 0)
    returned = [swapped(b, way) for way, b in enumerate(backs)]
    out, grad_t = local_backward(local_src.T, tiles_l, d_pre, d_agg, w_self, hidden)
    rough, near = collect(send_blocks, hub_rows, grad_t, returned)
    grad, g_self, g_neigh, g_bias = finish(hub_rows, pieces, near, rough)
    return (out, grad, g_self.reshape(width, 1), g_neigh.reshape(width, 1), g_bias[0, :1])


def solution(mesh):
    in_specs = (
        P("dom", None),
        P("dom", None, None, None),
        P("dom", None),
        P("dom", None, None, None),
        P("dom", None),
        P("dom", None),
        P("dom"),
        P(),
        P(),
        P(),
        P("dom", None),
    )
    out_specs = (P("dom", None), P("dom", None), P(None, "dom"), P(None, "dom"), P("dom"))
    return jax.shard_map(shards, mesh=mesh, in_specs=in_specs, out_specs=out_specs, check_vma=False)
```

time: 439 us -> 96.9 us (0.22)
  blocking collectives: 143 us -> 0 us
  waiting for transfers between devices: 115 us -> 4.63 us
  other arithmetic: 64.5 us -> 0 us
  local copies, waits for them, and re-layouts: 49.3 us -> 21 us
  matrix products: 28 us -> 0 us
  Pallas kernels: 0 us -> 24.5 us
  starting transfers between devices: 22.2 us -> 45.4 us
  between operations: 14.2 us -> 0.85 us
    unnamed x2 -> x0, waiting for transfers between devices: 115 us -> none
    unnamed x1 -> x0, blocking collectives: 77.8 us -> none
    all_gather x1 -> x0, blocking collectives: 65.1 us -> none  [shards(): hub_all = lax.all_gather(features[hub_rows], 'dom', axis=0, tiled=True)]
    scatter-add x7 -> x0, other arithmetic: 52.7 us -> none  [the longest x1 20 us: shards(): jnp.zeros((remote.shape[0], tile, width), jnp.float32).at[remote_src]]
    dot_general x10 -> x0, matrix products: 28 us -> none  [the longest x1 3.99 us: shards(): jnp.dot(features, w_self, preferred_element_type=jnp.float32)]
    pallas_call x0 -> x6, Pallas kernels: none -> 24.5 us  [the longest x1 9.76 us: layer(): pl.pallas_call(layer_kernel, out_shape=[pltpu.VMEM((nodes, units), BF16),...]
    all_to_all x0 -> x2, starting transfers between devices: none -> 23.9 us  [the longest x1 15.7 us: shards(): hub_all = lax.all_to_all(hub_mine, 'dom', 0, 0)]
    gather x7 -> x0, local copies, waits for them, and re-layouts: 19.6 us -> none  [the longest x4 9.79 us: shards(): received.append(shifted(blocks[send_blocks[j]], 'dom', step))]
  transfers between devices with their start and end apart: 9 -> 10, of which waited for: 1 -> 1; matrix products, arithmetic and copies ran while one was open for 17% -> 0% of each run, Pallas kernels for 0% -> 10%
where the time goes in v2:
time: 96.9 us; the launch traced here: 96.3 us
  starting transfers between devices  45.4 us (47%)
  Pallas kernels  24.5 us (25%)
  local copies, waits for them, and re-layouts  21 us (22%)
  waiting for transfers between devices  4.63 us (5%)
    ppermute x8, starting transfers between devices, swapped(): lax.ppermute(block, 'dom', [(i, partner(i, way, n)) for i in range(n)])  21.5 us
    unnamed x46, local copies, waits for them, and re-layouts  21 us
    all_to_all x1, starting transfers between devices, shards(): hub_all = lax.all_to_all(hub_mine, 'dom', 0, 0)  15.7 us
    pallas_call x1, Pallas kernels, layer(): pl.pallas_call(layer_kernel, out_shape=[pltpu.VMEM((nodes, units), BF16),...  9.76 us
    all_to_all x1, starting transfers between devices, shards(): pieces = lax.all_to_all(packed, 'dom', 0, 0)  8.2 us
    ppermute x8, waiting for transfers between devices, swapped(): lax.ppermute(block, 'dom', [(i, partner(i, way, n)) for i in range(n)])  4.62 us
    pallas_call x1, Pallas kernels, local_aggregate(): pl.pallas_call(local_kernel, out_shape=[pltpu.VMEM((count * tile, width),...  3.54 us
    pallas_call x1, Pallas kernels, local_backward(): pl.pallas_call(back_kernel, out_shape=[jax.ShapeDtypeStruct(hidden.shape,...  3.41 us
  transfers between devices with their start and end apart: 10, of which 1 were waited for; matrix products, arithmetic and copies ran while one was open for 0% of the time, Pallas kernels for 10%

profile of v2, /device:TPU:1, one launch (start us, length us, event | category | flops | bytes accessed | tf_op | source)
XLA Modules:
  0.0 96.3 jit_solution(3151045363027257458)
XLA Ops:
  0.6 2.9 %sends.1 = (bf16[4,128,128]{2,1,0:T(8,128)(2,1)S(1)}, bf16[4,128,128]{2,1,0:T(8,128)(2,1)S(1)}, bf16[4,128,128]{2,1,0:T(8,128)(2,1)S(1)}, bf16[4,128,128]{2,1,0:...) custom-call(s32[4,4]{1,0:T(4,128)} %send_hbm.3, s32[4]{0:T(128)} %hubs_hbm.5, ...), custom_call_target="tpu_custom_call" | custom-call | tf_op jit(solution)/shard_map/sends/pallas_call | solution.py:112
  3.6 15.7 %all-to-all-start = ((bf16[256,4,128]{2,1,0:T(4,128)(2,1)}), bf16[256,4,128]{2,1,0:T(4,128)(2,1)S(1)}, u32[]{:S(2)}, u32[]{:S(2)}) async-start(bf16[256,4,128]{2,1,0:T(4,128)(2,1)} %get-tuple-element.40), calls=%async_computation | async-start | bytes 524288 | tf_op jit(solution)/shard_map/all_to_all | solution.py:542
  19.2 2.2 %collective-permute-start = (bf16[4,128,128]{2,1,0:T(8,128)(2,1)S(1)}, bf16[4,128,128]{2,1,0:T(8,128)(2,1)S(1)}, u32[]{:S(2)}, u32[]{:S(2)}) collective-permute-start(bf16[4,128,128]{2,1,0:T(8,128)(2,1)S(1)} %get-tuple-element.36), channel_id=1, source_target_pairs={{0,1},{1,0},{2,3},{3,2},{4,5},{5,4},{6,7},{7,6},{8,9},{9,8},{10,11... | collective-permute-start | bytes 393224 | tf_op jit(solution)/shard_map/ppermute | solution.py:31
  22.7 7.3 %collective-permute-start.3 = (bf16[4,128,128]{2,1,0:T(8,128)(2,1)S(1)}, bf16[4,128,128]{2,1,0:T(8,128)(2,1)S(1)}, u32[]{:S(2)}, u32[]{:S(2)}) collective-permute-start(bf16[4,128,128]{2,1,0:T(8,128)(2,1)S(1)} %get-tuple-element.39), channel_id=1, source_target_pairs={{0,254},{1,255},{2,4},{3,5},{4,2},{5,3},{6,8},{7,9},{8,6},{9,7},{1... | collective-permute-start | bytes 393224 | tf_op jit(solution)/shard_map/ppermute | solution.py:31
  30.0 3.5 %local_aggregate.1 = (f32[4096,128]{1,0:T(8,128)S(1)}, bf16[32,3,128,128]{3,2,1,0:T(8,128)(2,1)S(1)}, bf16[32,3,128,128]{3,2,1,0:T(8,128)(2,1)S(1)}, bf16[4096,256]{1,0:T(8,128)(2,1)S(1)}) custom-call(s32[3,32]{1,0:T(4,128)} %bitcast.13, bf16[32,3,128,128]{3,2,1,0:T(8,128)(2,1)} %tiles_hbm.1, bf16[32,3,128,128]{3,2,1,0:T(8,128)(2,1)} %remote_hbm.1, ...), custom_call_target="tpu_custom_call" | custom-call | flops 402653184 | bytes 8388608 | tf_op jit(solution)/shard_map/local_aggregate/pallas_call | solution.py:170
  33.6 1.6 %copy-done = bf16[32,3,128,128]{3,2,1,0:T(8,128)(2,1)} copy-done((bf16[32,3,128,128]{3,2,1,0:T(8,128)(2,1)}, bf16[32,3,128,128]{3,2,1,0:T(8,128)(2,1)S(1)}, u32[]{:S(2)}) %copy-start) | copy-done | bytes 3145752
  35.2 1.7 %copy-done.2 = bf16[32,3,128,128]{3,2,1,0:T(8,128)(2,1)} copy-done((bf16[32,3,128,128]{3,2,1,0:T(8,128)(2,1)}, bf16[32,3,128,128]{3,2,1,0:T(8,128)(2,1)S(1)}, u32[]{:S(2)}) %copy-start.2) | copy-done | bytes 3145752
  36.9 1.3 %copy-done.6 = f32[4096,128]{1,0:T(8,128)} copy-done((f32[4096,128]{1,0:T(8,128)}, f32[4096,128]{1,0:T(8,128)S(1)}, u32[]{:S(2)}) %copy-start.6) | copy-done | bytes 2097176
  38.2 1.4 %copy-done.8 = bf16[4096,256]{1,0:T(8,128)(2,1)} copy-done((bf16[4096,256]{1,0:T(8,128)(2,1)}, bf16[4096,256]{1,0:T(8,128)(2,1)S(1)}, u32[]{:S(2)}) %copy-start.8) | copy-done | bytes 2097176
  40.5 1.9 %copy-done.3 = bf16[32,3,128,128]{3,2,1,0:T(8,128)(2,1)S(1)} copy-done((bf16[32,3,128,128]{3,2,1,0:T(8,128)(2,1)S(1)}, bf16[32,3,128,128]{3,2,1,0:T(8,128)(2,1)}, u32[]{:S(2)}) %copy-start.3) | copy-done | bytes 3145752
  42.4 1.6 %copy-done.7 = f32[4096,128]{1,0:T(8,128)S(1)} copy-done((f32[4096,128]{1,0:T(8,128)S(1)}, f32[4096,128]{1,0:T(8,128)}, u32[]{:S(2)}) %copy-start.7) | copy-done | bytes 2097176
  44.0 1.6 %copy-done.9 = bf16[4096,256]{1,0:T(8,128)(2,1)S(1)} copy-done((bf16[4096,256]{1,0:T(8,128)(2,1)S(1)}, bf16[4096,256]{1,0:T(8,128)(2,1)}, u32[]{:S(2)}) %copy-start.9) | copy-done | bytes 2097176
  45.6 9.8 %layer.1 = (bf16[4096,256]{1,0:T(8,128)(2,1)S(1)}, bf16[4096,256]{1,0:T(8,128)(2,1)S(1)}, bf16[32,128,128]{2,1,0:T(8,128)(2,1)S(1)}, bf16[4,128,128]{2,1,0:T(8,1...) custom-call(s32[3,32]{1,0:T(4,128)} %bitcast.15, ...), custom_call_target="tpu_custom_call" | custom-call | flops 2415919104 | bytes 14680064 | tf_op jit(solution)/shard_map/layer/pallas_call | solution.py:294
  55.3 1.3 %copy-done.4 = bf16[4096,256]{1,0:T(8,128)(2,1)} copy-done((bf16[4096,256]{1,0:T(8,128)(2,1)}, bf16[4096,256]{1,0:T(8,128)(2,1)S(1)}, u32[]{:S(2)}) %copy-start.4) | copy-done | bytes 2097176
  58.3 8.2 %all-to-all-start.1 = ((bf16[256,8,128]{2,1,0:T(8,128)(2,1)}), bf16[256,8,128]{2,1,0:T(8,128)(2,1)S(1)}, u32[]{:S(2)}, u32[]{:S(2)}) async-start(bf16[256,8,128]{2,1,0:T(8,128)(2,1)} %get-tuple-element.45), calls=%async_computation.1 | async-start | bytes 1048576 | tf_op jit(solution)/shard_map/all_to_all | solution.py:561
  66.5 2.2 %collective-permute-start.4 = (bf16[4,128,128]{2,1,0:T(8,128)(2,1)}, bf16[4,128,128]{2,1,0:T(8,128)(2,1)S(1)}, u32[]{:S(2)}, u32[]{:S(2)}) collective-permute-start(bf16[4,128,128]{2,1,0:T(8,128)(2,1)} %copy-done.12), channel_id=1, source_target_pairs={{0,1},{1,0},{2,3},{3,2},{4,5},{5,4},{6,7},{7,6},{8,9},{9,8},{10,11... | collective-permute-start | bytes 393224 | tf_op jit(solution)/shard_map/ppermute | solution.py:31
  69.9 7.3 %collective-permute-start.7 = (bf16[4,128,128]{2,1,0:T(8,128)(2,1)S(1)}, bf16[4,128,128]{2,1,0:T(8,128)(2,1)S(1)}, u32[]{:S(2)}, u32[]{:S(2)}) collective-permute-start(bf16[4,128,128]{2,1,0:T(8,128)(2,1)S(1)} %get-tuple-element.50), channel_id=1, source_target_pairs={{0,254},{1,255},{2,4},{3,5},{4,2},{5,3},{6,8},{7,9},{8,6},{9,7},{1... | collective-permute-start | bytes 393224 | tf_op jit(solution)/shard_map/ppermute | solution.py:31
  77.3 1.9 %copy-done.1 = bf16[32,3,128,128]{3,2,1,0:T(8,128)(2,1)S(1)} copy-done((bf16[32,3,128,128]{3,2,1,0:T(8,128)(2,1)S(1)}, bf16[32,3,128,128]{3,2,1,0:T(8,128)(2,1)}, u32[]{:S(2)}) %copy-start.1) | copy-done | bytes 3145752
  79.1 1.6 %copy-done.5 = bf16[4096,256]{1,0:T(8,128)(2,1)S(1)} copy-done((bf16[4096,256]{1,0:T(8,128)(2,1)S(1)}, bf16[4096,256]{1,0:T(8,128)(2,1)}, u32[]{:S(2)}) %copy-start.5) | copy-done | bytes 2097176
  80.7 1.2 %copy-done.11 = bf16[32,128,128]{2,1,0:T(8,128)(2,1)S(1)} copy-done((bf16[32,128,128]{2,1,0:T(8,128)(2,1)S(1)}, bf16[32,128,128]{2,1,0:T(8,128)(2,1)}, u32[]{:S(2)}) %copy-start.11) | copy-done | bytes 1048600
  82.0 3.4 %local_backward.1 = (bf16[4096,256]{1,0:T(8,128)(2,1)}, f32[32,128,128]{2,1,0:T(8,128)S(1)}) custom-call(s32[3,32]{1,0:T(4,128)} %bitcast.14, bf16[128,256]{1,0:T(8,128)(2,1)} %weight_hbm.1, bf16[32,3,128,128]{3,2,1,0:T(8,128)(2,1)S(1)} %copy-done.1, bf16[4096,256]{1,0:T(8,128)(2,1)S(1)} %copy-done.5, bf16[32,128,128]{2,1,0:T(8,128)(2,1)S(1)} %copy-done.11, ...), custom_call_target="tpu_custom_call" | custom-call | flops 671088640 | bytes 8388608 | tf_op jit(solution)/shard_map/local_backward/pallas_call | solution.py:369
  85.4 4.6 %collective-permute-done.7.refs_3_ = bf16[4,128,128]{2,1,0:T(8,128)(2,1)S(1)} collective-permute-done((bf16[4,128,128]{2,1,0:T(8,128)(2,1)S(1)}, bf16[4,128,128]{2,1,0:T(8,128)(2,1)S(1)}, u32[]{:S(2)}, u32[]{:S(2)}) %collective-permute-start.7) | collective-permute-done | bytes 131104 | tf_op jit(solution)/shard_map/ppermute | solution.py:31
  90.7 2.4 %collect.1 = (f32[32,128,128]{2,1,0:T(8,128)S(1)}, bf16[4096,128]{1,0:T(8,128)(2,1)}, f32[4,16,128]{2,1,0:T(8,128)S(1)}) custom-call(s32[4,4]{1,0:T(4,128)} %send_hbm.3, s32[4]{0:T(128)} %hubs_hbm.5, f32[32,128,128]{2,1,0:T(8,128)S(1)} %get-tuple-element.46._, bf16[4,128,128]{2,1,0:T(8,128)(2,1)} %copy-done.19, ...), custom_call_target="tpu_custom_call", output_to_operand_aliasing={{0}: (2, {})} | custom-call | flops 4194304 | bytes 4194304 | tf_op jit(solution)/shard_map/collect/pallas_call | solution.py:429
  93.9 2.4 %finish.1 = (bf16[4096,128]{1,0:T(8,128)(2,1)}, f32[1,128]{1,0:T(1,128)}, f32[1,128]{1,0:T(1,128)}, f32[1,128]{1,0:T(1,128)}) custom-call(s32[4]{0:T(128)} %hubs_hbm.5, bf16[256,8,128]{2,1,0:T(8,128)(2,1)} %copy-done.13, f32[4,16,128]{2,1,0:T(8,128)S(1)} %get-tuple-element.51.near, ...), custom_call_target="tpu_custom_call", output_to_operand_aliasing={{0}: (3, {})} | custom-call | tf_op jit(solution)/shard_map/finish/pallas_call | solution.py:505
  (48 shorter events, 6.3 us)
Async XLA Ops:
  3.6 36.1 %all-to-all-start = ((bf16[256,4,128]{2,1,0:T(4,128)(2,1)}), bf16[256,4,128]{2,1,0:T(4,128)(2,1)S(1)}, u32[]{:S(2)}, u32[]{:S(2)}) async-start(bf16[256,4,128]{2,1,0:T(4,128)(2,1)} %get-tuple-element.40), calls=%async_computation | async-start | bytes 524288 | tf_op jit(solution)/shard_map/all_to_all | solution.py:542
  19.2 20.4 %collective-permute-start = (bf16[4,128,128]{2,1,0:T(8,128)(2,1)S(1)}, bf16[4,128,128]{2,1,0:T(8,128)(2,1)S(1)}, u32[]{:S(2)}, u32[]{:S(2)}) collective-permute-start(bf16[4,128,128]{2,1,0:T(8,128)(2,1)S(1)} %get-tuple-element.36), channel_id=1, source_target_pairs={{0,1},{1,0},{2,3},{3,2},{4,5},{5,4},{6,7},{7,6},{8,9},{9,8},{10,11... | collective-permute-start | bytes 393224 | tf_op jit(solution)/shard_map/ppermute | solution.py:31
  21.5 18.1 %collective-permute-start.1 = (bf16[4,128,128]{2,1,0:T(8,128)(2,1)S(1)}, bf16[4,128,128]{2,1,0:T(8,128)(2,1)S(1)}, u32[]{:S(2)}, u32[]{:S(2)}) collective-permute-start(bf16[4,128,128]{2,1,0:T(8,128)(2,1)S(1)} %get-tuple-element.37), channel_id=1, source_target_pairs={{0,255},{1,2},{2,1},{3,4},{4,3},{5,6},{6,5},{7,8},{8,7},{9,10},{10... | collective-permute-start | bytes 393224 | tf_op jit(solution)/shard_map/ppermute | solution.py:31
  21.5 18.2 %collective-permute-start.2 = (bf16[4,128,128]{2,1,0:T(8,128)(2,1)S(1)}, bf16[4,128,128]{2,1,0:T(8,128)(2,1)S(1)}, u32[]{:S(2)}, u32[]{:S(2)}) collective-permute-start(bf16[4,128,128]{2,1,0:T(8,128)(2,1)S(1)} %get-tuple-element.38), channel_id=1, source_target_pairs={{0,2},{1,3},{2,0},{3,1},{4,6},{5,7},{6,4},{7,5},{8,10},{9,11},{10,... | collective-permute-start | bytes 393224 | tf_op jit(solution)/shard_map/ppermute | solution.py:31
  22.7 17.0 %collective-permute-start.3 = (bf16[4,128,128]{2,1,0:T(8,128)(2,1)S(1)}, bf16[4,128,128]{2,1,0:T(8,128)(2,1)S(1)}, u32[]{:S(2)}, u32[]{:S(2)}) collective-permute-start(bf16[4,128,128]{2,1,0:T(8,128)(2,1)S(1)} %get-tuple-element.39), channel_id=1, source_target_pairs={{0,254},{1,255},{2,4},{3,5},{4,2},{5,3},{6,8},{7,9},{8,6},{9,7},{1... | collective-permute-start | bytes 393224 | tf_op jit(solution)/shard_map/ppermute | solution.py:31
  33.6 1.6 %copy-start = (bf16[32,3,128,128]{3,2,1,0:T(8,128)(2,1)}, bf16[32,3,128,128]{3,2,1,0:T(8,128)(2,1)S(1)}, u32[]{:S(2)}) copy-start(bf16[32,3,128,128]{3,2,1,0:T(8,128)(2,1)S(1)} %get-tuple-element.32.tiles) | copy-start | bytes 9437188
  35.2 1.7 %copy-start.2 = (bf16[32,3,128,128]{3,2,1,0:T(8,128)(2,1)}, bf16[32,3,128,128]{3,2,1,0:T(8,128)(2,1)S(1)}, u32[]{:S(2)}) copy-start(bf16[32,3,128,128]{3,2,1,0:T(8,128)(2,1)S(1)} %get-tuple-element.33.refs_0_) | copy-start | bytes 9437188
  36.9 1.3 %copy-start.6 = (f32[4096,128]{1,0:T(8,128)}, f32[4096,128]{1,0:T(8,128)S(1)}, u32[]{:S(2)}) copy-start(f32[4096,128]{1,0:T(8,128)S(1)} %get-tuple-element.34.refs_2_) | copy-start | bytes 6291460
  38.2 1.4 %copy-start.8 = (bf16[4096,256]{1,0:T(8,128)(2,1)}, bf16[4096,256]{1,0:T(8,128)(2,1)S(1)}, u32[]{:S(2)}) copy-start(bf16[4096,256]{1,0:T(8,128)(2,1)S(1)} %get-tuple-element.35.refs_3_) | copy-start | bytes 6291460
  40.5 1.9 %copy-start.3 = (bf16[32,3,128,128]{3,2,1,0:T(8,128)(2,1)S(1)}, bf16[32,3,128,128]{3,2,1,0:T(8,128)(2,1)}, u32[]{:S(2)}) copy-start(bf16[32,3,128,128]{3,2,1,0:T(8,128)(2,1)} %copy-done.2) | copy-start | bytes 9437188
  42.4 1.6 %copy-start.7 = (f32[4096,128]{1,0:T(8,128)S(1)}, f32[4096,128]{1,0:T(8,128)}, u32[]{:S(2)}) copy-start(f32[4096,128]{1,0:T(8,128)} %copy-done.6) | copy-start | bytes 6291460
  44.0 1.6 %copy-start.9 = (bf16[4096,256]{1,0:T(8,128)(2,1)S(1)}, bf16[4096,256]{1,0:T(8,128)(2,1)}, u32[]{:S(2)}) copy-start(bf16[4096,256]{1,0:T(8,128)(2,1)} %copy-done.8) | copy-start | bytes 6291460
  55.3 1.3 %copy-start.4 = (bf16[4096,256]{1,0:T(8,128)(2,1)}, bf16[4096,256]{1,0:T(8,128)(2,1)S(1)}, u32[]{:S(2)}) copy-start(bf16[4096,256]{1,0:T(8,128)(2,1)S(1)} %get-tuple-element.41.d_pre) | copy-start | bytes 6291460
  58.3 34.8 %all-to-all-start.1 = ((bf16[256,8,128]{2,1,0:T(8,128)(2,1)}), bf16[256,8,128]{2,1,0:T(8,128)(2,1)S(1)}, u32[]{:S(2)}, u32[]{:S(2)}) async-start(bf16[256,8,128]{2,1,0:T(8,128)(2,1)} %get-tuple-element.45), calls=%async_computation.1 | async-start | bytes 1048576 | tf_op jit(solution)/shard_map/all_to_all | solution.py:561
  66.5 18.9 %collective-permute-start.4 = (bf16[4,128,128]{2,1,0:T(8,128)(2,1)}, bf16[4,128,128]{2,1,0:T(8,128)(2,1)S(1)}, u32[]{:S(2)}, u32[]{:S(2)}) collective-permute-start(bf16[4,128,128]{2,1,0:T(8,128)(2,1)} %copy-done.12), channel_id=1, source_target_pairs={{0,1},{1,0},{2,3},{3,2},{4,5},{5,4},{6,7},{7,6},{8,9},{9,8},{10,11... | collective-permute-start | bytes 393224 | tf_op jit(solution)/shard_map/ppermute | solution.py:31
  68.7 16.7 %collective-permute-start.5 = (bf16[4,128,128]{2,1,0:T(8,128)(2,1)S(1)}, bf16[4,128,128]{2,1,0:T(8,128)(2,1)S(1)}, u32[]{:S(2)}, u32[]{:S(2)}) collective-permute-start(bf16[4,128,128]{2,1,0:T(8,128)(2,1)S(1)} %get-tuple-element.48), channel_id=1, source_target_pairs={{0,255},{1,2},{2,1},{3,4},{4,3},{5,6},{6,5},{7,8},{8,7},{9,10},{10... | collective-permute-start | bytes 393224 | tf_op jit(solution)/shard_map/ppermute | solution.py:31
  68.7 16.7 %collective-permute-start.6 = (bf16[4,128,128]{2,1,0:T(8,128)(2,1)S(1)}, bf16[4,128,128]{2,1,0:T(8,128)(2,1)S(1)}, u32[]{:S(2)}, u32[]{:S(2)}) collective-permute-start(bf16[4,128,128]{2,1,0:T(8,128)(2,1)S(1)} %get-tuple-element.49), channel_id=1, source_target_pairs={{0,2},{1,3},{2,0},{3,1},{4,6},{5,7},{6,4},{7,5},{8,10},{9,11},{10,... | collective-permute-start | bytes 393224 | tf_op jit(solution)/shard_map/ppermute | solution.py:31
  69.9 20.1 %collective-permute-start.7 = (bf16[4,128,128]{2,1,0:T(8,128)(2,1)S(1)}, bf16[4,128,128]{2,1,0:T(8,128)(2,1)S(1)}, u32[]{:S(2)}, u32[]{:S(2)}) collective-permute-start(bf16[4,128,128]{2,1,0:T(8,128)(2,1)S(1)} %get-tuple-element.50), channel_id=1, source_target_pairs={{0,254},{1,255},{2,4},{3,5},{4,2},{5,3},{6,8},{7,9},{8,6},{9,7},{1... | collective-permute-start | bytes 393224 | tf_op jit(solution)/shard_map/ppermute | solution.py:31
  77.3 1.9 %copy-start.1 = (bf16[32,3,128,128]{3,2,1,0:T(8,128)(2,1)S(1)}, bf16[32,3,128,128]{3,2,1,0:T(8,128)(2,1)}, u32[]{:S(2)}) copy-start(bf16[32,3,128,128]{3,2,1,0:T(8,128)(2,1)} %copy-done) | copy-start | bytes 9437188
  79.1 1.6 %copy-start.5 = (bf16[4096,256]{1,0:T(8,128)(2,1)S(1)}, bf16[4096,256]{1,0:T(8,128)(2,1)}, u32[]{:S(2)}) copy-start(bf16[4096,256]{1,0:T(8,128)(2,1)} %copy-done.4) | copy-start | bytes 6291460
  80.7 1.2 %copy-start.11 = (bf16[32,128,128]{2,1,0:T(8,128)(2,1)S(1)}, bf16[32,128,128]{2,1,0:T(8,128)(2,1)}, u32[]{:S(2)}) copy-start(bf16[32,128,128]{2,1,0:T(8,128)(2,1)} %copy-done.10) | copy-start | bytes 3145732
  85.4 4.7 %copy-start.19 = (bf16[4,128,128]{2,1,0:T(8,128)(2,1)}, bf16[4,128,128]{2,1,0:T(8,128)(2,1)S(1)}, u32[]{:S(2)}) copy-start(bf16[4,128,128]{2,1,0:T(8,128)(2,1)S(1)} %collective-permute-done.4.refs_0_) | copy-start | bytes 393220
  85.4 4.6 %copy-start.20 = (bf16[4,128,128]{2,1,0:T(8,128)(2,1)}, bf16[4,128,128]{2,1,0:T(8,128)(2,1)S(1)}, u32[]{:S(2)}) copy-start(bf16[4,128,128]{2,1,0:T(8,128)(2,1)S(1)} %collective-permute-done.5.refs_1_) | copy-start | bytes 393220
  85.4 4.6 %copy-start.21 = (bf16[4,128,128]{2,1,0:T(8,128)(2,1)}, bf16[4,128,128]{2,1,0:T(8,128)(2,1)S(1)}, u32[]{:S(2)}) copy-start(bf16[4,128,128]{2,1,0:T(8,128)(2,1)S(1)} %collective-permute-done.6.refs_2_) | copy-start | bytes 393220
  (9 other events, 6.8 us)

commit v3 on v2

--- a/solution.py
+++ b/solution.py
@@ -111,13 +111,13 @@
     _, tile, width = blocks.shape
     return pl.pallas_call(
         send_kernel,
-        out_shape=[jax.ShapeDtypeStruct((per_list, tile, width), BF16)] * lists
+        out_shape=[pltpu.HBM((per_list, tile, width), BF16)] * lists
         + [
             jax.ShapeDtypeStruct((parts, hubs.shape[0], width), BF16),
             pltpu.VMEM(blocks.shape, BF16),
         ],
         in_specs=[HBM_SPEC] * 3,
-        out_specs=[ANY_SPEC] * lists + [VMEM_SPEC, VMEM_SPEC],
+        out_specs=[HBM_SPEC] * lists + [VMEM_SPEC, VMEM_SPEC],
         scratch_shapes=[
             pltpu.SMEM(send.shape, jnp.int32),
             pltpu.SMEM(hubs.shape, jnp.int32),
@@ -130,7 +130,7 @@
 
 
 def local_kernel(
-    src_hbm, tiles_hbm, remote_hbm, d_hbm, blocks, agg, tiles, remote, d_hidden, src, sem, sem_in
+    src_hbm, tiles_hbm, d_hbm, blocks, agg_hbm, d_hidden, src, tiles, agg, sem, sem_in, sem_out
 ):
     count, per_block, tile, _ = tiles.shape
     chunks = count // STEP
@@ -138,16 +138,17 @@
     def fetch(i):
         part = pl.ds(i * STEP, STEP)
         return pltpu.make_async_copy(tiles_hbm.at[part], tiles.at[part], sem_in.at[i])
+
+    def store(i):
+        part = rows_of(i, STEP * tile)
+        return pltpu.make_async_copy(agg.at[part], agg_hbm.at[part], sem_out.at[i])
 
     index = pltpu.make_async_copy(src_hbm, src, sem.at[0])
     index.start()
     for i in range(chunks):
         fetch(i).start()
-    later = [
-        pltpu.make_async_copy(remote_hbm, remote, sem.at[1]),
-        pltpu.make_async_copy(d_hbm, d_hidden, sem.at[2]),
-    ]
-    start(later)
+    later = pltpu.make_async_copy(d_hbm, d_hidden, sem.at[1])
+    later.start()
     index.wait()
 
     @pl.loop(0, chunks)
@@ -160,26 +161,27 @@
             agg[rows_of(at, tile), :] = jnp.dot(
                 jnp.concatenate(edges, 1), jnp.concatenate(taken, 0), preferred_element_type=F32
             )
-
-    wait(later)
-
-
-def local_aggregate(src, tiles, remote, d_hidden, blocks):
+        store(i).start()
+
+    later.wait()
+    wait([store(i) for i in range(chunks)])
+
+
+def local_aggregate(src, tiles, d_hidden, blocks):
     count, per_block, tile, _ = tiles.shape
     width = blocks.shape[-1]
+    agg = (count * tile, width)
     return pl.pallas_call(
         local_kernel,
-        out_shape=[
-            pltpu.VMEM((count * tile, width), F32),
-            pltpu.VMEM(tiles.shape, BF16),
-            pltpu.VMEM(remote.shape, BF16),
-            pltpu.VMEM(d_hidden.shape, BF16),
-        ],
-        in_specs=[HBM_SPEC] * 4 + [VMEM_SPEC],
-        out_specs=[VMEM_SPEC] * 4,
+        out_shape=[pltpu.HBM(agg, F32), pltpu.VMEM(d_hidden.shape, BF16)],
+        in_specs=[HBM_SPEC] * 3 + [VMEM_SPEC],
+        out_specs=[HBM_SPEC, VMEM_SPEC],
         scratch_shapes=[
             pltpu.SMEM(src.shape, jnp.int32),
-            pltpu.SemaphoreType.DMA((3,)),
+            pltpu.VMEM(tiles.shape, BF16),
+            pltpu.VMEM(agg, F32),
+            pltpu.SemaphoreType.DMA((2,)),
+            pltpu.SemaphoreType.DMA((count // STEP,)),
             pltpu.SemaphoreType.DMA((count // STEP,)),
         ],
         compiler_params=params(),
@@ -187,17 +189,17 @@
             flops=2 * tiles.size * width, bytes_accessed=8 << 20, transcendentals=0
         ),
         name="local_aggregate",
-    )(hbm(src), hbm(tiles), hbm(remote), hbm(d_hidden), vmem(blocks))
+    )(hbm(src), hbm(tiles), hbm(d_hidden), vmem(blocks))
 
 
 def layer_kernel(src_hbm, *refs):
     lists = len(OFFSETS)
-    tiles, rows, agg_local, d_hidden = refs[:4]
+    tiles_hbm, rows_hbm, agg_hbm, d_hidden = refs[:4]
     halos, refs = refs[4 : 4 + lists], refs[4 + lists :]
-    hub, self_hbm, neigh_hbm, bias_hbm, hidden, d_pre_out, d_agg_out = refs[:7]
+    hub, self_hbm, neigh_hbm, bias_hbm, hidden_hbm, d_pre_out, d_agg_out = refs[:7]
     backs, refs = refs[7 : 7 + lists], refs[7 + lists :]
     packed, src, weights, bias, table, rem_grad, backs_out, w_grad, b_grad, spread = refs[:10]
-    pack_out, sem_t, sem_back = refs[10:]
+    pack_out, tiles, rows, agg_local, hidden, sem_t, sem_back, sem_in, sem_out = refs[10:]
     count, per_block, tile, _ = tiles.shape
     width = rows.shape[-1]
     per_list = halos[0].shape[0]
@@ -214,14 +216,32 @@
     for w, s in enumerate(slots):
         pairs.append((halos[w], table.at[pl.ds(s * per_list, per_list)]))
     moves = [pltpu.make_async_copy(*p, sem_t.at[n]) for n, p in enumerate(pairs)]
+    chunks = count // STEP
+
+    def fetch(i):
+        few, many = pl.ds(i * STEP, STEP), rows_of(i, STEP * tile)
+        pairs = (
+            (tiles_hbm.at[few], tiles.at[few]),
+            (agg_hbm.at[many], agg_local.at[many]),
+            (rows_hbm.at[many], rows.at[many]),
+        )
+        return [pltpu.make_async_copy(*p, sem_in.at[i, n]) for n, p in enumerate(pairs)]
+
+    def store(i):
+        many = rows_of(i, STEP * tile)
+        return pltpu.make_async_copy(hidden.at[many], hidden_hbm.at[many], sem_out.at[i])
+
     start(moves)
+    for i in range(chunks):
+        start(fetch(i))
     rem_grad[...] = jnp.zeros_like(rem_grad)
     w_grad[...] = jnp.zeros_like(w_grad)
     b_grad[...] = jnp.zeros_like(b_grad)
     wait(moves)
 
-    @pl.loop(0, count // STEP)
+    @pl.loop(0, chunks)
     def _(i):
+        wait(fetch(i))
         many = rows_of(i, STEP * tile)
 
         def edges(b):
@@ -241,6 +261,7 @@
         pre = jnp.dot(both, weights[...], preferred_element_type=F32) + bias[...]
         sig = jax.nn.sigmoid(pre)
         hidden[many, :] = (pre * sig).astype(BF16)
+        store(i).start()
         d_pre = d_hidden[many, :].astype(F32) * (sig * (1.0 + pre * (1.0 - sig)))
         b_grad[...] += jnp.sum(d_pre.reshape(-1, 8, d_pre.shape[-1]), 0)
         d_pre_b = d_pre.astype(BF16)
@@ -281,6 +302,7 @@
     last = pltpu.make_async_copy(pack_out, packed, sem_back.at[lists])
     last.start()
     wait(sent)
+    wait([store(i) for i in range(chunks)])
     last.wait()
 
 
@@ -291,17 +313,18 @@
     lists, per_list = len(halos), halos[0].shape[0]
     table = lists * per_list + hub.shape[0]
     packed = (parts, CHUNK, width)
+    chunks = count // STEP
     return pl.pallas_call(
         layer_kernel,
         out_shape=[
-            pltpu.VMEM((nodes, units), BF16),
+            pltpu.HBM((nodes, units), BF16),
             pltpu.VMEM((nodes, units), BF16),
             pltpu.VMEM((count, width, tile), BF16),
         ]
-        + [jax.ShapeDtypeStruct((per_list, width, tile), BF16)] * lists
-        + [jax.ShapeDtypeStruct(packed, BF16)],
-        in_specs=[HBM_SPEC] + [VMEM_SPEC] * 4 + [HBM_SPEC] * (lists + 4),
-        out_specs=[VMEM_SPEC] * 3 + [ANY_SPEC] * (lists + 1),
+        + [pltpu.HBM((per_list, width, tile), BF16)] * lists
+        + [pltpu.HBM(packed, BF16)],
+        in_specs=[HBM_SPEC] * 4 + [VMEM_SPEC] + [ANY_SPEC] * (lists + 1) + [HBM_SPEC] * 3,
+        out_specs=[HBM_SPEC] + [VMEM_SPEC] * 2 + [HBM_SPEC] * (lists + 1),
         scratch_shapes=[
             pltpu.SMEM(src.shape, jnp.int32),
             pltpu.VMEM((2 * width, units), BF16),
@@ -313,8 +336,14 @@
             pltpu.VMEM((8, units), F32),
             pltpu.VMEM((parts * CHUNK, width), F32),
             pltpu.VMEM(packed, BF16),
+            pltpu.VMEM(tiles.shape, BF16),
+            pltpu.VMEM((nodes, width), BF16),
+            pltpu.VMEM((nodes, width), F32),
+            pltpu.VMEM((nodes, units), BF16),
             pltpu.SemaphoreType.DMA((lists + 5,)),
             pltpu.SemaphoreType.DMA((lists + 1,)),
+            pltpu.SemaphoreType.DMA((chunks, 3)),
+            pltpu.SemaphoreType.DMA((chunks,)),
         ],
         compiler_params=params(),
         cost_estimate=pl.CostEstimate(
@@ -325,29 +354,40 @@
         name="layer",
     )(
         hbm(src),
-        vmem(tiles),
-        vmem(rows),
-        vmem(agg_local),
+        hbm(tiles),
+        hbm(rows),
+        hbm(agg_local),
         vmem(d_hidden),
-        *[hbm(x) for x in (*halos, hub, w_self, w_neigh, bias)],
+        *halos,
+        hub,
+        hbm(w_self),
+        hbm(w_neigh),
+        hbm(bias),
     )
 
 
-def back_kernel(src_hbm, weight_hbm, tiles, d_pre, d_agg, hidden, out, total, src, weight, sems):
+def back_kernel(
+    src_hbm, weight_hbm, tiles_hbm, d_pre, d_agg, total, src, weight, tiles, sems, sem_in
+):
     count, per_block, tile, _ = tiles.shape
     size = STEP * tile
-    result = pltpu.make_async_copy(hidden, out, sems.at[0])
-    result.start()
+
+    def fetch(i):
+        part = pl.ds(i * STEP, STEP)
+        return pltpu.make_async_copy(tiles_hbm.at[part], tiles.at[part], sem_in.at[i])
+
     loads = [
-        pltpu.make_async_copy(src_hbm, src, sems.at[1]),
-        pltpu.make_async_copy(weight_hbm, weight, sems.at[2]),
+        pltpu.make_async_copy(src_hbm, src, sems.at[0]),
+        pltpu.make_async_copy(weight_hbm, weight, sems.at[1]),
     ]
     start(loads)
+    start([fetch(i) for i in range(count // STEP)])
     total[...] = jnp.zeros_like(total)
     wait(loads)
 
     @pl.loop(0, count // STEP)
     def _(i):
+        fetch(i).wait()
         own = lax.dot_general(
             weight[...], d_pre[rows_of(i, size), :], NT, preferred_element_type=F32
         )
@@ -360,24 +400,21 @@
                 s = src[k, at]
                 total[s] += terms[:, k * tile : (k + 1) * tile]
 
-    result.wait()
-
-
-def local_backward(src, tiles, d_pre, d_agg, weight, hidden):
+
+def local_backward(src, tiles, d_pre, d_agg, weight):
     count, per_block, tile, _ = tiles.shape
     width, units = weight.shape
     return pl.pallas_call(
         back_kernel,
-        out_shape=[
-            jax.ShapeDtypeStruct(hidden.shape, BF16),
-            pltpu.VMEM((count, width, tile), F32),
-        ],
-        in_specs=[HBM_SPEC] * 2 + [VMEM_SPEC] * 4,
-        out_specs=[ANY_SPEC, VMEM_SPEC],
+        out_shape=pltpu.VMEM((count, width, tile), F32),
+        in_specs=[HBM_SPEC] * 3 + [VMEM_SPEC] * 2,
+        out_specs=VMEM_SPEC,
         scratch_shapes=[
             pltpu.SMEM(src.shape, jnp.int32),
             pltpu.VMEM(weight.shape, BF16),
-            pltpu.SemaphoreType.DMA((3,)),
+            pltpu.VMEM(tiles.shape, BF16),
+            pltpu.SemaphoreType.DMA((2,)),
+            pltpu.SemaphoreType.DMA((count // STEP,)),
         ],
         compiler_params=params(),
         cost_estimate=pl.CostEstimate(
@@ -386,7 +423,7 @@
             transcendentals=0,
         ),
         name="local_backward",
-    )(hbm(src), hbm(weight), vmem(tiles), vmem(d_pre), vmem(d_agg), vmem(hidden))
+    )(hbm(src), hbm(weight), hbm(tiles), vmem(d_pre), vmem(d_agg))
 
 
 def collect_kernel(send_hbm, hubs_hbm, _, *refs):
@@ -430,11 +467,11 @@
         collect_kernel,
         out_shape=[
             pltpu.VMEM(grad.shape, F32),
-            jax.ShapeDtypeStruct((count * tile, width), BF16),
+            pltpu.HBM((count * tile, width), BF16),
             pltpu.VMEM(near, F32),
         ],
-        in_specs=[HBM_SPEC] * 2 + [VMEM_SPEC] + [HBM_SPEC] * lists,
-        out_specs=[VMEM_SPEC, ANY_SPEC, VMEM_SPEC],
+        in_specs=[HBM_SPEC] * 2 + [VMEM_SPEC] + [ANY_SPEC] * lists,
+        out_specs=[VMEM_SPEC, HBM_SPEC, VMEM_SPEC],
         scratch_shapes=[
             pltpu.SMEM(send.shape, jnp.int32),
             pltpu.SMEM(hubs.shape, jnp.int32),
@@ -449,7 +486,7 @@
             flops=grad.size * 8, bytes_accessed=4 << 20, transcendentals=0
         ),
         name="collect",
-    )(hbm(send), hbm(hubs), vmem(grad), *[hbm(x) for x in halos])[1:]
+    )(hbm(send), hbm(hubs), vmem(grad), *halos)[1:]
 
 
 def finish_kernel(
@@ -504,9 +541,9 @@
     line = jax.ShapeDtypeStruct((1, width), F32)
     return pl.pallas_call(
         finish_kernel,
-        out_shape=[jax.ShapeDtypeStruct(grad.shape, grad.dtype), line, line, line],
-        in_specs=[HBM_SPEC, HBM_SPEC, VMEM_SPEC, ANY_SPEC],
-        out_specs=[ANY_SPEC, VMEM_SPEC, VMEM_SPEC, VMEM_SPEC],
+        out_shape=[pltpu.HBM(grad.shape, grad.dtype), line, line, line],
+        in_specs=[HBM_SPEC, ANY_SPEC, VMEM_SPEC, HBM_SPEC],
+        out_specs=[HBM_SPEC, VMEM_SPEC, VMEM_SPEC, VMEM_SPEC],
         scratch_shapes=[
             pltpu.SMEM(hubs.shape, jnp.int32),
             pltpu.VMEM(pieces.shape, BF16),
@@ -517,7 +554,7 @@
         input_output_aliases={3: 0},
         compiler_params=params(),
         name="finish",
-    )(hbm(hubs), hbm(pieces), vmem(near), grad)
+    )(hbm(hubs), pieces, vmem(near), hbm(grad))
 
 
 def shards(
@@ -541,13 +578,11 @@
     *sends, hub_mine, own = gather_sends(send_blocks, hub_rows, blocks, parts)
     hub_all = lax.all_to_all(hub_mine, "dom", 0, 0)
     halos = [swapped(b, way) for way, b in enumerate(sends)]
-    agg_local, tiles_l, tiles_r, d_hid = local_aggregate(
-        local_src.T, local_tiles, remote_tiles, d_hidden, own
-    )
+    agg_local, d_hid = local_aggregate(local_src.T, local_tiles, d_hidden, own)
     hidden, d_pre, d_agg, *rest = layer(
         remote_src.T,
-        tiles_r,
-        own.reshape(nodes, width),
+        remote_tiles,
+        features,
         agg_local,
         halos,
         hub_all.reshape(parts * owned // tile, tile, width),
@@ -560,10 +595,10 @@
     *backs, packed = rest
     pieces = lax.all_to_all(packed, "dom", 0, 0)
     returned = [swapped(b, way) for way, b in enumerate(backs)]
-    out, grad_t = local_backward(local_src.T, tiles_l, d_pre, d_agg, w_self, hidden)
+    grad_t = local_backward(local_src.T, local_tiles, d_pre, d_agg, w_self)
     rough, near = collect(send_blocks, hub_rows, grad_t, returned)
     grad, g_self, g_neigh, g_bias = finish(hub_rows, pieces, near, rough)
-    return (out, grad, g_self.reshape(width, 1), g_neigh.reshape(width, 1), g_bias[0, :1])
+    return (hidden, grad, g_self.reshape(width, 1), g_neigh.reshape(width, 1), g_bias[0, :1])
 
 
 def solution(mesh):

time: 96.9 us -> 85.6 us (0.88)
  local copies, waits for them, and re-layouts: 21 us -> 5.09 us
  waiting for transfers between devices: 4.63 us -> 8.55 us
    unnamed x46 -> x8, local copies, waits for them, and re-layouts: 21 us -> 5.09 us
    ppermute x8, waiting for transfers between devices: 4.62 us -> 8.55 us  [swapped(): lax.ppermute(block, 'dom', [(i, partner(i, way, n)) for i in range(n)])]
  transfers between devices with their start and end apart: 10 -> 10, of which waited for: 1 -> 2; matrix products, arithmetic and copies ran while one was open for 0% -> 0% of each run, Pallas kernels for 10% -> 11%
where the time goes in v3:
time: 85.6 us; the launch traced here: 85.2 us
  starting transfers between devices  45.9 us (54%)
  Pallas kernels  24.9 us (29%)
  waiting for transfers between devices  8.55 us (10%)
  local copies, waits for them, and re-layouts  5.09 us (6%)
    ppermute x8, starting transfers between devices, swapped(): lax.ppermute(block, 'dom', [(i, partner(i, way, n)) for i in range(n)])  21.7 us
    all_to_all x1, starting transfers between devices, shards(): hub_all = lax.all_to_all(hub_mine, 'dom', 0, 0)  15.7 us
    pallas_call x1, Pallas kernels, layer(): pl.pallas_call(layer_kernel, out_shape=[pltpu.HBM((nodes, units), BF16),...  10.2 us
    all_to_all x1, starting transfers between devices, shards(): pieces = lax.all_to_all(packed, 'dom', 0, 0)  8.55 us
    ppermute x8, waiting for transfers between devices, swapped(): lax.ppermute(block, 'dom', [(i, partner(i, way, n)) for i in range(n)])  8.55 us
    unnamed x8, local copies, waits for them, and re-layouts  5.09 us
    pallas_call x1, Pallas kernels, local_backward(): pl.pallas_call(back_kernel, out_shape=pltpu.VMEM((count, width, tile), F3...  4.1 us
    pallas_call x1, Pallas kernels, local_aggregate(): pl.pallas_call(local_kernel, out_shape=[pltpu.HBM(agg, F32), pltpu.VMEM(d...  3.52 us
  transfers between devices with their start and end apart: 10, of which 2 were waited for; matrix products, arithmetic and copies ran while one was open for 0% of the time, Pallas kernels for 11%

profile of v3, /device:TPU:1, one launch (start us, length us, event | category | flops | bytes accessed | tf_op | source)
XLA Modules:
  0.0 85.2 jit_solution(5937230061749525219)
XLA Ops:
  0.6 2.9 %sends.1 = (bf16[4,128,128]{2,1,0:T(8,128)(2,1)}, bf16[4,128,128]{2,1,0:T(8,128)(2,1)}, bf16[4,128,128]{2,1,0:T(8,128)(2,1)}, bf16[4,128,128]{2,1,0:T(8,128)(2,1...) custom-call(s32[4,4]{1,0:T(4,128)} %send_hbm.3, s32[4]{0:T(128)} %hubs_hbm.5, ...), custom_call_target="tpu_custom_call" | custom-call | tf_op jit(solution)/shard_map/sends/pallas_call | solution.py:112
  3.6 15.7 %all-to-all-start = ((bf16[256,4,128]{2,1,0:T(4,128)(2,1)}), bf16[256,4,128]{2,1,0:T(4,128)(2,1)S(1)}, u32[]{:S(2)}, u32[]{:S(2)}) async-start(bf16[256,4,128]{2,1,0:T(4,128)(2,1)} %get-tuple-element.34), calls=%async_computation | async-start | bytes 524288 | tf_op jit(solution)/shard_map/all_to_all | solution.py:579
  19.2 2.2 %collective-permute-start = (bf16[4,128,128]{2,1,0:T(8,128)(2,1)}, bf16[4,128,128]{2,1,0:T(8,128)(2,1)S(1)}, u32[]{:S(2)}, u32[]{:S(2)}) collective-permute-start(bf16[4,128,128]{2,1,0:T(8,128)(2,1)} %get-tuple-element.30), channel_id=1, source_target_pairs={{0,1},{1,0},{2,3},{3,2},{4,5},{5,4},{6,7},{7,6},{8,9},{9,8},{10,11... | collective-permute-start | bytes 393224 | tf_op jit(solution)/shard_map/ppermute | solution.py:31
  21.5 1.2 %collective-permute-start.2 = (bf16[4,128,128]{2,1,0:T(8,128)(2,1)}, bf16[4,128,128]{2,1,0:T(8,128)(2,1)S(1)}, u32[]{:S(2)}, u32[]{:S(2)}) collective-permute-start(bf16[4,128,128]{2,1,0:T(8,128)(2,1)} %get-tuple-element.32), channel_id=1, source_target_pairs={{0,2},{1,3},{2,0},{3,1},{4,6},{5,7},{6,4},{7,5},{8,10},{9,11},{10,... | collective-permute-start | bytes 393224 | tf_op jit(solution)/shard_map/ppermute | solution.py:31
  22.7 7.3 %collective-permute-start.3 = (bf16[4,128,128]{2,1,0:T(8,128)(2,1)}, bf16[4,128,128]{2,1,0:T(8,128)(2,1)S(1)}, u32[]{:S(2)}, u32[]{:S(2)}) collective-permute-start(bf16[4,128,128]{2,1,0:T(8,128)(2,1)} %get-tuple-element.33), channel_id=1, source_target_pairs={{0,254},{1,255},{2,4},{3,5},{4,2},{5,3},{6,8},{7,9},{8,6},{9,7},{1... | collective-permute-start | bytes 393224 | tf_op jit(solution)/shard_map/ppermute | solution.py:31
  30.0 3.5 %local_aggregate.1 = (f32[4096,128]{1,0:T(8,128)}, bf16[4096,256]{1,0:T(8,128)(2,1)S(1)}) custom-call(s32[3,32]{1,0:T(4,128)} %bitcast.11, bf16[32,3,128,128]{3,2,1,0:T(8,128)(2,1)} %tiles_hbm.3, bf16[4096,256]{1,0:T(8,128)(2,1)} %d_hbm.1, bf16[32,128,128]{2,1,0:T(8,128)(2,1)S(1)} %get-tuple-element.27.blocks), custom_call_target="tpu_custom_call" | custom-call | flops 402653184 | bytes 8388608 | tf_op jit(solution)/shard_map/local_aggregate/pallas_call | solution.py:174
  33.5 0.0 copy-start
  33.5 1.3 %copy-done = bf16[4096,256]{1,0:T(8,128)(2,1)} copy-done((bf16[4096,256]{1,0:T(8,128)(2,1)}, bf16[4096,256]{1,0:T(8,128)(2,1)S(1)}, u32[]{:S(2)}) %copy-start) | copy-done | bytes 2097176
  34.9 0.0 collective-permute-done.refs_4_
  34.9 0.0 collective-permute-done.1.refs_5_
  34.9 1.1 %collective-permute-done.3.refs_7_ = bf16[4,128,128]{2,1,0:T(8,128)(2,1)S(1)} collective-permute-done((bf16[4,128,128]{2,1,0:T(8,128)(2,1)}, bf16[4,128,128]{2,1,0:T(8,128)(2,1)S(1)}, u32[]{:S(2)}, u32[]{:S(2)}) %collective-permute-start.3) | collective-permute-done | bytes 131104 | tf_op jit(solution)/shard_map/ppermute | solution.py:31
  36.0 1.6 %copy-done.1 = bf16[4096,256]{1,0:T(8,128)(2,1)S(1)} copy-done((bf16[4096,256]{1,0:T(8,128)(2,1)S(1)}, bf16[4096,256]{1,0:T(8,128)(2,1)}, u32[]{:S(2)}) %copy-start.1) | copy-done | bytes 2097176
  37.6 10.2 %layer.1 = (bf16[4096,256]{1,0:T(8,128)(2,1)}, bf16[4096,256]{1,0:T(8,128)(2,1)S(1)}, bf16[32,128,128]{2,1,0:T(8,128)(2,1)S(1)}, bf16[4,128,128]{2,1,0:T(8,128)(...) custom-call(s32[3,32]{1,0:T(4,128)} %bitcast.13, ...), custom_call_target="tpu_custom_call" | custom-call | flops 2415919104 | bytes 14680064 | tf_op jit(solution)/shard_map/layer/pallas_call | solution.py:317
  47.7 0.0 copy-start.2
  47.7 1.0 %copy-done.2 = bf16[32,128,128]{2,1,0:T(8,128)(2,1)} copy-done((bf16[32,128,128]{2,1,0:T(8,128)(2,1)}, bf16[32,128,128]{2,1,0:T(8,128)(2,1)S(1)}, u32[]{:S(2)}) %copy-start.2) | copy-done | bytes 1048600
  48.7 8.6 %all-to-all-start.1 = ((bf16[256,8,128]{2,1,0:T(8,128)(2,1)}), bf16[256,8,128]{2,1,0:T(8,128)(2,1)S(1)}, u32[]{:S(2)}, u32[]{:S(2)}) async-start(bf16[256,8,128]{2,1,0:T(8,128)(2,1)} %get-tuple-element.36), calls=%async_computation.1 | async-start | bytes 1048576 | tf_op jit(solution)/shard_map/all_to_all | solution.py:596
  57.3 2.4 %collective-permute-start.4 = (bf16[4,128,128]{2,1,0:T(8,128)(2,1)}, bf16[4,128,128]{2,1,0:T(8,128)(2,1)S(1)}, u32[]{:S(2)}, u32[]{:S(2)}) collective-permute-start(bf16[4,128,128]{2,1,0:T(8,128)(2,1)} %get-tuple-element.39), channel_id=1, source_target_pairs={{0,1},{1,0},{2,3},{3,2},{4,5},{5,4},{6,7},{7,6},{8,9},{9,8},{10,11... | collective-permute-start | bytes 393224 | tf_op jit(solution)/shard_map/ppermute | solution.py:31
  59.6 1.2 %collective-permute-start.6 = (bf16[4,128,128]{2,1,0:T(8,128)(2,1)}, bf16[4,128,128]{2,1,0:T(8,128)(2,1)S(1)}, u32[]{:S(2)}, u32[]{:S(2)}) collective-permute-start(bf16[4,128,128]{2,1,0:T(8,128)(2,1)} %get-tuple-element.41), channel_id=1, source_target_pairs={{0,2},{1,3},{2,0},{3,1},{4,6},{5,7},{6,4},{7,5},{8,10},{9,11},{10,... | collective-permute-start | bytes 393224 | tf_op jit(solution)/shard_map/ppermute | solution.py:31
  60.9 7.3 %collective-permute-start.7 = (bf16[4,128,128]{2,1,0:T(8,128)(2,1)}, bf16[4,128,128]{2,1,0:T(8,128)(2,1)S(1)}, u32[]{:S(2)}, u32[]{:S(2)}) collective-permute-start(bf16[4,128,128]{2,1,0:T(8,128)(2,1)} %get-tuple-element.42), channel_id=1, source_target_pairs={{0,254},{1,255},{2,4},{3,5},{4,2},{5,3},{6,8},{7,9},{8,6},{9,7},{1... | collective-permute-start | bytes 393224 | tf_op jit(solution)/shard_map/ppermute | solution.py:31
  68.2 1.2 %copy-done.3 = bf16[32,128,128]{2,1,0:T(8,128)(2,1)S(1)} copy-done((bf16[32,128,128]{2,1,0:T(8,128)(2,1)S(1)}, bf16[32,128,128]{2,1,0:T(8,128)(2,1)}, u32[]{:S(2)}) %copy-start.3) | copy-done | bytes 1048600
  69.4 4.1 %local_backward.1._ = f32[32,128,128]{2,1,0:T(8,128)S(1)} custom-call(s32[3,32]{1,0:T(4,128)} %bitcast.12, bf16[128,256]{1,0:T(8,128)(2,1)} %weight_hbm.1, bf16[32,3,128,128]{3,2,1,0:T(8,128)(2,1)} %tiles_hbm.3, bf16[4096,256]{1,0:T(8,128)(2,1)S(1)} %get-tuple-element.37.d_pre, bf16[32,128,128]{2,1,0:T(8,128)(2,1)S(1)} %copy-done.3), custom_call_target="tpu_custom_call" | custom-call | flops 671088640 | bytes 8388608 | tf_op jit(solution)/shard_map/local_backward/pallas_call | solution.py:407
  73.5 7.4 %collective-permute-done.7.refs_3_ = bf16[4,128,128]{2,1,0:T(8,128)(2,1)S(1)} collective-permute-done((bf16[4,128,128]{2,1,0:T(8,128)(2,1)}, bf16[4,128,128]{2,1,0:T(8,128)(2,1)S(1)}, u32[]{:S(2)}, u32[]{:S(2)}) %collective-permute-start.7) | collective-permute-done | bytes 131104 | tf_op jit(solution)/shard_map/ppermute | solution.py:31
  81.0 2.0 %collect.1 = (f32[32,128,128]{2,1,0:T(8,128)S(1)}, bf16[4096,128]{1,0:T(8,128)(2,1)}, f32[4,16,128]{2,1,0:T(8,128)S(1)}) custom-call(s32[4,4]{1,0:T(4,128)} %send_hbm.3, s32[4]{0:T(128)} %hubs_hbm.5, f32[32,128,128]{2,1,0:T(8,128)S(1)} %local_backward.1._, bf16[4,128,128]{2,1,0:T(8,128)(2,1)S(1)} %collective-permute-done.4.refs_0_, ...), custom_call_target="tpu_custom_call", output_to_operand_aliasing={{0}: (2, {})} | custom-call | flops 4194304 | bytes 4194304 | tf_op jit(solution)/shard_map/collect/pallas_call | solution.py:466
  83.0 2.2 %finish.1 = (bf16[4096,128]{1,0:T(8,128)(2,1)}, f32[1,128]{1,0:T(1,128)}, f32[1,128]{1,0:T(1,128)}, f32[1,128]{1,0:T(1,128)}) custom-call(s32[4]{0:T(128)} %hubs_hbm.5, bf16[256,8,128]{2,1,0:T(8,128)(2,1)S(1)} %all-to-all-done.1.pieces_hbm, f32[4,16,128]{2,1,0:T(8,128)S(1)} %get-tuple-element.43.near, ...), custom_call_target="tpu_custom_call", output_to_operand_aliasing={{0}: (3, {})} | custom-call | tf_op jit(solution)/shard_map/finish/pallas_call | solution.py:542
  (10 shorter events, 0.0 us)
Async XLA Ops:
  3.6 32.4 %all-to-all-start = ((bf16[256,4,128]{2,1,0:T(4,128)(2,1)}), bf16[256,4,128]{2,1,0:T(4,128)(2,1)S(1)}, u32[]{:S(2)}, u32[]{:S(2)}) async-start(bf16[256,4,128]{2,1,0:T(4,128)(2,1)} %get-tuple-element.34), calls=%async_computation | async-start | bytes 524288 | tf_op jit(solution)/shard_map/all_to_all | solution.py:579
  19.2 15.6 %collective-permute-start = (bf16[4,128,128]{2,1,0:T(8,128)(2,1)}, bf16[4,128,128]{2,1,0:T(8,128)(2,1)S(1)}, u32[]{:S(2)}, u32[]{:S(2)}) collective-permute-start(bf16[4,128,128]{2,1,0:T(8,128)(2,1)} %get-tuple-element.30), channel_id=1, source_target_pairs={{0,1},{1,0},{2,3},{3,2},{4,5},{5,4},{6,7},{7,6},{8,9},{9,8},{10,11... | collective-permute-start | bytes 393224 | tf_op jit(solution)/shard_map/ppermute | solution.py:31
  21.5 13.4 %collective-permute-start.1 = (bf16[4,128,128]{2,1,0:T(8,128)(2,1)}, bf16[4,128,128]{2,1,0:T(8,128)(2,1)S(1)}, u32[]{:S(2)}, u32[]{:S(2)}) collective-permute-start(bf16[4,128,128]{2,1,0:T(8,128)(2,1)} %get-tuple-element.31), channel_id=1, source_target_pairs={{0,255},{1,2},{2,1},{3,4},{4,3},{5,6},{6,5},{7,8},{8,7},{9,10},{10... | collective-permute-start | bytes 393224 | tf_op jit(solution)/shard_map/ppermute | solution.py:31
  21.5 13.4 %collective-permute-start.2 = (bf16[4,128,128]{2,1,0:T(8,128)(2,1)}, bf16[4,128,128]{2,1,0:T(8,128)(2,1)S(1)}, u32[]{:S(2)}, u32[]{:S(2)}) collective-permute-start(bf16[4,128,128]{2,1,0:T(8,128)(2,1)} %get-tuple-element.32), channel_id=1, source_target_pairs={{0,2},{1,3},{2,0},{3,1},{4,6},{5,7},{6,4},{7,5},{8,10},{9,11},{10,... | collective-permute-start | bytes 393224 | tf_op jit(solution)/shard_map/ppermute | solution.py:31
  22.7 13.3 %collective-permute-start.3 = (bf16[4,128,128]{2,1,0:T(8,128)(2,1)}, bf16[4,128,128]{2,1,0:T(8,128)(2,1)S(1)}, u32[]{:S(2)}, u32[]{:S(2)}) collective-permute-start(bf16[4,128,128]{2,1,0:T(8,128)(2,1)} %get-tuple-element.33), channel_id=1, source_target_pairs={{0,254},{1,255},{2,4},{3,5},{4,2},{5,3},{6,8},{7,9},{8,6},{9,7},{1... | collective-permute-start | bytes 393224 | tf_op jit(solution)/shard_map/ppermute | solution.py:31
  33.5 1.3 %copy-start = (bf16[4096,256]{1,0:T(8,128)(2,1)}, bf16[4096,256]{1,0:T(8,128)(2,1)S(1)}, u32[]{:S(2)}) copy-start(bf16[4096,256]{1,0:T(8,128)(2,1)S(1)} %get-tuple-element.29.refs_3_) | copy-start | bytes 6291460
  36.0 1.6 %copy-start.1 = (bf16[4096,256]{1,0:T(8,128)(2,1)S(1)}, bf16[4096,256]{1,0:T(8,128)(2,1)}, u32[]{:S(2)}) copy-start(bf16[4096,256]{1,0:T(8,128)(2,1)} %copy-done) | copy-start | bytes 6291460
  47.7 1.0 %copy-start.2 = (bf16[32,128,128]{2,1,0:T(8,128)(2,1)}, bf16[32,128,128]{2,1,0:T(8,128)(2,1)S(1)}, u32[]{:S(2)}) copy-start(bf16[32,128,128]{2,1,0:T(8,128)(2,1)S(1)} %get-tuple-element.38.d_agg) | copy-start | bytes 3145732
  48.7 34.3 %all-to-all-start.1 = ((bf16[256,8,128]{2,1,0:T(8,128)(2,1)}), bf16[256,8,128]{2,1,0:T(8,128)(2,1)S(1)}, u32[]{:S(2)}, u32[]{:S(2)}) async-start(bf16[256,8,128]{2,1,0:T(8,128)(2,1)} %get-tuple-element.36), calls=%async_computation.1 | async-start | bytes 1048576 | tf_op jit(solution)/shard_map/all_to_all | solution.py:596
  57.3 16.2 %collective-permute-start.4 = (bf16[4,128,128]{2,1,0:T(8,128)(2,1)}, bf16[4,128,128]{2,1,0:T(8,128)(2,1)S(1)}, u32[]{:S(2)}, u32[]{:S(2)}) collective-permute-start(bf16[4,128,128]{2,1,0:T(8,128)(2,1)} %get-tuple-element.39), channel_id=1, source_target_pairs={{0,1},{1,0},{2,3},{3,2},{4,5},{5,4},{6,7},{7,6},{8,9},{9,8},{10,11... | collective-permute-start | bytes 393224 | tf_op jit(solution)/shard_map/ppermute | solution.py:31
  59.6 13.9 %collective-permute-start.5 = (bf16[4,128,128]{2,1,0:T(8,128)(2,1)}, bf16[4,128,128]{2,1,0:T(8,128)(2,1)S(1)}, u32[]{:S(2)}, u32[]{:S(2)}) collective-permute-start(bf16[4,128,128]{2,1,0:T(8,128)(2,1)} %get-tuple-element.40), channel_id=1, source_target_pairs={{0,255},{1,2},{2,1},{3,4},{4,3},{5,6},{6,5},{7,8},{8,7},{9,10},{10... | collective-permute-start | bytes 393224 | tf_op jit(solution)/shard_map/ppermute | solution.py:31
  59.6 13.9 %collective-permute-start.6 = (bf16[4,128,128]{2,1,0:T(8,128)(2,1)}, bf16[4,128,128]{2,1,0:T(8,128)(2,1)S(1)}, u32[]{:S(2)}, u32[]{:S(2)}) collective-permute-start(bf16[4,128,128]{2,1,0:T(8,128)(2,1)} %get-tuple-element.41), channel_id=1, source_target_pairs={{0,2},{1,3},{2,0},{3,1},{4,6},{5,7},{6,4},{7,5},{8,10},{9,11},{10,... | collective-permute-start | bytes 393224 | tf_op jit(solution)/shard_map/ppermute | solution.py:31
  60.9 20.1 %collective-permute-start.7 = (bf16[4,128,128]{2,1,0:T(8,128)(2,1)}, bf16[4,128,128]{2,1,0:T(8,128)(2,1)S(1)}, u32[]{:S(2)}, u32[]{:S(2)}) collective-permute-start(bf16[4,128,128]{2,1,0:T(8,128)(2,1)} %get-tuple-element.42), channel_id=1, source_target_pairs={{0,254},{1,255},{2,4},{3,5},{4,2},{5,3},{6,8},{7,9},{8,6},{9,7},{1... | collective-permute-start | bytes 393224 | tf_op jit(solution)/shard_map/ppermute | solution.py:31
  68.2 1.2 %copy-start.3 = (bf16[32,128,128]{2,1,0:T(8,128)(2,1)S(1)}, bf16[32,128,128]{2,1,0:T(8,128)(2,1)}, u32[]{:S(2)}) copy-start(bf16[32,128,128]{2,1,0:T(8,128)(2,1)} %copy-done.2) | copy-start | bytes 3145732

commit v4 on v3

--- a/solution.py
+++ b/solution.py
@@ -130,7 +130,7 @@
 
 
 def local_kernel(
-    src_hbm, tiles_hbm, d_hbm, blocks, agg_hbm, d_hidden, src, tiles, agg, sem, sem_in, sem_out
+    src_hbm, tiles_hbm, blocks, agg_hbm, src, tiles, agg, sem, sem_in, sem_out
 ):
     count, per_block, tile, _ = tiles.shape
     chunks = count // STEP
@@ -143,12 +143,10 @@
         part = rows_of(i, STEP * tile)
         return pltpu.make_async_copy(agg.at[part], agg_hbm.at[part], sem_out.at[i])
 
-    index = pltpu.make_async_copy(src_hbm, src, sem.at[0])
+    index = pltpu.make_async_copy(src_hbm, src, sem)
     index.start()
     for i in range(chunks):
         fetch(i).start()
-    later = pltpu.make_async_copy(d_hbm, d_hidden, sem.at[1])
-    later.start()
     index.wait()
 
     @pl.loop(0, chunks)
@@ -163,24 +161,23 @@
             )
         store(i).start()
 
-    later.wait()
     wait([store(i) for i in range(chunks)])
 
 
-def local_aggregate(src, tiles, d_hidden, blocks):
+def local_aggregate(src, tiles, blocks):
     count, per_block, tile, _ = tiles.shape
     width = blocks.shape[-1]
     agg = (count * tile, width)
     return pl.pallas_call(
         local_kernel,
-        out_shape=[pltpu.HBM(agg, F32), pltpu.VMEM(d_hidden.shape, BF16)],
-        in_specs=[HBM_SPEC] * 3 + [VMEM_SPEC],
-        out_specs=[HBM_SPEC, VMEM_SPEC],
+        out_shape=pltpu.HBM(agg, F32),
+        in_specs=[HBM_SPEC] * 2 + [VMEM_SPEC],
+        out_specs=HBM_SPEC,
         scratch_shapes=[
             pltpu.SMEM(src.shape, jnp.int32),
             pltpu.VMEM(tiles.shape, BF16),
             pltpu.VMEM(agg, F32),
-            pltpu.SemaphoreType.DMA((2,)),
+            pltpu.SemaphoreType.DMA,
             pltpu.SemaphoreType.DMA((count // STEP,)),
             pltpu.SemaphoreType.DMA((count // STEP,)),
         ],
@@ -189,17 +186,18 @@
             flops=2 * tiles.size * width, bytes_accessed=8 << 20, transcendentals=0
         ),
         name="local_aggregate",
-    )(hbm(src), hbm(tiles), hbm(d_hidden), vmem(blocks))
+    )(hbm(src), hbm(tiles), vmem(blocks))
 
 
 def layer_kernel(src_hbm, *refs):
     lists = len(OFFSETS)
-    tiles_hbm, rows_hbm, agg_hbm, d_hidden = refs[:4]
+    tiles_hbm, rows_hbm, agg_hbm, d_hbm = refs[:4]
     halos, refs = refs[4 : 4 + lists], refs[4 + lists :]
-    hub, self_hbm, neigh_hbm, bias_hbm, hidden_hbm, d_pre_out, d_agg_out = refs[:7]
+    hub, self_hbm, neigh_hbm, bias_hbm, hidden_hbm, d_pre_out, d_agg_hbm = refs[:7]
     backs, refs = refs[7 : 7 + lists], refs[7 + lists :]
-    packed, src, weights, bias, table, rem_grad, backs_out, w_grad, b_grad, spread = refs[:10]
-    pack_out, tiles, rows, agg_local, hidden, sem_t, sem_back, sem_in, sem_out = refs[10:]
+    mine, theirs, src, weights, bias, table, rem_grad, backs_out, w_grad, b_grad = refs[:10]
+    spread, pack_out, tiles, rows, agg_local, d_hidden, hidden, d_agg_out = refs[10:18]
+    sem_t, sem_back, sem_in, sem_out = refs[18:]
     count, per_block, tile, _ = tiles.shape
     width = rows.shape[-1]
     per_list = halos[0].shape[0]
@@ -224,12 +222,17 @@
             (tiles_hbm.at[few], tiles.at[few]),
             (agg_hbm.at[many], agg_local.at[many]),
             (rows_hbm.at[many], rows.at[many]),
+            (d_hbm.at[many], d_hidden.at[many]),
         )
         return [pltpu.make_async_copy(*p, sem_in.at[i, n]) for n, p in enumerate(pairs)]
 
     def store(i):
-        many = rows_of(i, STEP * tile)
-        return pltpu.make_async_copy(hidden.at[many], hidden_hbm.at[many], sem_out.at[i])
+        few, many = pl.ds(i * STEP, STEP), rows_of(i, STEP * tile)
+        pairs = (
+            (hidden.at[many], hidden_hbm.at[many]),
+            (d_agg_out.at[few], d_agg_hbm.at[few]),
+        )
+        return [pltpu.make_async_copy(*p, sem_out.at[i, n]) for n, p in enumerate(pairs)]
 
     start(moves)
     for i in range(chunks):
@@ -261,7 +264,6 @@
         pre = jnp.dot(both, weights[...], preferred_element_type=F32) + bias[...]
         sig = jax.nn.sigmoid(pre)
         hidden[many, :] = (pre * sig).astype(BF16)
-        store(i).start()
         d_pre = d_hidden[many, :].astype(F32) * (sig * (1.0 + pre * (1.0 - sig)))
         b_grad[...] += jnp.sum(d_pre.reshape(-1, 8, d_pre.shape[-1]), 0)
         d_pre_b = d_pre.astype(BF16)
@@ -274,6 +276,7 @@
             terms = jnp.dot(own, edges(b), preferred_element_type=F32)
             for k, s in enumerate(sources[b]):
                 rem_grad[s] += terms[:, k * tile : (k + 1) * tile]
+        start(store(i))
         w_grad[...] += lax.dot_general(d_pre_b, both, TN, preferred_element_type=F32)
 
     sent = []
@@ -281,7 +284,8 @@
         backs_out[w] = rem_grad[pl.ds(s * per_list, per_list)].astype(BF16)
         sent.append(pltpu.make_async_copy(backs_out.at[w], backs[w], sem_back.at[w]))
     start(sent)
-    parts, chunk, _ = packed.shape
+    half, chunk, _ = mine.shape
+    parts = 2 * half
     owned = hub_blocks * tile // parts
     hub_rows = jnp.concatenate(
         [jnp.transpose(rem_grad[halo_count + q]) for q in range(hub_blocks)], 0
@@ -298,11 +302,15 @@
     spread[pl.ds(owned + 2, parts, stride=chunk), :] = jnp.transpose(two)
     for i in range(owned + 3, chunk):
         spread[pl.ds(i, parts, stride=chunk), :] = jnp.zeros((parts, width), F32)
-    pack_out[...] = spread[...].reshape(parts, chunk, width).astype(BF16)
-    last = pltpu.make_async_copy(pack_out, packed, sem_back.at[lists])
+    by_core = spread[...].reshape(half, 2, chunk, width)
+    odd = lists_of_ways()[0] == 1
+    pack_out[...] = jnp.where(odd, by_core[:, 0], by_core[:, 1]).astype(BF16)
+    last = pltpu.make_async_copy(pack_out, theirs, sem_back.at[lists])
     last.start()
+    mine[...] = jnp.where(odd, by_core[:, 1], by_core[:, 0])
     wait(sent)
-    wait([store(i) for i in range(chunks)])
+    for i in range(chunks):
+        wait(store(i))
     last.wait()
 
 
@@ -312,19 +320,19 @@
     units = d_hidden.shape[-1]
     lists, per_list = len(halos), halos[0].shape[0]
     table = lists * per_list + hub.shape[0]
-    packed = (parts, CHUNK, width)
+    pieces = (parts // 2, CHUNK, width)
     chunks = count // STEP
     return pl.pallas_call(
         layer_kernel,
         out_shape=[
             pltpu.HBM((nodes, units), BF16),
             pltpu.VMEM((nodes, units), BF16),
-            pltpu.VMEM((count, width, tile), BF16),
+            pltpu.HBM((count, width, tile), BF16),
         ]
         + [pltpu.HBM((per_list, width, tile), BF16)] * lists
-        + [pltpu.HBM(packed, BF16)],
-        in_specs=[HBM_SPEC] * 4 + [VMEM_SPEC] + [ANY_SPEC] * (lists + 1) + [HBM_SPEC] * 3,
-        out_specs=[HBM_SPEC] + [VMEM_SPEC] * 2 + [HBM_SPEC] * (lists + 1),
+        + [pltpu.VMEM(pieces, F32), pltpu.HBM(pieces, BF16)],
+        in_specs=[HBM_SPEC] * 5 + [ANY_SPEC] * (lists + 1) + [HBM_SPEC] * 3,
+        out_specs=[HBM_SPEC, VMEM_SPEC] + [HBM_SPEC] * (lists + 1) + [VMEM_SPEC, HBM_SPEC],
         scratch_shapes=[
             pltpu.SMEM(src.shape, jnp.int32),
             pltpu.VMEM((2 * width, units), BF16),
@@ -335,15 +343,17 @@
             pltpu.VMEM((units, 2 * width), F32),
             pltpu.VMEM((8, units), F32),
             pltpu.VMEM((parts * CHUNK, width), F32),
-            pltpu.VMEM(packed, BF16),
+            pltpu.VMEM(pieces, BF16),
             pltpu.VMEM(tiles.shape, BF16),
             pltpu.VMEM((nodes, width), BF16),
             pltpu.VMEM((nodes, width), F32),
             pltpu.VMEM((nodes, units), BF16),
+            pltpu.VMEM((nodes, units), BF16),
+            pltpu.VMEM((count, width, tile), BF16),
             pltpu.SemaphoreType.DMA((lists + 5,)),
             pltpu.SemaphoreType.DMA((lists + 1,)),
-            pltpu.SemaphoreType.DMA((chunks, 3)),
-            pltpu.SemaphoreType.DMA((chunks,)),
+            pltpu.SemaphoreType.DMA((chunks, 4)),
+            pltpu.SemaphoreType.DMA((chunks, 2)),
         ],
         compiler_params=params(),
         cost_estimate=pl.CostEstimate(
@@ -357,7 +367,7 @@
         hbm(tiles),
         hbm(rows),
         hbm(agg_local),
-        vmem(d_hidden),
+        hbm(d_hidden),
         *halos,
         hub,
         hbm(w_self),
@@ -366,28 +376,56 @@
     )
 
 
+def add_kernel(mine, theirs_any, out_hbm, theirs, out, sems):
+    load = pltpu.make_async_copy(theirs_any, theirs, sems.at[0])
+    load.start()
+    load.wait()
+    out[...] = (mine[...] + theirs[...].astype(F32)).astype(BF16)
+    save = pltpu.make_async_copy(out, out_hbm, sems.at[1])
+    save.start()
+    save.wait()
+
+
+def add_pieces(mine, theirs):
+    return pl.pallas_call(
+        add_kernel,
+        out_shape=pltpu.HBM(theirs.shape, BF16),
+        in_specs=[VMEM_SPEC, ANY_SPEC],
+        out_specs=HBM_SPEC,
+        scratch_shapes=[
+            pltpu.VMEM(theirs.shape, BF16),
+            pltpu.VMEM(theirs.shape, BF16),
+            pltpu.SemaphoreType.DMA((2,)),
+        ],
+        compiler_params=params(),
+        name="add_pieces",
+    )(vmem(mine), theirs)
+
+
 def back_kernel(
-    src_hbm, weight_hbm, tiles_hbm, d_pre, d_agg, total, src, weight, tiles, sems, sem_in
+    src_hbm, weight_hbm, tiles_hbm, d_hbm, d_pre, total, src, weight, tiles, d_agg, sems, sem_in
 ):
     count, per_block, tile, _ = tiles.shape
     size = STEP * tile
 
     def fetch(i):
         part = pl.ds(i * STEP, STEP)
-        return pltpu.make_async_copy(tiles_hbm.at[part], tiles.at[part], sem_in.at[i])
+        pairs = ((tiles_hbm.at[part], tiles.at[part]), (d_hbm.at[part], d_agg.at[part]))
+        return [pltpu.make_async_copy(*p, sem_in.at[i, n]) for n, p in enumerate(pairs)]
 
     loads = [
         pltpu.make_async_copy(src_hbm, src, sems.at[0]),
         pltpu.make_async_copy(weight_hbm, weight, sems.at[1]),
     ]
     start(loads)
-    start([fetch(i) for i in range(count // STEP)])
+    for i in range(count // STEP):
+        start(fetch(i))
     total[...] = jnp.zeros_like(total)
     wait(loads)
 
     @pl.loop(0, count // STEP)
     def _(i):
-        fetch(i).wait()
+        wait(fetch(i))
         own = lax.dot_general(
             weight[...], d_pre[rows_of(i, size), :], NT, preferred_element_type=F32
         )
@@ -407,14 +445,15 @@
     return pl.pallas_call(
         back_kernel,
         out_shape=pltpu.VMEM((count, width, tile), F32),
-        in_specs=[HBM_SPEC] * 3 + [VMEM_SPEC] * 2,
+        in_specs=[HBM_SPEC] * 4 + [VMEM_SPEC],
         out_specs=VMEM_SPEC,
         scratch_shapes=[
             pltpu.SMEM(src.shape, jnp.int32),
             pltpu.VMEM(weight.shape, BF16),
             pltpu.VMEM(tiles.shape, BF16),
+            pltpu.VMEM(d_agg.shape, BF16),
             pltpu.SemaphoreType.DMA((2,)),
-            pltpu.SemaphoreType.DMA((count // STEP,)),
+            pltpu.SemaphoreType.DMA((count // STEP, 2)),
         ],
         compiler_params=params(),
         cost_estimate=pl.CostEstimate(
@@ -423,7 +462,7 @@
             transcendentals=0,
         ),
         name="local_backward",
-    )(hbm(src), hbm(weight), hbm(tiles), vmem(d_pre), vmem(d_agg))
+    )(hbm(src), hbm(weight), hbm(tiles), hbm(d_agg), vmem(d_pre))
 
 
 def collect_kernel(send_hbm, hubs_hbm, _, *refs):
@@ -578,7 +617,7 @@
     *sends, hub_mine, own = gather_sends(send_blocks, hub_rows, blocks, parts)
     hub_all = lax.all_to_all(hub_mine, "dom", 0, 0)
     halos = [swapped(b, way) for way, b in enumerate(sends)]
-    agg_local, d_hid = local_aggregate(local_src.T, local_tiles, d_hidden, own)
+    agg_local = local_aggregate(local_src.T, local_tiles, own)
     hidden, d_pre, d_agg, *rest = layer(
         remote_src.T,
         remote_tiles,
@@ -589,11 +628,13 @@
         w_self,
         w_neigh,
         bias[None],
-        d_hid,
+        d_hidden,
         parts,
     )
-    *backs, packed = rest
-    pieces = lax.all_to_all(packed, "dom", 0, 0)
+    *backs, mine, theirs = rest
+    packed = add_pieces(mine, swapped(theirs, 0))
+    same_core = [list(range(c, parts, 2)) for c in range(2)]
+    pieces = lax.all_to_all(packed, "dom", 0, 0, axis_index_groups=same_core)
     returned = [swapped(b, way) for way, b in enumerate(backs)]
     grad_t = local_backward(local_src.T, local_tiles, d_pre, d_agg, w_self)
     rough, near = collect(send_blocks, hub_rows, grad_t, returned)

time: 85.6 us -> 78.4 us (0.916)
  local copies, waits for them, and re-layouts: 5.09 us -> 0 us
  waiting for transfers between devices: 8.55 us -> 5.84 us
  Pallas kernels: 24.9 us -> 26.2 us
    unnamed x8 -> x0, local copies, waits for them, and re-layouts: 5.09 us -> none
    ppermute x8 -> x9, waiting for transfers between devices: 8.55 us -> 5.84 us  [swapped(): lax.ppermute(block, 'dom', [(i, partner(i, way, n)) for i in range(n)])]
    all_to_all x1, starting transfers between devices: 8.55 us -> 6.17 us  [shards(): pieces = lax.all_to_all(packed, 'dom', 0, 0, axis_index_groups=same_core)]
    ppermute x8 -> x9, starting transfers between devices: 21.7 us -> 23.5 us  [swapped(): lax.ppermute(block, 'dom', [(i, partner(i, way, n)) for i in range(n)])]
    pallas_call x1 -> x2, Pallas kernels: 3.52 us -> 4.28 us  [the longest x1 3.51 us: local_aggregate(): pl.pallas_call(local_kernel, out_shape=pltpu.HBM(agg, F32), in_specs=[HBM...]
  transfers between devices with their start and end apart: 10 -> 11, of which waited for: 2 -> 3; matrix products, arithmetic and copies ran while one was open for 0% -> 0% of each run, Pallas kernels for 11% -> 13%
where the time goes in v4:
time: 78.4 us; the launch traced here: 78.1 us
  starting transfers between devices  45.3 us (58%)
  Pallas kernels  26.2 us (33%)
  waiting for transfers between devices  5.84 us (7%)
    ppermute x9, starting transfers between devices, swapped(): lax.ppermute(block, 'dom', [(i, partner(i, way, n)) for i in range(n)])  23.5 us
    all_to_all x1, starting transfers between devices, shards(): hub_all = lax.all_to_all(hub_mine, 'dom', 0, 0)  15.7 us
    pallas_call x1, Pallas kernels, layer(): pl.pallas_call(layer_kernel, out_shape=[pltpu.HBM((nodes, units), BF16),...  10.4 us
    all_to_all x1, starting transfers between devices, shards(): pieces = lax.all_to_all(packed, 'dom', 0, 0, axis_index_groups=same_core)  6.17 us
    ppermute x9, waiting for transfers between devices, swapped(): lax.ppermute(block, 'dom', [(i, partner(i, way, n)) for i in range(n)])  5.84 us
    pallas_call x1, Pallas kernels, local_backward(): pl.pallas_call(back_kernel, out_shape=pltpu.VMEM((count, width, tile), F3...  4.54 us
    pallas_call x1, Pallas kernels, local_aggregate(): pl.pallas_call(local_kernel, out_shape=pltpu.HBM(agg, F32), in_specs=[HBM...  3.51 us
    pallas_call x1, Pallas kernels, gather_sends(): pl.pallas_call(send_kernel, out_shape=[pltpu.HBM((per_list, tile, width),...  2.9 us
  transfers between devices with their start and end apart: 11, of which 3 were waited for; matrix products, arithmetic and copies ran while one was open for 0% of the time, Pallas kernels for 13%

profile of v4, /device:TPU:1, one launch (start us, length us, event | category | flops | bytes accessed | tf_op | source)
XLA Modules:
  0.0 78.1 jit_solution(10762158810756308819)
XLA Ops:
  0.6 2.9 %sends.1 = (bf16[4,128,128]{2,1,0:T(8,128)(2,1)}, bf16[4,128,128]{2,1,0:T(8,128)(2,1)}, bf16[4,128,128]{2,1,0:T(8,128)(2,1)}, bf16[4,128,128]{2,1,0:T(8,128)(2,1...) custom-call(s32[4,4]{1,0:T(4,128)} %send_hbm.3, s32[4]{0:T(128)} %hubs_hbm.5, ...), custom_call_target="tpu_custom_call" | custom-call | tf_op jit(solution)/shard_map/sends/pallas_call | solution.py:112
  3.5 15.7 %all-to-all-start = ((bf16[256,4,128]{2,1,0:T(4,128)(2,1)}), bf16[256,4,128]{2,1,0:T(4,128)(2,1)S(1)}, u32[]{:S(2)}, u32[]{:S(2)}) async-start(bf16[256,4,128]{2,1,0:T(4,128)(2,1)} %get-tuple-element.31), calls=%async_computation | async-start | bytes 524288 | tf_op jit(solution)/shard_map/all_to_all | solution.py:618
  19.2 2.2 %collective-permute-start = (bf16[4,128,128]{2,1,0:T(8,128)(2,1)}, bf16[4,128,128]{2,1,0:T(8,128)(2,1)S(1)}, u32[]{:S(2)}, u32[]{:S(2)}) collective-permute-start(bf16[4,128,128]{2,1,0:T(8,128)(2,1)} %get-tuple-element.27), channel_id=1, source_target_pairs={{0,1},{1,0},{2,3},{3,2},{4,5},{5,4},{6,7},{7,6},{8,9},{9,8},{10,11... | collective-permute-start | bytes 393224 | tf_op jit(solution)/shard_map/ppermute | solution.py:31
  21.4 0.0 collective-permute-start.1
  21.4 1.2 %collective-permute-start.2 = (bf16[4,128,128]{2,1,0:T(8,128)(2,1)}, bf16[4,128,128]{2,1,0:T(8,128)(2,1)S(1)}, u32[]{:S(2)}, u32[]{:S(2)}) collective-permute-start(bf16[4,128,128]{2,1,0:T(8,128)(2,1)} %get-tuple-element.29), channel_id=1, source_target_pairs={{0,2},{1,3},{2,0},{3,1},{4,6},{5,7},{6,4},{7,5},{8,10},{9,11},{10,... | collective-permute-start | bytes 393224 | tf_op jit(solution)/shard_map/ppermute | solution.py:31
  22.7 7.3 %collective-permute-start.3 = (bf16[4,128,128]{2,1,0:T(8,128)(2,1)}, bf16[4,128,128]{2,1,0:T(8,128)(2,1)S(1)}, u32[]{:S(2)}, u32[]{:S(2)}) collective-permute-start(bf16[4,128,128]{2,1,0:T(8,128)(2,1)} %get-tuple-element.30), channel_id=1, source_target_pairs={{0,254},{1,255},{2,4},{3,5},{4,2},{5,3},{6,8},{7,9},{8,6},{9,7},{1... | collective-permute-start | bytes 393224 | tf_op jit(solution)/shard_map/ppermute | solution.py:31
  30.0 3.5 %local_aggregate.1.refs_2_ = f32[4096,128]{1,0:T(8,128)} custom-call(s32[3,32]{1,0:T(4,128)} %bitcast.11, bf16[32,3,128,128]{3,2,1,0:T(8,128)(2,1)} %tiles_hbm.3, bf16[32,128,128]{2,1,0:T(8,128)(2,1)S(1)} %get-tuple-element.26.blocks), custom_call_target="tpu_custom_call" | custom-call | flops 402653184 | bytes 8388608 | tf_op jit(solution)/shard_map/local_aggregate/pallas_call | solution.py:171
  33.5 0.0 collective-permute-done.refs_4_
  33.5 0.0 collective-permute-done.2.refs_6_
  33.5 2.4 %collective-permute-done.3.refs_7_ = bf16[4,128,128]{2,1,0:T(8,128)(2,1)S(1)} collective-permute-done((bf16[4,128,128]{2,1,0:T(8,128)(2,1)}, bf16[4,128,128]{2,1,0:T(8,128)(2,1)S(1)}, u32[]{:S(2)}, u32[]{:S(2)}) %collective-permute-start.3) | collective-permute-done | bytes 131104 | tf_op jit(solution)/shard_map/ppermute | solution.py:31
  36.0 0.0 all-to-all-done
  36.0 10.4 %layer.1 = (bf16[4096,256]{1,0:T(8,128)(2,1)}, bf16[4096,256]{1,0:T(8,128)(2,1)S(1)}, bf16[32,128,128]{2,1,0:T(8,128)(2,1)}, bf16[4,128,128]{2,1,0:T(8,128)(2,1)...) custom-call(s32[3,32]{1,0:T(4,128)} %bitcast.13, ...), custom_call_target="tpu_custom_call" | custom-call | flops 2415919104 | bytes 14680064 | tf_op jit(solution)/shard_map/layer/pallas_call | solution.py:325
  46.4 3.6 %collective-permute-start.4 = (bf16[128,8,128]{2,1,0:T(8,128)(2,1)}, bf16[128,8,128]{2,1,0:T(8,128)(2,1)S(1)}, u32[]{:S(2)}, u32[]{:S(2)}) collective-permute-start(bf16[128,8,128]{2,1,0:T(8,128)(2,1)} %get-tuple-element.34), channel_id=1, source_target_pairs={{0,1},{1,0},{2,3},{3,2},{4,5},{5,4},{6,7},{7,6},{8,9},{9,8},{10,11... | collective-permute-start | bytes 786440 | tf_op jit(solution)/shard_map/ppermute | solution.py:31
  50.0 1.4 %collective-permute-done.4.theirs_any = bf16[128,8,128]{2,1,0:T(8,128)(2,1)S(1)} collective-permute-done((bf16[128,8,128]{2,1,0:T(8,128)(2,1)}, bf16[128,8,128]{2,1,0:T(8,128)(2,1)S(1)}, u32[]{:S(2)}, u32[]{:S(2)}) %collective-permute-start.4) | collective-permute-done | bytes 262176 | tf_op jit(solution)/shard_map/ppermute | solution.py:31
  51.3 0.8 add_pieces.1
  52.1 6.2 %all-to-all-start.1 = ((bf16[128,8,128]{2,1,0:T(8,128)(2,1)}), bf16[128,8,128]{2,1,0:T(8,128)(2,1)S(1)}, u32[]{:S(2)}, u32[]{:S(2)}) async-start(bf16[128,8,128]{2,1,0:T(8,128)(2,1)} %add_pieces.1), calls=%async_computation.1 | async-start | bytes 524288 | tf_op jit(solution)/shard_map/all_to_all | solution.py:637
  58.3 0.6 collective-permute-start.5
  58.9 0.8 %collective-permute-start.6 = (bf16[4,128,128]{2,1,0:T(8,128)(2,1)}, bf16[4,128,128]{2,1,0:T(8,128)(2,1)S(1)}, u32[]{:S(2)}, u32[]{:S(2)}) collective-permute-start(bf16[4,128,128]{2,1,0:T(8,128)(2,1)} %get-tuple-element.38), channel_id=1, source_target_pairs={{0,255},{1,2},{2,1},{3,4},{4,3},{5,6},{6,5},{7,8},{8,7},{9,10},{10... | collective-permute-start | bytes 393224 | tf_op jit(solution)/shard_map/ppermute | solution.py:31
  59.8 1.2 %collective-permute-start.7 = (bf16[4,128,128]{2,1,0:T(8,128)(2,1)}, bf16[4,128,128]{2,1,0:T(8,128)(2,1)S(1)}, u32[]{:S(2)}, u32[]{:S(2)}) collective-permute-start(bf16[4,128,128]{2,1,0:T(8,128)(2,1)} %get-tuple-element.39), channel_id=1, source_target_pairs={{0,2},{1,3},{2,0},{3,1},{4,6},{5,7},{6,4},{7,5},{8,10},{9,11},{10,... | collective-permute-start | bytes 393224 | tf_op jit(solution)/shard_map/ppermute | solution.py:31
  60.9 6.5 %collective-permute-start.8 = (bf16[4,128,128]{2,1,0:T(8,128)(2,1)}, bf16[4,128,128]{2,1,0:T(8,128)(2,1)S(1)}, u32[]{:S(2)}, u32[]{:S(2)}) collective-permute-start(bf16[4,128,128]{2,1,0:T(8,128)(2,1)} %get-tuple-element.40), channel_id=1, source_target_pairs={{0,254},{1,255},{2,4},{3,5},{4,2},{5,3},{6,8},{7,9},{8,6},{9,7},{1... | collective-permute-start | bytes 393224 | tf_op jit(solution)/shard_map/ppermute | solution.py:31
  67.4 4.5 %local_backward.1._ = f32[32,128,128]{2,1,0:T(8,128)S(1)} custom-call(s32[3,32]{1,0:T(4,128)} %bitcast.12, bf16[128,256]{1,0:T(8,128)(2,1)} %weight_hbm.1, bf16[32,3,128,128]{3,2,1,0:T(8,128)(2,1)} %tiles_hbm.3, bf16[32,128,128]{2,1,0:T(8,128)(2,1)} %get-tuple-element.35.d_hbm, bf16[4096,256]{1,0:T(8,128)(2,1)S(1)} %get-tuple-element.36.d_pre), custom_call_target="tpu_custom_call" | custom-call | flops 671088640 | bytes 8388608 | tf_op jit(solution)/shard_map/local_backward/pallas_call | solution.py:445
  72.0 2.0 %collective-permute-done.8.refs_3_ = bf16[4,128,128]{2,1,0:T(8,128)(2,1)S(1)} collective-permute-done((bf16[4,128,128]{2,1,0:T(8,128)(2,1)}, bf16[4,128,128]{2,1,0:T(8,128)(2,1)S(1)}, u32[]{:S(2)}, u32[]{:S(2)}) %collective-permute-start.8) | collective-permute-done | bytes 131104 | tf_op jit(solution)/shard_map/ppermute | solution.py:31
  74.0 2.0 %collect.1 = (f32[32,128,128]{2,1,0:T(8,128)S(1)}, bf16[4096,128]{1,0:T(8,128)(2,1)}, f32[4,16,128]{2,1,0:T(8,128)S(1)}) custom-call(s32[4,4]{1,0:T(4,128)} %send_hbm.3, s32[4]{0:T(128)} %hubs_hbm.5, f32[32,128,128]{2,1,0:T(8,128)S(1)} %local_backward.1._, bf16[4,128,128]{2,1,0:T(8,128)(2,1)S(1)} %collective-permute-done.5.refs_0_, ...), custom_call_target="tpu_custom_call", output_to_operand_aliasing={{0}: (2, {})} | custom-call | flops 4194304 | bytes 4194304 | tf_op jit(solution)/shard_map/collect/pallas_call | solution.py:505
  76.1 2.0 %finish.1 = (bf16[4096,128]{1,0:T(8,128)(2,1)}, f32[1,128]{1,0:T(1,128)}, f32[1,128]{1,0:T(1,128)}, f32[1,128]{1,0:T(1,128)}) custom-call(s32[4]{0:T(128)} %hubs_hbm.5, bf16[128,8,128]{2,1,0:T(8,128)(2,1)S(1)} %all-to-all-done.1.pieces_hbm, f32[4,16,128]{2,1,0:T(8,128)S(1)} %get-tuple-element.41.near, ...), custom_call_target="tpu_custom_call", output_to_operand_aliasing={{0}: (3, {})} | custom-call | tf_op jit(solution)/shard_map/finish/pallas_call | solution.py:581
  (5 shorter events, 0.0 us)
Async XLA Ops:
  3.5 32.4 %all-to-all-start = ((bf16[256,4,128]{2,1,0:T(4,128)(2,1)}), bf16[256,4,128]{2,1,0:T(4,128)(2,1)S(1)}, u32[]{:S(2)}, u32[]{:S(2)}) async-start(bf16[256,4,128]{2,1,0:T(4,128)(2,1)} %get-tuple-element.31), calls=%async_computation | async-start | bytes 524288 | tf_op jit(solution)/shard_map/all_to_all | solution.py:618
  19.2 14.3 %collective-permute-start = (bf16[4,128,128]{2,1,0:T(8,128)(2,1)}, bf16[4,128,128]{2,1,0:T(8,128)(2,1)S(1)}, u32[]{:S(2)}, u32[]{:S(2)}) collective-permute-start(bf16[4,128,128]{2,1,0:T(8,128)(2,1)} %get-tuple-element.27), channel_id=1, source_target_pairs={{0,1},{1,0},{2,3},{3,2},{4,5},{5,4},{6,7},{7,6},{8,9},{9,8},{10,11... | collective-permute-start | bytes 393224 | tf_op jit(solution)/shard_map/ppermute | solution.py:31
  21.4 12.1 %collective-permute-start.1 = (bf16[4,128,128]{2,1,0:T(8,128)(2,1)}, bf16[4,128,128]{2,1,0:T(8,128)(2,1)S(1)}, u32[]{:S(2)}, u32[]{:S(2)}) collective-permute-start(bf16[4,128,128]{2,1,0:T(8,128)(2,1)} %get-tuple-element.28), channel_id=1, source_target_pairs={{0,255},{1,2},{2,1},{3,4},{4,3},{5,6},{6,5},{7,8},{8,7},{9,10},{10... | collective-permute-start | bytes 393224 | tf_op jit(solution)/shard_map/ppermute | solution.py:31
  21.4 12.1 %collective-permute-start.2 = (bf16[4,128,128]{2,1,0:T(8,128)(2,1)}, bf16[4,128,128]{2,1,0:T(8,128)(2,1)S(1)}, u32[]{:S(2)}, u32[]{:S(2)}) collective-permute-start(bf16[4,128,128]{2,1,0:T(8,128)(2,1)} %get-tuple-element.29), channel_id=1, source_target_pairs={{0,2},{1,3},{2,0},{3,1},{4,6},{5,7},{6,4},{7,5},{8,10},{9,11},{10,... | collective-permute-start | bytes 393224 | tf_op jit(solution)/shard_map/ppermute | solution.py:31
  22.7 13.3 %collective-permute-start.3 = (bf16[4,128,128]{2,1,0:T(8,128)(2,1)}, bf16[4,128,128]{2,1,0:T(8,128)(2,1)S(1)}, u32[]{:S(2)}, u32[]{:S(2)}) collective-permute-start(bf16[4,128,128]{2,1,0:T(8,128)(2,1)} %get-tuple-element.30), channel_id=1, source_target_pairs={{0,254},{1,255},{2,4},{3,5},{4,2},{5,3},{6,8},{7,9},{8,6},{9,7},{1... | collective-permute-start | bytes 393224 | tf_op jit(solution)/shard_map/ppermute | solution.py:31
  46.4 5.0 %collective-permute-start.4 = (bf16[128,8,128]{2,1,0:T(8,128)(2,1)}, bf16[128,8,128]{2,1,0:T(8,128)(2,1)S(1)}, u32[]{:S(2)}, u32[]{:S(2)}) collective-permute-start(bf16[128,8,128]{2,1,0:T(8,128)(2,1)} %get-tuple-element.34), channel_id=1, source_target_pairs={{0,1},{1,0},{2,3},{3,2},{4,5},{5,4},{6,7},{7,6},{8,9},{9,8},{10,11... | collective-permute-start | bytes 786440 | tf_op jit(solution)/shard_map/ppermute | solution.py:31
  52.1 23.9 %all-to-all-start.1 = ((bf16[128,8,128]{2,1,0:T(8,128)(2,1)}), bf16[128,8,128]{2,1,0:T(8,128)(2,1)S(1)}, u32[]{:S(2)}, u32[]{:S(2)}) async-start(bf16[128,8,128]{2,1,0:T(8,128)(2,1)} %add_pieces.1), calls=%async_computation.1 | async-start | bytes 524288 | tf_op jit(solution)/shard_map/all_to_all | solution.py:637
  58.3 13.6 %collective-permute-start.5 = (bf16[4,128,128]{2,1,0:T(8,128)(2,1)}, bf16[4,128,128]{2,1,0:T(8,128)(2,1)S(1)}, u32[]{:S(2)}, u32[]{:S(2)}) collective-permute-start(bf16[4,128,128]{2,1,0:T(8,128)(2,1)} %get-tuple-element.37), channel_id=1, source_target_pairs={{0,1},{1,0},{2,3},{3,2},{4,5},{5,4},{6,7},{7,6},{8,9},{9,8},{10,11... | collective-permute-start | bytes 393224 | tf_op jit(solution)/shard_map/ppermute | solution.py:31
  58.9 13.0 %collective-permute-start.6 = (bf16[4,128,128]{2,1,0:T(8,128)(2,1)}, bf16[4,128,128]{2,1,0:T(8,128)(2,1)S(1)}, u32[]{:S(2)}, u32[]{:S(2)}) collective-permute-start(bf16[4,128,128]{2,1,0:T(8,128)(2,1)} %get-tuple-element.38), channel_id=1, source_target_pairs={{0,255},{1,2},{2,1},{3,4},{4,3},{5,6},{6,5},{7,8},{8,7},{9,10},{10... | collective-permute-start | bytes 393224 | tf_op jit(solution)/shard_map/ppermute | solution.py:31
  59.8 12.2 %collective-permute-start.7 = (bf16[4,128,128]{2,1,0:T(8,128)(2,1)}, bf16[4,128,128]{2,1,0:T(8,128)(2,1)S(1)}, u32[]{:S(2)}, u32[]{:S(2)}) collective-permute-start(bf16[4,128,128]{2,1,0:T(8,128)(2,1)} %get-tuple-element.39), channel_id=1, source_target_pairs={{0,2},{1,3},{2,0},{3,1},{4,6},{5,7},{6,4},{7,5},{8,10},{9,11},{10,... | collective-permute-start | bytes 393224 | tf_op jit(solution)/shard_map/ppermute | solution.py:31
  60.9 13.1 %collective-permute-start.8 = (bf16[4,128,128]{2,1,0:T(8,128)(2,1)}, bf16[4,128,128]{2,1,0:T(8,128)(2,1)S(1)}, u32[]{:S(2)}, u32[]{:S(2)}) collective-permute-start(bf16[4,128,128]{2,1,0:T(8,128)(2,1)} %get-tuple-element.40), channel_id=1, source_target_pairs={{0,254},{1,255},{2,4},{3,5},{4,2},{5,3},{6,8},{7,9},{8,6},{9,7},{1... | collective-permute-start | bytes 393224 | tf_op jit(solution)/shard_map/ppermute | solution.py:31

commit v5 on v4

--- a/solution.py
+++ b/solution.py
@@ -102,8 +102,23 @@
         near = blocks[row // tile, pl.ds(base, GROUP), :].astype(F32)
         chosen = jnp.where(place == lax.rem(row, GROUP), near, 0.0)
         rows.append(jnp.sum(chosen, 0, keepdims=True))
-    hub_out[...] = jnp.broadcast_to(jnp.concatenate(rows, 0).astype(BF16)[None], hub_out.shape)
+    hub_out[...] = jnp.concatenate(rows, 0)
     wait(moves)
+
+
+def spread_kernel(hub, _, out):
+    out[...] = jnp.broadcast_to(hub[...].astype(BF16)[None], out.shape)
+
+
+def spread_hubs(hub, after, parts):
+    return pl.pallas_call(
+        spread_kernel,
+        out_shape=jax.ShapeDtypeStruct((parts,) + hub.shape, BF16),
+        in_specs=[VMEM_SPEC, ANY_SPEC],
+        out_specs=VMEM_SPEC,
+        compiler_params=params(),
+        name="spread_hubs",
+    )(hub, after)
 
 
 def gather_sends(send, hubs, blocks, parts):
@@ -113,7 +128,7 @@
         send_kernel,
         out_shape=[pltpu.HBM((per_list, tile, width), BF16)] * lists
         + [
-            jax.ShapeDtypeStruct((parts, hubs.shape[0], width), BF16),
+            pltpu.VMEM((hubs.shape[0], width), F32),
             pltpu.VMEM(blocks.shape, BF16),
         ],
         in_specs=[HBM_SPEC] * 3,
@@ -183,7 +198,7 @@
         ],
         compiler_params=params(),
         cost_estimate=pl.CostEstimate(
-            flops=2 * tiles.size * width, bytes_accessed=8 << 20, transcendentals=0
+            flops=10**10, bytes_accessed=64 << 20, transcendentals=0
         ),
         name="local_aggregate",
     )(hbm(src), hbm(tiles), vmem(blocks))
@@ -457,9 +472,7 @@
         ],
         compiler_params=params(),
         cost_estimate=pl.CostEstimate(
-            flops=2 * tiles.size * width + 2 * d_pre.size * width,
-            bytes_accessed=8 << 20,
-            transcendentals=0,
+            flops=10**10, bytes_accessed=64 << 20, transcendentals=0
         ),
         name="local_backward",
     )(hbm(src), hbm(weight), hbm(tiles), hbm(d_agg), vmem(d_pre))
@@ -615,8 +628,8 @@
     owned = hub_rows.shape[0]
     blocks = features.reshape(nodes // tile, tile, width)
     *sends, hub_mine, own = gather_sends(send_blocks, hub_rows, blocks, parts)
-    hub_all = lax.all_to_all(hub_mine, "dom", 0, 0)
     halos = [swapped(b, way) for way, b in enumerate(sends)]
+    hub_all = lax.all_to_all(spread_hubs(vmem(hub_mine), halos[0], parts), "dom", 0, 0)
     agg_local = local_aggregate(local_src.T, local_tiles, own)
     hidden, d_pre, d_agg, *rest = layer(
         remote_src.T,

time: 78.4 us -> 83.5 us (1.065)
  waiting for transfers between devices: 5.84 us -> 20.6 us
  starting transfers between devices: 45.3 us -> 35.6 us
    all_to_all x1, waiting for transfers between devices: 0.01 us -> 12.4 us  [shards(): lax.all_to_all(spread_hubs(vmem(hub_mine), halos[0], parts), 'dom', 0, 0)]
    all_to_all x1, waiting for transfers between devices: 0.01 us -> 8.22 us  [shards(): pieces = lax.all_to_all(packed, 'dom', 0, 0, axis_index_groups=same_core)]
    all_to_all x1, starting transfers between devices: 15.7 us -> 8.28 us  [shards(): lax.all_to_all(spread_hubs(vmem(hub_mine), halos[0], parts), 'dom', 0, 0)]
    ppermute x9, waiting for transfers between devices: 5.84 us -> 0.02 us  [swapped(): lax.ppermute(block, 'dom', [(i, partner(i, way, n)) for i in range(n)])]
    ppermute x9, starting transfers between devices: 23.5 us -> 21.2 us  [swapped(): lax.ppermute(block, 'dom', [(i, partner(i, way, n)) for i in range(n)])]
  transfers between devices with their start and end apart: 11 -> 11, of which waited for: 3 -> 2; matrix products, arithmetic and copies ran while one was open for 0% -> 0% of each run, Pallas kernels for 13% -> 14%
where the time goes in v5:
time: 83.5 us; the launch traced here: 83.2 us
  starting transfers between devices  35.6 us (43%)
  Pallas kernels  26.2 us (31%)
  waiting for transfers between devices  20.6 us (25%)
    ppermute x9, starting transfers between devices, swapped(): lax.ppermute(block, 'dom', [(i, partner(i, way, n)) for i in range(n)])  21.2 us
    all_to_all x1, waiting for transfers between devices, shards(): lax.all_to_all(spread_hubs(vmem(hub_mine), halos[0], parts), 'dom', 0, 0)  12.4 us
    pallas_call x1, Pallas kernels, layer(): pl.pallas_call(layer_kernel, out_shape=[pltpu.HBM((nodes, units), BF16),...  10.4 us
    all_to_all x1, starting transfers between devices, shards(): lax.all_to_all(spread_hubs(vmem(hub_mine), halos[0], parts), 'dom', 0, 0)  8.28 us
    all_to_all x1, waiting for transfers between devices, shards(): pieces = lax.all_to_all(packed, 'dom', 0, 0, axis_index_groups=same_core)  8.22 us
    all_to_all x1, starting transfers between devices, shards(): pieces = lax.all_to_all(packed, 'dom', 0, 0, axis_index_groups=same_core)  6.17 us
    pallas_call x1, Pallas kernels, local_backward(): pl.pallas_call(back_kernel, out_shape=pltpu.VMEM((count, width, tile), F3...  4.54 us
    pallas_call x1, Pallas kernels, local_aggregate(): pl.pallas_call(local_kernel, out_shape=pltpu.HBM(agg, F32), in_specs=[HBM...  3.51 us
  transfers between devices with their start and end apart: 11, of which 2 were waited for; matrix products, arithmetic and copies ran while one was open for 0% of the time, Pallas kernels for 14%

profile of v5, /device:TPU:1, one launch (start us, length us, event | category | flops | bytes accessed | tf_op | source)
XLA Modules:
  0.0 83.2 jit_solution(1201360650686678140)
XLA Ops:
  0.6 2.1 %sends.1 = (bf16[4,128,128]{2,1,0:T(8,128)(2,1)}, bf16[4,128,128]{2,1,0:T(8,128)(2,1)}, bf16[4,128,128]{2,1,0:T(8,128)(2,1)}, bf16[4,128,128]{2,1,0:T(8,128)(2,1...) custom-call(s32[4,4]{1,0:T(4,128)} %send_hbm.3, s32[4]{0:T(128)} %hubs_hbm.5, bf16[32,128,128]{2,1,0:T(8,128)(2,1)} %bitcast.10), custom_call_target="tpu_custom_call" | custom-call | tf_op jit(solution)/shard_map/sends/pallas_call | solution.py:127
  2.8 3.3 %collective-permute-start = (bf16[4,128,128]{2,1,0:T(8,128)(2,1)}, bf16[4,128,128]{2,1,0:T(8,128)(2,1)S(1)}, u32[]{:S(2)}, u32[]{:S(2)}) collective-permute-start(bf16[4,128,128]{2,1,0:T(8,128)(2,1)} %get-tuple-element.27), channel_id=1, source_target_pairs={{0,1},{1,0},{2,3},{3,2},{4,5},{5,4},{6,7},{7,6},{8,9},{9,8},{10,11... | collective-permute-start | bytes 393224 | tf_op jit(solution)/shard_map/ppermute | solution.py:31
  6.1 1.5 %collective-permute-start.2 = (bf16[4,128,128]{2,1,0:T(8,128)(2,1)}, bf16[4,128,128]{2,1,0:T(8,128)(2,1)S(1)}, u32[]{:S(2)}, u32[]{:S(2)}) collective-permute-start(bf16[4,128,128]{2,1,0:T(8,128)(2,1)} %get-tuple-element.29), channel_id=1, source_target_pairs={{0,2},{1,3},{2,0},{3,1},{4,6},{5,7},{6,4},{7,5},{8,10},{9,11},{10,... | collective-permute-start | bytes 393224 | tf_op jit(solution)/shard_map/ppermute | solution.py:31
  7.6 8.4 %collective-permute-start.3 = (bf16[4,128,128]{2,1,0:T(8,128)(2,1)}, bf16[4,128,128]{2,1,0:T(8,128)(2,1)S(1)}, u32[]{:S(2)}, u32[]{:S(2)}) collective-permute-start(bf16[4,128,128]{2,1,0:T(8,128)(2,1)} %get-tuple-element.30), channel_id=1, source_target_pairs={{0,254},{1,255},{2,4},{3,5},{4,2},{5,3},{6,8},{7,9},{8,6},{9,7},{1... | collective-permute-start | bytes 393224 | tf_op jit(solution)/shard_map/ppermute | solution.py:31
  16.1 0.8 spread_hubs.1
  16.8 8.3 %all-to-all-start = ((bf16[256,4,128]{2,1,0:T(4,128)(2,1)}), bf16[256,4,128]{2,1,0:T(4,128)(2,1)S(1)}, u32[]{:S(2)}, u32[]{:S(2)}) async-start(bf16[256,4,128]{2,1,0:T(4,128)(2,1)} %spread_hubs.1), calls=%async_computation | async-start | bytes 524288 | tf_op jit(solution)/shard_map/all_to_all | solution.py:632
  25.1 3.5 %local_aggregate.1.refs_2_ = f32[4096,128]{1,0:T(8,128)} custom-call(s32[3,32]{1,0:T(4,128)} %bitcast.13, bf16[32,3,128,128]{3,2,1,0:T(8,128)(2,1)} %tiles_hbm.3, bf16[32,128,128]{2,1,0:T(8,128)(2,1)S(1)} %get-tuple-element.26.blocks), custom_call_target="tpu_custom_call" | custom-call | flops 10000000000 | bytes 67108864 | tf_op jit(solution)/shard_map/local_aggregate/pallas_call | solution.py:186
  28.6 0.0 collective-permute-done.1.refs_5_
  28.7 12.4 %all-to-all-done = bf16[256,4,128]{2,1,0:T(4,128)(2,1)S(1)} async-done(((bf16[256,4,128]{2,1,0:T(4,128)(2,1)}), bf16[256,4,128]{2,1,0:T(4,128)(2,1)S(1)}, u32[]{:S(2)}, u32[]{:S(2)}) %all-to-all-start) | async-done | bytes 262176 | tf_op jit(solution)/shard_map/all_to_all | solution.py:632
  41.0 10.4 %layer.1 = (bf16[4096,256]{1,0:T(8,128)(2,1)}, bf16[4096,256]{1,0:T(8,128)(2,1)S(1)}, bf16[32,128,128]{2,1,0:T(8,128)(2,1)}, bf16[4,128,128]{2,1,0:T(8,128)(2,1)...) custom-call(s32[3,32]{1,0:T(4,128)} %bitcast.11, ...), custom_call_target="tpu_custom_call" | custom-call | flops 2415919104 | bytes 14680064 | tf_op jit(solution)/shard_map/layer/pallas_call | solution.py:340
  51.4 0.6 collective-permute-start.4
  52.0 0.1 collective-permute-start.5
  52.1 1.0 %collective-permute-start.6 = (bf16[4,128,128]{2,1,0:T(8,128)(2,1)}, bf16[4,128,128]{2,1,0:T(8,128)(2,1)S(1)}, u32[]{:S(2)}, u32[]{:S(2)}) collective-permute-start(bf16[4,128,128]{2,1,0:T(8,128)(2,1)} %get-tuple-element.38), channel_id=1, source_target_pairs={{0,255},{1,2},{2,1},{3,4},{4,3},{5,6},{6,5},{7,8},{8,7},{9,10},{10... | collective-permute-start | bytes 393224 | tf_op jit(solution)/shard_map/ppermute | solution.py:31
  53.2 0.0 collective-permute-start.7
  53.2 6.2 %collective-permute-start.8 = (bf16[4,128,128]{2,1,0:T(8,128)(2,1)}, bf16[4,128,128]{2,1,0:T(8,128)(2,1)S(1)}, u32[]{:S(2)}, u32[]{:S(2)}) collective-permute-start(bf16[4,128,128]{2,1,0:T(8,128)(2,1)} %get-tuple-element.40), channel_id=1, source_target_pairs={{0,254},{1,255},{2,4},{3,5},{4,2},{5,3},{6,8},{7,9},{8,6},{9,7},{1... | collective-permute-start | bytes 393224 | tf_op jit(solution)/shard_map/ppermute | solution.py:31
  59.3 0.0 collective-permute-done.4.theirs_any
  59.3 0.8 add_pieces.1
  60.1 6.2 %all-to-all-start.1 = ((bf16[128,8,128]{2,1,0:T(8,128)(2,1)}), bf16[128,8,128]{2,1,0:T(8,128)(2,1)S(1)}, u32[]{:S(2)}, u32[]{:S(2)}) async-start(bf16[128,8,128]{2,1,0:T(8,128)(2,1)} %add_pieces.1), calls=%async_computation.1 | async-start | bytes 524288 | tf_op jit(solution)/shard_map/all_to_all | solution.py:650
  66.3 4.5 %local_backward.1._ = f32[32,128,128]{2,1,0:T(8,128)S(1)} custom-call(s32[3,32]{1,0:T(4,128)} %bitcast.14, bf16[128,256]{1,0:T(8,128)(2,1)} %weight_hbm.1, bf16[32,3,128,128]{3,2,1,0:T(8,128)(2,1)} %tiles_hbm.3, bf16[32,128,128]{2,1,0:T(8,128)(2,1)} %get-tuple-element.35.d_hbm, bf16[4096,256]{1,0:T(8,128)(2,1)S(1)} %get-tuple-element.36.d_pre), custom_call_target="tpu_custom_call" | custom-call | flops 10000000000 | bytes 67108864 | tf_op jit(solution)/shard_map/local_backward/pallas_call | solution.py:460
  70.9 0.0 collective-permute-done.6.refs_1_
  70.9 0.0 collective-permute-done.7.refs_2_
  70.9 2.0 %collect.1 = (f32[32,128,128]{2,1,0:T(8,128)S(1)}, bf16[4096,128]{1,0:T(8,128)(2,1)}, f32[4,16,128]{2,1,0:T(8,128)S(1)}) custom-call(s32[4,4]{1,0:T(4,128)} %send_hbm.3, s32[4]{0:T(128)} %hubs_hbm.5, f32[32,128,128]{2,1,0:T(8,128)S(1)} %local_backward.1._, bf16[4,128,128]{2,1,0:T(8,128)(2,1)S(1)} %collective-permute-done.5.refs_0_, ...), custom_call_target="tpu_custom_call", output_to_operand_aliasing={{0}: (2, {})} | custom-call | flops 4194304 | bytes 4194304 | tf_op jit(solution)/shard_map/collect/pallas_call | solution.py:518
  72.9 8.2 %all-to-all-done.1.pieces_hbm = bf16[128,8,128]{2,1,0:T(8,128)(2,1)S(1)} async-done(((bf16[128,8,128]{2,1,0:T(8,128)(2,1)}), bf16[128,8,128]{2,1,0:T(8,128)(2,1)S(1)}, u32[]{:S(2)}, u32[]{:S(2)}) %all-to-all-start.1) | async-done | bytes 262176 | tf_op jit(solution)/shard_map/all_to_all | solution.py:650
  81.1 2.0 %finish.1 = (bf16[4096,128]{1,0:T(8,128)(2,1)}, f32[1,128]{1,0:T(1,128)}, f32[1,128]{1,0:T(1,128)}, f32[1,128]{1,0:T(1,128)}) custom-call(s32[4]{0:T(128)} %hubs_hbm.5, bf16[128,8,128]{2,1,0:T(8,128)(2,1)S(1)} %all-to-all-done.1.pieces_hbm, f32[4,16,128]{2,1,0:T(8,128)S(1)} %get-tuple-element.41.near, ...), custom_call_target="tpu_custom_call", output_to_operand_aliasing={{0}: (3, {})} | custom-call | tf_op jit(solution)/shard_map/finish/pallas_call | solution.py:594
  (6 shorter events, 0.0 us)
Async XLA Ops:
  2.8 13.3 %collective-permute-start = (bf16[4,128,128]{2,1,0:T(8,128)(2,1)}, bf16[4,128,128]{2,1,0:T(8,128)(2,1)S(1)}, u32[]{:S(2)}, u32[]{:S(2)}) collective-permute-start(bf16[4,128,128]{2,1,0:T(8,128)(2,1)} %get-tuple-element.27), channel_id=1, source_target_pairs={{0,1},{1,0},{2,3},{3,2},{4,5},{5,4},{6,7},{7,6},{8,9},{9,8},{10,11... | collective-permute-start | bytes 393224 | tf_op jit(solution)/shard_map/ppermute | solution.py:31
  6.1 22.5 %collective-permute-start.1 = (bf16[4,128,128]{2,1,0:T(8,128)(2,1)}, bf16[4,128,128]{2,1,0:T(8,128)(2,1)S(1)}, u32[]{:S(2)}, u32[]{:S(2)}) collective-permute-start(bf16[4,128,128]{2,1,0:T(8,128)(2,1)} %get-tuple-element.28), channel_id=1, source_target_pairs={{0,255},{1,2},{2,1},{3,4},{4,3},{5,6},{6,5},{7,8},{8,7},{9,10},{10... | collective-permute-start | bytes 393224 | tf_op jit(solution)/shard_map/ppermute | solution.py:31
  6.1 22.5 %collective-permute-start.2 = (bf16[4,128,128]{2,1,0:T(8,128)(2,1)}, bf16[4,128,128]{2,1,0:T(8,128)(2,1)S(1)}, u32[]{:S(2)}, u32[]{:S(2)}) collective-permute-start(bf16[4,128,128]{2,1,0:T(8,128)(2,1)} %get-tuple-element.29), channel_id=1, source_target_pairs={{0,2},{1,3},{2,0},{3,1},{4,6},{5,7},{6,4},{7,5},{8,10},{9,11},{10,... | collective-permute-start | bytes 393224 | tf_op jit(solution)/shard_map/ppermute | solution.py:31
  7.6 21.0 %collective-permute-start.3 = (bf16[4,128,128]{2,1,0:T(8,128)(2,1)}, bf16[4,128,128]{2,1,0:T(8,128)(2,1)S(1)}, u32[]{:S(2)}, u32[]{:S(2)}) collective-permute-start(bf16[4,128,128]{2,1,0:T(8,128)(2,1)} %get-tuple-element.30), channel_id=1, source_target_pairs={{0,254},{1,255},{2,4},{3,5},{4,2},{5,3},{6,8},{7,9},{8,6},{9,7},{1... | collective-permute-start | bytes 393224 | tf_op jit(solution)/shard_map/ppermute | solution.py:31
  16.8 24.2 %all-to-all-start = ((bf16[256,4,128]{2,1,0:T(4,128)(2,1)}), bf16[256,4,128]{2,1,0:T(4,128)(2,1)S(1)}, u32[]{:S(2)}, u32[]{:S(2)}) async-start(bf16[256,4,128]{2,1,0:T(4,128)(2,1)} %spread_hubs.1), calls=%async_computation | async-start | bytes 524288 | tf_op jit(solution)/shard_map/all_to_all | solution.py:632
  51.4 7.9 %collective-permute-start.4 = (bf16[128,8,128]{2,1,0:T(8,128)(2,1)}, bf16[128,8,128]{2,1,0:T(8,128)(2,1)S(1)}, u32[]{:S(2)}, u32[]{:S(2)}) collective-permute-start(bf16[128,8,128]{2,1,0:T(8,128)(2,1)} %get-tuple-element.34), channel_id=1, source_target_pairs={{0,1},{1,0},{2,3},{3,2},{4,5},{5,4},{6,7},{7,6},{8,9},{9,8},{10,11... | collective-permute-start | bytes 786440 | tf_op jit(solution)/shard_map/ppermute | solution.py:31
  52.0 18.8 %collective-permute-start.5 = (bf16[4,128,128]{2,1,0:T(8,128)(2,1)}, bf16[4,128,128]{2,1,0:T(8,128)(2,1)S(1)}, u32[]{:S(2)}, u32[]{:S(2)}) collective-permute-start(bf16[4,128,128]{2,1,0:T(8,128)(2,1)} %get-tuple-element.37), channel_id=1, source_target_pairs={{0,1},{1,0},{2,3},{3,2},{4,5},{5,4},{6,7},{7,6},{8,9},{9,8},{10,11... | collective-permute-start | bytes 393224 | tf_op jit(solution)/shard_map/ppermute | solution.py:31
  52.1 18.7 %collective-permute-start.6 = (bf16[4,128,128]{2,1,0:T(8,128)(2,1)}, bf16[4,128,128]{2,1,0:T(8,128)(2,1)S(1)}, u32[]{:S(2)}, u32[]{:S(2)}) collective-permute-start(bf16[4,128,128]{2,1,0:T(8,128)(2,1)} %get-tuple-element.38), channel_id=1, source_target_pairs={{0,255},{1,2},{2,1},{3,4},{4,3},{5,6},{6,5},{7,8},{8,7},{9,10},{10... | collective-permute-start | bytes 393224 | tf_op jit(solution)/shard_map/ppermute | solution.py:31
  53.2 17.7 %collective-permute-start.7 = (bf16[4,128,128]{2,1,0:T(8,128)(2,1)}, bf16[4,128,128]{2,1,0:T(8,128)(2,1)S(1)}, u32[]{:S(2)}, u32[]{:S(2)}) collective-permute-start(bf16[4,128,128]{2,1,0:T(8,128)(2,1)} %get-tuple-element.39), channel_id=1, source_target_pairs={{0,2},{1,3},{2,0},{3,1},{4,6},{5,7},{6,4},{7,5},{8,10},{9,11},{10,... | collective-permute-start | bytes 393224 | tf_op jit(solution)/shard_map/ppermute | solution.py:31
  53.2 17.7 %collective-permute-start.8 = (bf16[4,128,128]{2,1,0:T(8,128)(2,1)}, bf16[4,128,128]{2,1,0:T(8,128)(2,1)S(1)}, u32[]{:S(2)}, u32[]{:S(2)}) collective-permute-start(bf16[4,128,128]{2,1,0:T(8,128)(2,1)} %get-tuple-element.40), channel_id=1, source_target_pairs={{0,254},{1,255},{2,4},{3,5},{4,2},{5,3},{6,8},{7,9},{8,6},{9,7},{1... | collective-permute-start | bytes 393224 | tf_op jit(solution)/shard_map/ppermute | solution.py:31
  60.1 21.0 %all-to-all-start.1 = ((bf16[128,8,128]{2,1,0:T(8,128)(2,1)}), bf16[128,8,128]{2,1,0:T(8,128)(2,1)S(1)}, u32[]{:S(2)}, u32[]{:S(2)}) async-start(bf16[128,8,128]{2,1,0:T(8,128)(2,1)} %add_pieces.1), calls=%async_computation.1 | async-start | bytes 524288 | tf_op jit(solution)/shard_map/all_to_all | solution.py:650

commit v6 on v5

--- a/solution.py
+++ b/solution.py
@@ -17,9 +17,14 @@
 STEP = 8
 
 
+QUAD = 4
+
+
 def partner(i, way, n):
     if way == 0:
         return i ^ 1
+    if way == 4:
+        return i ^ 3
     if way == 1:
         return (i + (1 if i & 1 else -1)) % n
     ahead = (i >> 1) & 1 == way - 2
@@ -35,6 +40,13 @@
     me = lax.axis_index("dom")
     odd, odd_chip = me & 1, (me >> 1) & 1
     return odd, 1 - odd, 2 + odd_chip, 3 - odd_chip
+
+
+SHARING = (0, 2, 4)
+
+
+def same_place(n):
+    return [list(range(c, n, QUAD)) for c in range(QUAD)]
 
 
 def rows_of(chunk, size):
@@ -208,26 +220,34 @@
     lists = len(OFFSETS)
     tiles_hbm, rows_hbm, agg_hbm, d_hbm = refs[:4]
     halos, refs = refs[4 : 4 + lists], refs[4 + lists :]
-    hub, self_hbm, neigh_hbm, bias_hbm, hidden_hbm, d_pre_out, d_agg_hbm = refs[:7]
-    backs, refs = refs[7 : 7 + lists], refs[7 + lists :]
-    mine, theirs, src, weights, bias, table, rem_grad, backs_out, w_grad, b_grad = refs[:10]
-    spread, pack_out, tiles, rows, agg_local, d_hidden, hidden, d_agg_out = refs[10:18]
-    sem_t, sem_back, sem_in, sem_out = refs[18:]
+    hubs, refs = refs[:QUAD], refs[QUAD:]
+    self_hbm, neigh_hbm, bias_hbm, hidden_hbm, d_pre_out, d_agg_hbm = refs[:6]
+    backs, mine, refs = refs[6 : 6 + lists], refs[6 + lists], refs[7 + lists :]
+    theirs, refs = refs[: QUAD - 1], refs[QUAD - 1 :]
+    hubs_in, hubs_f32, hub_rows = refs[:3]
+    refs = refs[3:]
+    src, weights, bias, table, rem_grad, backs_out, w_grad, b_grad = refs[:8]
+    w_self_grad, w_neigh_grad, b_rows = refs[8:11]
+    refs = refs[11:]
+    spread, pack_out, tiles, rows, agg_local, d_hidden, hidden, d_agg_out = refs[:8]
+    sem_t, sem_back, sem_in, sem_out = refs[8:]
     count, per_block, tile, _ = tiles.shape
     width = rows.shape[-1]
     per_list = halos[0].shape[0]
     halo_count = lists * per_list
-    hub_blocks = hub.shape[0]
+    hub_blocks = table.shape[0] - halo_count
+    place = lax.axis_index("dom") % QUAD
     slots = [j ^ 1 for j in lists_of_ways()]
     pairs = [
         (src_hbm, src),
-        (hub, table.at[pl.ds(halo_count, hub_blocks)]),
         (self_hbm, weights.at[pl.ds(0, width)]),
         (neigh_hbm, weights.at[pl.ds(width, width)]),
         (bias_hbm, bias),
     ]
     for w, s in enumerate(slots):
         pairs.append((halos[w], table.at[pl.ds(s * per_list, per_list)]))
+    for x in range(QUAD):
+        pairs.append((hubs[x], hubs_in.at[place ^ x]))
     moves = [pltpu.make_async_copy(*p, sem_t.at[n]) for n, p in enumerate(pairs)]
     chunks = count // STEP
 
@@ -256,6 +276,16 @@
     w_grad[...] = jnp.zeros_like(w_grad)
     b_grad[...] = jnp.zeros_like(b_grad)
     wait(moves)
+    parts = QUAD * mine.shape[0]
+    owned = hub_blocks * tile // parts
+    each = parts // QUAD
+    for c in range(QUAD):
+        hubs_f32[...] = hubs_in[c].astype(F32)
+        for r in range(owned):
+            hub_rows[pl.ds(c * owned + r, each, stride=QUAD * owned), :] = hubs_f32[
+                pl.ds(r, each, stride=owned), :
+            ]
+    table[halo_count:] = hub_rows[...].reshape(hub_blocks, tile, width).astype(BF16)
 
     @pl.loop(0, chunks)
     def _(i):
@@ -299,43 +329,49 @@
         backs_out[w] = rem_grad[pl.ds(s * per_list, per_list)].astype(BF16)
         sent.append(pltpu.make_async_copy(backs_out.at[w], backs[w], sem_back.at[w]))
     start(sent)
-    half, chunk, _ = mine.shape
-    parts = 2 * half
-    owned = hub_blocks * tile // parts
-    hub_rows = jnp.concatenate(
-        [jnp.transpose(rem_grad[halo_count + q]) for q in range(hub_blocks)], 0
-    )
-    split = hub_rows.reshape(parts, owned, width)
-    for i in range(owned):
-        spread[pl.ds(i, parts, stride=chunk), :] = split[:, i, :]
-    spread[pl.ds(owned, parts, stride=chunk), :] = w_grad[:, :width]
-    spread[pl.ds(owned + 1, parts, stride=chunk), :] = w_grad[:, width:]
+    chunk = mine.shape[1]
+    w_self_grad[...] = w_grad[:, :width]
+    w_neigh_grad[...] = w_grad[:, width:]
+    for q in range(hub_blocks):
+        hub_rows[q * tile : (q + 1) * tile, :] = jnp.transpose(rem_grad[halo_count + q])
     total = jnp.sum(b_grad[...], 0, keepdims=True)
     high = total.astype(BF16).astype(F32)
     lane = lax.broadcasted_iota(jnp.int32, (width, parts), 0)
     two = jnp.where(lane == 0, high, jnp.where(lane == 1, total - high, 0.0))
-    spread[pl.ds(owned + 2, parts, stride=chunk), :] = jnp.transpose(two)
-    for i in range(owned + 3, chunk):
-        spread[pl.ds(i, parts, stride=chunk), :] = jnp.zeros((parts, width), F32)
-    by_core = spread[...].reshape(half, 2, chunk, width)
-    odd = lists_of_ways()[0] == 1
-    pack_out[...] = jnp.where(odd, by_core[:, 0], by_core[:, 1]).astype(BF16)
-    last = pltpu.make_async_copy(pack_out, theirs, sem_back.at[lists])
-    last.start()
-    mine[...] = jnp.where(odd, by_core[:, 1], by_core[:, 0])
+    b_rows[...] = jnp.transpose(two)
+    for c in range(QUAD):
+        base = c * each * chunk
+        for i in range(owned):
+            spread[pl.ds(base + i, each, stride=chunk), :] = hub_rows[
+                pl.ds(c * owned + i, each, stride=QUAD * owned), :
+            ]
+        every = pl.ds(c, each, stride=QUAD)
+        spread[pl.ds(base + owned, each, stride=chunk), :] = w_self_grad[every, :]
+        spread[pl.ds(base + owned + 1, each, stride=chunk), :] = w_neigh_grad[every, :]
+        spread[pl.ds(base + owned + 2, each, stride=chunk), :] = b_rows[every, :]
+        for i in range(owned + 3, chunk):
+            spread[pl.ds(base + i, each, stride=chunk), :] = jnp.zeros((each, width), F32)
+    for x in range(1, QUAD):
+        part = spread[rows_of(place ^ x, each * chunk), :].reshape(each, chunk, width)
+        pack_out[x - 1] = part.astype(BF16)
+        sent.append(
+            pltpu.make_async_copy(pack_out.at[x - 1], theirs[x - 1], sem_back.at[lists + x - 1])
+        )
+        sent[-1].start()
+    mine[...] = spread[rows_of(place, each * chunk), :].reshape(each, chunk, width)
     wait(sent)
     for i in range(chunks):
         wait(store(i))
-    last.wait()
-
-
-def layer(src, tiles, rows, agg_local, halos, hub, w_self, w_neigh, bias, d_hidden, parts):
+
+
+def layer(src, tiles, rows, agg_local, halos, hubs, w_self, w_neigh, bias, d_hidden, parts):
     count, per_block, tile, _ = tiles.shape
     nodes, width = rows.shape
     units = d_hidden.shape[-1]
     lists, per_list = len(halos), halos[0].shape[0]
-    table = lists * per_list + hub.shape[0]
-    pieces = (parts // 2, CHUNK, width)
+    hub_total = QUAD * hubs[0].shape[0]
+    table = lists * per_list + hub_total // tile
+    pieces = (parts // QUAD, CHUNK, width)
     chunks = count // STEP
     return pl.pallas_call(
         layer_kernel,
@@ -345,10 +381,17 @@
             pltpu.HBM((count, width, tile), BF16),
         ]
         + [pltpu.HBM((per_list, width, tile), BF16)] * lists
-        + [pltpu.VMEM(pieces, F32), pltpu.HBM(pieces, BF16)],
-        in_specs=[HBM_SPEC] * 5 + [ANY_SPEC] * (lists + 1) + [HBM_SPEC] * 3,
-        out_specs=[HBM_SPEC, VMEM_SPEC] + [HBM_SPEC] * (lists + 1) + [VMEM_SPEC, HBM_SPEC],
+        + [pltpu.VMEM(pieces, F32)]
+        + [pltpu.HBM(pieces, BF16)] * (QUAD - 1),
+        in_specs=[HBM_SPEC] * 5 + [ANY_SPEC] * (lists + QUAD) + [HBM_SPEC] * 3,
+        out_specs=[HBM_SPEC, VMEM_SPEC]
+        + [HBM_SPEC] * (lists + 1)
+        + [VMEM_SPEC]
+        + [HBM_SPEC] * (QUAD - 1),
         scratch_shapes=[
+            pltpu.VMEM((QUAD,) + hubs[0].shape, BF16),
+            pltpu.VMEM(hubs[0].shape, F32),
+            pltpu.VMEM((hub_total, width), F32),
             pltpu.SMEM(src.shape, jnp.int32),
             pltpu.VMEM((2 * width, units), BF16),
             pltpu.VMEM((1, units), F32),
@@ -357,16 +400,19 @@
             pltpu.VMEM((lists, per_list, width, tile), BF16),
             pltpu.VMEM((units, 2 * width), F32),
             pltpu.VMEM((8, units), F32),
+            pltpu.VMEM((units, width), F32),
+            pltpu.VMEM((units, width), F32),
+            pltpu.VMEM((units, width), F32),
             pltpu.VMEM((parts * CHUNK, width), F32),
-            pltpu.VMEM(pieces, BF16),
+            pltpu.VMEM((QUAD - 1,) + pieces, BF16),
             pltpu.VMEM(tiles.shape, BF16),
             pltpu.VMEM((nodes, width), BF16),
             pltpu.VMEM((nodes, width), F32),
             pltpu.VMEM((nodes, units), BF16),
             pltpu.VMEM((nodes, units), BF16),
             pltpu.VMEM((count, width, tile), BF16),
-            pltpu.SemaphoreType.DMA((lists + 5,)),
-            pltpu.SemaphoreType.DMA((lists + 1,)),
+            pltpu.SemaphoreType.DMA((lists + 4 + QUAD,)),
+            pltpu.SemaphoreType.DMA((lists + QUAD - 1,)),
             pltpu.SemaphoreType.DMA((chunks, 4)),
             pltpu.SemaphoreType.DMA((chunks, 2)),
         ],
@@ -384,19 +430,25 @@
         hbm(agg_local),
         hbm(d_hidden),
         *halos,
-        hub,
+        *hubs,
         hbm(w_self),
         hbm(w_neigh),
         hbm(bias),
     )
 
 
-def add_kernel(mine, theirs_any, out_hbm, theirs, out, sems):
-    load = pltpu.make_async_copy(theirs_any, theirs, sems.at[0])
-    load.start()
-    load.wait()
-    out[...] = (mine[...] + theirs[...].astype(F32)).astype(BF16)
-    save = pltpu.make_async_copy(out, out_hbm, sems.at[1])
+def add_kernel(mine, *refs):
+    theirs_any, (out_hbm, theirs, out, sems, sem_out) = refs[: QUAD - 1], refs[QUAD - 1 :]
+    loads = [
+        pltpu.make_async_copy(t, theirs.at[x], sems.at[x]) for x, t in enumerate(theirs_any)
+    ]
+    start(loads)
+    wait(loads)
+    total = mine[...]
+    for x in range(QUAD - 1):
+        total = total + theirs[x].astype(F32)
+    out[...] = total.astype(BF16)
+    save = pltpu.make_async_copy(out, out_hbm, sem_out)
     save.start()
     save.wait()
 
@@ -404,17 +456,18 @@
 def add_pieces(mine, theirs):
     return pl.pallas_call(
         add_kernel,
-        out_shape=pltpu.HBM(theirs.shape, BF16),
-        in_specs=[VMEM_SPEC, ANY_SPEC],
+        out_shape=pltpu.HBM(mine.shape, BF16),
+        in_specs=[VMEM_SPEC] + [ANY_SPEC] * (QUAD - 1),
         out_specs=HBM_SPEC,
         scratch_shapes=[
-            pltpu.VMEM(theirs.shape, BF16),
-            pltpu.VMEM(theirs.shape, BF16),
-            pltpu.SemaphoreType.DMA((2,)),
+            pltpu.VMEM((QUAD - 1,) + mine.shape, BF16),
+            pltpu.VMEM(mine.shape, BF16),
+            pltpu.SemaphoreType.DMA((QUAD - 1,)),
+            pltpu.SemaphoreType.DMA,
         ],
         compiler_params=params(),
         name="add_pieces",
-    )(vmem(mine), theirs)
+    )(vmem(mine), *theirs)
 
 
 def back_kernel(
@@ -625,11 +678,13 @@
     parts = lax.axis_size("dom")
     nodes, width = features.shape
     tile = local_tiles.shape[-1]
-    owned = hub_rows.shape[0]
     blocks = features.reshape(nodes // tile, tile, width)
     *sends, hub_mine, own = gather_sends(send_blocks, hub_rows, blocks, parts)
     halos = [swapped(b, way) for way, b in enumerate(sends)]
-    hub_all = lax.all_to_all(spread_hubs(vmem(hub_mine), halos[0], parts), "dom", 0, 0)
+    groups = same_place(parts)
+    spread = spread_hubs(vmem(hub_mine), halos[0], parts // QUAD)
+    hub_quarter = lax.all_to_all(spread, "dom", 0, 0, axis_index_groups=groups)
+    hub_quarter = hub_quarter.reshape(-1, width)
     agg_local = local_aggregate(local_src.T, local_tiles, own)
     hidden, d_pre, d_agg, *rest = layer(
         remote_src.T,
@@ -637,17 +692,16 @@
         features,
         agg_local,
         halos,
-        hub_all.reshape(parts * owned // tile, tile, width),
+        [hub_quarter] + [swapped(hub_quarter, way) for way in SHARING],
         w_self,
         w_neigh,
         bias[None],
         d_hidden,
         parts,
     )
-    *backs, mine, theirs = rest
-    packed = add_pieces(mine, swapped(theirs, 0))
-    same_core = [list(range(c, parts, 2)) for c in range(2)]
-    pieces = lax.all_to_all(packed, "dom", 0, 0, axis_index_groups=same_core)
+    backs, mine, theirs = rest[: len(OFFSETS)], rest[len(OFFSETS)], rest[len(OFFSETS) + 1 :]
+    packed = add_pieces(mine, [swapped(x, way) for x, way in zip(theirs, SHARING)])
+    pieces = lax.all_to_all(packed, "dom", 0, 0, axis_index_groups=groups)
     returned = [swapped(b, way) for way, b in enumerate(backs)]
     grad_t = local_backward(local_src.T, local_tiles, d_pre, d_agg, w_self)
     rough, near = collect(send_blocks, hub_rows, grad_t, returned)

time: 83.5 us -> 80.5 us (0.964); the launches traced: 83.2 us -> 78.9 us
  waiting for transfers between devices: 20.6 us -> 12.1 us
  starting transfers between devices: 35.6 us -> 39.2 us
    all_to_all x2, waiting for transfers between devices: 20.6 us -> 8.45 us  [the longest x1 5.42 us: shards(): pieces = lax.all_to_all(packed, 'dom', 0, 0, axis_index_groups=groups)]
    ppermute x9 -> x14, waiting for transfers between devices: 0.02 us -> 3.62 us  [swapped(): lax.ppermute(block, 'dom', [(i, partner(i, way, n)) for i in range(n)])]
    all_to_all x2, starting transfers between devices: 14.4 us -> 17.2 us  [the longest x1 12.6 us: shards(): hub_quarter = lax.all_to_all(spread, 'dom', 0, 0, axis_index_groups=groups)]
    ppermute x9 -> x14, starting transfers between devices: 21.2 us -> 22 us  [swapped(): lax.ppermute(block, 'dom', [(i, partner(i, way, n)) for i in range(n)])]
  transfers between devices with their start and end apart: 11 -> 16, of which waited for: 2 -> 4; matrix products, arithmetic and copies ran while one was open for 0% -> 0% of each run, Pallas kernels for 14% -> 15%
where the time goes in v6:
time: 80.5 us; the launch traced here: 78.9 us
  starting transfers between devices  39.2 us (49%)
  Pallas kernels  26.9 us (33%)
  waiting for transfers between devices  12.1 us (15%)
    ppermute x14, starting transfers between devices, swapped(): lax.ppermute(block, 'dom', [(i, partner(i, way, n)) for i in range(n)])  22 us
    all_to_all x1, starting transfers between devices, shards(): hub_quarter = lax.all_to_all(spread, 'dom', 0, 0, axis_index_groups=groups)  12.6 us
    pallas_call x1, Pallas kernels, layer(): pl.pallas_call(layer_kernel, out_shape=[pltpu.HBM((nodes, units), BF16),...  10.8 us
    all_to_all x1, waiting for transfers between devices, shards(): pieces = lax.all_to_all(packed, 'dom', 0, 0, axis_index_groups=groups)  5.42 us
    all_to_all x1, starting transfers between devices, shards(): pieces = lax.all_to_all(packed, 'dom', 0, 0, axis_index_groups=groups)  4.6 us
    pallas_call x1, Pallas kernels, local_backward(): pl.pallas_call(back_kernel, out_shape=pltpu.VMEM((count, width, tile), F3...  4.55 us
    ppermute x14, waiting for transfers between devices, swapped(): lax.ppermute(block, 'dom', [(i, partner(i, way, n)) for i in range(n)])  3.62 us
    pallas_call x1, Pallas kernels, local_aggregate(): pl.pallas_call(local_kernel, out_shape=pltpu.HBM(agg, F32), in_specs=[HBM...  3.5 us
  transfers between devices with their start and end apart: 16, of which 4 were waited for; matrix products, arithmetic and copies ran while one was open for 0% of the time, Pallas kernels for 15%

profile of v6, /device:TPU:1, one launch (start us, length us, event | category | flops | bytes accessed | tf_op | source)
XLA Modules:
  0.0 78.9 jit_solution(17388795251433982157)
XLA Ops:
  0.6 2.1 %sends.1 = (bf16[4,128,128]{2,1,0:T(8,128)(2,1)}, bf16[4,128,128]{2,1,0:T(8,128)(2,1)}, bf16[4,128,128]{2,1,0:T(8,128)(2,1)}, bf16[4,128,128]{2,1,0:T(8,128)(2,1...) custom-call(s32[4,4]{1,0:T(4,128)} %send_hbm.3, s32[4]{0:T(128)} %hubs_hbm.5, bf16[32,128,128]{2,1,0:T(8,128)(2,1)} %bitcast.13), custom_call_target="tpu_custom_call" | custom-call | tf_op jit(solution)/shard_map/sends/pallas_call | solution.py:139
  2.8 3.3 %collective-permute-start = (bf16[4,128,128]{2,1,0:T(8,128)(2,1)}, bf16[4,128,128]{2,1,0:T(8,128)(2,1)S(1)}, u32[]{:S(2)}, u32[]{:S(2)}) collective-permute-start(bf16[4,128,128]{2,1,0:T(8,128)(2,1)} %get-tuple-element.29), channel_id=1, source_target_pairs={{0,1},{1,0},{2,3},{3,2},{4,5},{5,4},{6,7},{7,6},{8,9},{9,8},{10,11... | collective-permute-start | bytes 393224 | tf_op jit(solution)/shard_map/ppermute | solution.py:36
  6.1 1.2 %collective-permute-done._.refs_4_ = bf16[4,128,128]{2,1,0:T(8,128)(2,1)S(1)} collective-permute-done((bf16[4,128,128]{2,1,0:T(8,128)(2,1)}, bf16[4,128,128]{2,1,0:T(8,128)(2,1)S(1)}, u32[]{:S(2)}, u32[]{:S(2)}) %collective-permute-start) | collective-permute-done | bytes 131104 | tf_op jit(solution)/shard_map/ppermute | solution.py:36
  7.3 0.6 spread_hubs.1
  8.0 12.6 %all-to-all-start = ((bf16[64,4,128]{2,1,0:T(4,128)(2,1)}), bf16[64,4,128]{2,1,0:T(4,128)(2,1)S(1)}, u32[]{:S(2)}, u32[]{:S(2)}) async-start(bf16[64,4,128]{2,1,0:T(4,128)(2,1)} %spread_hubs.1), calls=%async_computation | async-start | bytes 131072 | tf_op jit(solution)/shard_map/all_to_all | solution.py:686
  20.5 0.8 %collective-permute-start.2 = (bf16[4,128,128]{2,1,0:T(8,128)(2,1)}, bf16[4,128,128]{2,1,0:T(8,128)(2,1)S(1)}, u32[]{:S(2)}, u32[]{:S(2)}) collective-permute-start(bf16[4,128,128]{2,1,0:T(8,128)(2,1)} %get-tuple-element.31), channel_id=1, source_target_pairs={{0,2},{1,3},{2,0},{3,1},{4,6},{5,7},{6,4},{7,5},{8,10},{9,11},{10,... | collective-permute-start | bytes 393224 | tf_op jit(solution)/shard_map/ppermute | solution.py:36
  21.3 7.2 %collective-permute-start.3 = (bf16[4,128,128]{2,1,0:T(8,128)(2,1)}, bf16[4,128,128]{2,1,0:T(8,128)(2,1)S(1)}, u32[]{:S(2)}, u32[]{:S(2)}) collective-permute-start(bf16[4,128,128]{2,1,0:T(8,128)(2,1)} %get-tuple-element.32), channel_id=1, source_target_pairs={{0,254},{1,255},{2,4},{3,5},{4,2},{5,3},{6,8},{7,9},{8,6},{9,7},{1... | collective-permute-start | bytes 393224 | tf_op jit(solution)/shard_map/ppermute | solution.py:36
  28.5 3.0 %all-to-all-done = bf16[64,4,128]{2,1,0:T(4,128)(2,1)S(1)} async-done(((bf16[64,4,128]{2,1,0:T(4,128)(2,1)}), bf16[64,4,128]{2,1,0:T(4,128)(2,1)S(1)}, u32[]{:S(2)}, u32[]{:S(2)}) %all-to-all-start) | async-done | bytes 65568 | tf_op jit(solution)/shard_map/all_to_all | solution.py:686
  31.6 2.6 %collective-permute-start.6 = (bf16[256,128]{1,0:T(8,128)(2,1)S(1)}, bf16[256,128]{1,0:T(8,128)(2,1)S(1)}, u32[]{:S(2)}, u32[]{:S(2)}) collective-permute-start(bf16[256,128]{1,0:T(8,128)(2,1)S(1)} %bitcast.9), channel_id=1, source_target_pairs={{0,3},{1,2},{2,1},{3,0},{4,7},{5,6},{6,5},{7,4},{8,11},{9,10},{10,... | collective-permute-start | bytes 196616 | tf_op jit(solution)/shard_map/ppermute | solution.py:36
  34.2 0.7 collective-permute-start.5
  35.0 3.5 %local_aggregate.1.refs_2_ = f32[4096,128]{1,0:T(8,128)} custom-call(s32[3,32]{1,0:T(4,128)} %bitcast.16, bf16[32,3,128,128]{3,2,1,0:T(8,128)(2,1)} %tiles_hbm.3, bf16[32,128,128]{2,1,0:T(8,128)(2,1)S(1)} %get-tuple-element.28.blocks), custom_call_target="tpu_custom_call" | custom-call | flops 10000000000 | bytes 67108864 | tf_op jit(solution)/shard_map/local_aggregate/pallas_call | solution.py:198
  38.5 10.8 %layer.1 = (bf16[4096,256]{1,0:T(8,128)(2,1)}, bf16[4096,256]{1,0:T(8,128)(2,1)S(1)}, bf16[32,128,128]{2,1,0:T(8,128)(2,1)}, bf16[4,128,128]{2,1,0:T(8,128)(2,1)...) custom-call(s32[3,32]{1,0:T(4,128)} %bitcast.14, ...), custom_call_target="tpu_custom_call" | custom-call | flops 2415919104 | bytes 14680064 | tf_op jit(solution)/shard_map/layer/pallas_call | solution.py:376
  49.3 0.6 collective-permute-start.7
  49.9 0.8 collective-permute-start.8
  50.7 1.0 %collective-permute-start.9 = (bf16[64,8,128]{2,1,0:T(8,128)(2,1)}, bf16[64,8,128]{2,1,0:T(8,128)(2,1)S(1)}, u32[]{:S(2)}, u32[]{:S(2)}) collective-permute-start(bf16[64,8,128]{2,1,0:T(8,128)(2,1)} %get-tuple-element.38), channel_id=1, source_target_pairs={{0,3},{1,2},{2,1},{3,0},{4,7},{5,6},{6,5},{7,4},{8,11},{9,10},{10,... | collective-permute-start | bytes 393224 | tf_op jit(solution)/shard_map/ppermute | solution.py:36
  51.8 1.0 %collective-permute-start.11 = (bf16[4,128,128]{2,1,0:T(8,128)(2,1)}, bf16[4,128,128]{2,1,0:T(8,128)(2,1)S(1)}, u32[]{:S(2)}, u32[]{:S(2)}) collective-permute-start(bf16[4,128,128]{2,1,0:T(8,128)(2,1)} %get-tuple-element.42), channel_id=1, source_target_pairs={{0,255},{1,2},{2,1},{3,4},{4,3},{5,6},{6,5},{7,8},{8,7},{9,10},{10... | collective-permute-start | bytes 393224 | tf_op jit(solution)/shard_map/ppermute | solution.py:36
  52.8 2.4 %collective-permute-done.8.refs_1_ = bf16[64,8,128]{2,1,0:T(8,128)(2,1)S(1)} collective-permute-done((bf16[64,8,128]{2,1,0:T(8,128)(2,1)}, bf16[64,8,128]{2,1,0:T(8,128)(2,1)S(1)}, u32[]{:S(2)}, u32[]{:S(2)}) %collective-permute-start.8) | collective-permute-done | bytes 131104 | tf_op jit(solution)/shard_map/ppermute | solution.py:36
  55.2 3.9 %collective-permute-start.13 = (bf16[4,128,128]{2,1,0:T(8,128)(2,1)}, bf16[4,128,128]{2,1,0:T(8,128)(2,1)S(1)}, u32[]{:S(2)}, u32[]{:S(2)}) collective-permute-start(bf16[4,128,128]{2,1,0:T(8,128)(2,1)} %get-tuple-element.44), channel_id=1, source_target_pairs={{0,254},{1,255},{2,4},{3,5},{4,2},{5,3},{6,8},{7,9},{8,6},{9,7},{1... | collective-permute-start | bytes 393224 | tf_op jit(solution)/shard_map/ppermute | solution.py:36
  59.1 1.2 %add_pieces.1 = bf16[64,8,128]{2,1,0:T(8,128)(2,1)} custom-call(f32[64,8,128]{2,1,0:T(8,128)S(1)} %get-tuple-element.35.mine, bf16[64,8,128]{2,1,0:T(8,128)(2,1)S(1)} %collective-permute-done.7.refs_0_, bf16[64,8,128]{2,1,0:T(8,128)(2,1)S(1)} %collective-permute-done.8.refs_1_, bf16[64,8,128]{2,1,0:T(8,128)(2,1)S(1)} %collective-permute-done.9.refs_2_), custom_call_target="tpu_custom_call" | custom-call | tf_op jit(solution)/shard_map/add_pieces/pallas_call | solution.py:457
  60.3 4.6 %all-to-all-start.1 = ((bf16[64,8,128]{2,1,0:T(8,128)(2,1)}), bf16[64,8,128]{2,1,0:T(8,128)(2,1)S(1)}, u32[]{:S(2)}, u32[]{:S(2)}) async-start(bf16[64,8,128]{2,1,0:T(8,128)(2,1)} %add_pieces.1), calls=%async_computation.1 | async-start | bytes 262144 | tf_op jit(solution)/shard_map/all_to_all | solution.py:704
  64.9 4.5 %local_backward.1._ = f32[32,128,128]{2,1,0:T(8,128)S(1)} custom-call(s32[3,32]{1,0:T(4,128)} %bitcast.17, bf16[128,256]{1,0:T(8,128)(2,1)} %weight_hbm.1, bf16[32,3,128,128]{3,2,1,0:T(8,128)(2,1)} %tiles_hbm.3, bf16[32,128,128]{2,1,0:T(8,128)(2,1)} %get-tuple-element.39.d_hbm, bf16[4096,256]{1,0:T(8,128)(2,1)S(1)} %get-tuple-element.40.d_pre), custom_call_target="tpu_custom_call" | custom-call | flops 10000000000 | bytes 67108864 | tf_op jit(solution)/shard_map/local_backward/pallas_call | solution.py:513
  69.5 2.0 %collect.1 = (f32[32,128,128]{2,1,0:T(8,128)S(1)}, bf16[4096,128]{1,0:T(8,128)(2,1)}, f32[4,16,128]{2,1,0:T(8,128)S(1)}) custom-call(s32[4,4]{1,0:T(4,128)} %send_hbm.3, s32[4]{0:T(128)} %hubs_hbm.5, f32[32,128,128]{2,1,0:T(8,128)S(1)} %local_backward.1._, bf16[4,128,128]{2,1,0:T(8,128)(2,1)S(1)} %collective-permute-done.10.refs_0_, ...), custom_call_target="tpu_custom_call", output_to_operand_aliasing={{0}: (2, {})} | custom-call | flops 4194304 | bytes 4194304 | tf_op jit(solution)/shard_map/collect/pallas_call | solution.py:571
  71.5 5.4 %all-to-all-done.1.pieces_hbm = bf16[64,8,128]{2,1,0:T(8,128)(2,1)S(1)} async-done(((bf16[64,8,128]{2,1,0:T(8,128)(2,1)}), bf16[64,8,128]{2,1,0:T(8,128)(2,1)S(1)}, u32[]{:S(2)}, u32[]{:S(2)}) %all-to-all-start.1) | async-done | bytes 131104 | tf_op jit(solution)/shard_map/all_to_all | solution.py:704
  77.0 2.0 %finish.1 = (bf16[4096,128]{1,0:T(8,128)(2,1)}, f32[1,128]{1,0:T(1,128)}, f32[1,128]{1,0:T(1,128)}, f32[1,128]{1,0:T(1,128)}) custom-call(s32[4]{0:T(128)} %hubs_hbm.5, bf16[64,8,128]{2,1,0:T(8,128)(2,1)S(1)} %all-to-all-done.1.pieces_hbm, f32[4,16,128]{2,1,0:T(8,128)S(1)} %get-tuple-element.45.near, ...), custom_call_target="tpu_custom_call", output_to_operand_aliasing={{0}: (3, {})} | custom-call | tf_op jit(solution)/shard_map/finish/pallas_call | solution.py:647
  (16 shorter events, 0.2 us)
Async XLA Ops:
  2.8 4.5 %collective-permute-start = (bf16[4,128,128]{2,1,0:T(8,128)(2,1)}, bf16[4,128,128]{2,1,0:T(8,128)(2,1)S(1)}, u32[]{:S(2)}, u32[]{:S(2)}) collective-permute-start(bf16[4,128,128]{2,1,0:T(8,128)(2,1)} %get-tuple-element.29), channel_id=1, source_target_pairs={{0,1},{1,0},{2,3},{3,2},{4,5},{5,4},{6,7},{7,6},{8,9},{9,8},{10,11... | collective-permute-start | bytes 393224 | tf_op jit(solution)/shard_map/ppermute | solution.py:36
  6.1 28.8 %collective-permute-start.1 = (bf16[4,128,128]{2,1,0:T(8,128)(2,1)}, bf16[4,128,128]{2,1,0:T(8,128)(2,1)S(1)}, u32[]{:S(2)}, u32[]{:S(2)}) collective-permute-start(bf16[4,128,128]{2,1,0:T(8,128)(2,1)} %get-tuple-element.30), channel_id=1, source_target_pairs={{0,255},{1,2},{2,1},{3,4},{4,3},{5,6},{6,5},{7,8},{8,7},{9,10},{10... | collective-permute-start | bytes 393224 | tf_op jit(solution)/shard_map/ppermute | solution.py:36
  8.0 23.6 %all-to-all-start = ((bf16[64,4,128]{2,1,0:T(4,128)(2,1)}), bf16[64,4,128]{2,1,0:T(4,128)(2,1)S(1)}, u32[]{:S(2)}, u32[]{:S(2)}) async-start(bf16[64,4,128]{2,1,0:T(4,128)(2,1)} %spread_hubs.1), calls=%async_computation | async-start | bytes 131072 | tf_op jit(solution)/shard_map/all_to_all | solution.py:686
  20.5 18.0 %collective-permute-start.2 = (bf16[4,128,128]{2,1,0:T(8,128)(2,1)}, bf16[4,128,128]{2,1,0:T(8,128)(2,1)S(1)}, u32[]{:S(2)}, u32[]{:S(2)}) collective-permute-start(bf16[4,128,128]{2,1,0:T(8,128)(2,1)} %get-tuple-element.31), channel_id=1, source_target_pairs={{0,2},{1,3},{2,0},{3,1},{4,6},{5,7},{6,4},{7,5},{8,10},{9,11},{10,... | collective-permute-start | bytes 393224 | tf_op jit(solution)/shard_map/ppermute | solution.py:36
  21.3 17.1 %collective-permute-start.3 = (bf16[4,128,128]{2,1,0:T(8,128)(2,1)}, bf16[4,128,128]{2,1,0:T(8,128)(2,1)S(1)}, u32[]{:S(2)}, u32[]{:S(2)}) collective-permute-start(bf16[4,128,128]{2,1,0:T(8,128)(2,1)} %get-tuple-element.32), channel_id=1, source_target_pairs={{0,254},{1,255},{2,4},{3,5},{4,2},{5,3},{6,8},{7,9},{8,6},{9,7},{1... | collective-permute-start | bytes 393224 | tf_op jit(solution)/shard_map/ppermute | solution.py:36
  31.6 6.9 %collective-permute-start.6 = (bf16[256,128]{1,0:T(8,128)(2,1)S(1)}, bf16[256,128]{1,0:T(8,128)(2,1)S(1)}, u32[]{:S(2)}, u32[]{:S(2)}) collective-permute-start(bf16[256,128]{1,0:T(8,128)(2,1)S(1)} %bitcast.9), channel_id=1, source_target_pairs={{0,3},{1,2},{2,1},{3,0},{4,7},{5,6},{6,5},{7,4},{8,11},{9,10},{10,... | collective-permute-start | bytes 196616 | tf_op jit(solution)/shard_map/ppermute | solution.py:36
  34.2 4.3 %collective-permute-start.5 = (bf16[256,128]{1,0:T(8,128)(2,1)S(1)}, bf16[256,128]{1,0:T(8,128)(2,1)S(1)}, u32[]{:S(2)}, u32[]{:S(2)}) collective-permute-start(bf16[256,128]{1,0:T(8,128)(2,1)S(1)} %bitcast.10), channel_id=1, source_target_pairs={{0,2},{1,3},{2,0},{3,1},{4,6},{5,7},{6,4},{7,5},{8,10},{9,11},{10,... | collective-permute-start | bytes 196616 | tf_op jit(solution)/shard_map/ppermute | solution.py:36
  35.0 3.6 %collective-permute-start.4 = (bf16[256,128]{1,0:T(8,128)(2,1)S(1)}, bf16[256,128]{1,0:T(8,128)(2,1)S(1)}, u32[]{:S(2)}, u32[]{:S(2)}) collective-permute-start(bf16[256,128]{1,0:T(8,128)(2,1)S(1)} %bitcast.11), channel_id=1, source_target_pairs={{0,1},{1,0},{2,3},{3,2},{4,5},{5,4},{6,7},{7,6},{8,9},{9,8},{10,11... | collective-permute-start | bytes 196616 | tf_op jit(solution)/shard_map/ppermute | solution.py:36
  49.3 3.5 %collective-permute-start.7 = (bf16[64,8,128]{2,1,0:T(8,128)(2,1)}, bf16[64,8,128]{2,1,0:T(8,128)(2,1)S(1)}, u32[]{:S(2)}, u32[]{:S(2)}) collective-permute-start(bf16[64,8,128]{2,1,0:T(8,128)(2,1)} %get-tuple-element.36), channel_id=1, source_target_pairs={{0,1},{1,0},{2,3},{3,2},{4,5},{5,4},{6,7},{7,6},{8,9},{9,8},{10,11... | collective-permute-start | bytes 393224 | tf_op jit(solution)/shard_map/ppermute | solution.py:36
  49.9 5.3 %collective-permute-start.8 = (bf16[64,8,128]{2,1,0:T(8,128)(2,1)}, bf16[64,8,128]{2,1,0:T(8,128)(2,1)S(1)}, u32[]{:S(2)}, u32[]{:S(2)}) collective-permute-start(bf16[64,8,128]{2,1,0:T(8,128)(2,1)} %get-tuple-element.37), channel_id=1, source_target_pairs={{0,2},{1,3},{2,0},{3,1},{4,6},{5,7},{6,4},{7,5},{8,10},{9,11},{10,... | collective-permute-start | bytes 393224 | tf_op jit(solution)/shard_map/ppermute | solution.py:36
  50.7 8.4 %collective-permute-start.9 = (bf16[64,8,128]{2,1,0:T(8,128)(2,1)}, bf16[64,8,128]{2,1,0:T(8,128)(2,1)S(1)}, u32[]{:S(2)}, u32[]{:S(2)}) collective-permute-start(bf16[64,8,128]{2,1,0:T(8,128)(2,1)} %get-tuple-element.38), channel_id=1, source_target_pairs={{0,3},{1,2},{2,1},{3,0},{4,7},{5,6},{6,5},{7,4},{8,11},{9,10},{10,... | collective-permute-start | bytes 393224 | tf_op jit(solution)/shard_map/ppermute | solution.py:36
  51.7 17.8 %collective-permute-start.10 = (bf16[4,128,128]{2,1,0:T(8,128)(2,1)}, bf16[4,128,128]{2,1,0:T(8,128)(2,1)S(1)}, u32[]{:S(2)}, u32[]{:S(2)}) collective-permute-start(bf16[4,128,128]{2,1,0:T(8,128)(2,1)} %get-tuple-element.41), channel_id=1, source_target_pairs={{0,1},{1,0},{2,3},{3,2},{4,5},{5,4},{6,7},{7,6},{8,9},{9,8},{10,11... | collective-permute-start | bytes 393224 | tf_op jit(solution)/shard_map/ppermute | solution.py:36
  51.8 17.7 %collective-permute-start.11 = (bf16[4,128,128]{2,1,0:T(8,128)(2,1)}, bf16[4,128,128]{2,1,0:T(8,128)(2,1)S(1)}, u32[]{:S(2)}, u32[]{:S(2)}) collective-permute-start(bf16[4,128,128]{2,1,0:T(8,128)(2,1)} %get-tuple-element.42), channel_id=1, source_target_pairs={{0,255},{1,2},{2,1},{3,4},{4,3},{5,6},{6,5},{7,8},{8,7},{9,10},{10... | collective-permute-start | bytes 393224 | tf_op jit(solution)/shard_map/ppermute | solution.py:36
  52.8 16.7 %collective-permute-start.12 = (bf16[4,128,128]{2,1,0:T(8,128)(2,1)}, bf16[4,128,128]{2,1,0:T(8,128)(2,1)S(1)}, u32[]{:S(2)}, u32[]{:S(2)}) collective-permute-start(bf16[4,128,128]{2,1,0:T(8,128)(2,1)} %get-tuple-element.43), channel_id=1, source_target_pairs={{0,2},{1,3},{2,0},{3,1},{4,6},{5,7},{6,4},{7,5},{8,10},{9,11},{10,... | collective-permute-start | bytes 393224 | tf_op jit(solution)/shard_map/ppermute | solution.py:36
  55.2 14.3 %collective-permute-start.13 = (bf16[4,128,128]{2,1,0:T(8,128)(2,1)}, bf16[4,128,128]{2,1,0:T(8,128)(2,1)S(1)}, u32[]{:S(2)}, u32[]{:S(2)}) collective-permute-start(bf16[4,128,128]{2,1,0:T(8,128)(2,1)} %get-tuple-element.44), channel_id=1, source_target_pairs={{0,254},{1,255},{2,4},{3,5},{4,2},{5,3},{6,8},{7,9},{8,6},{9,7},{1... | collective-permute-start | bytes 393224 | tf_op jit(solution)/shard_map/ppermute | solution.py:36
  60.3 16.7 %all-to-all-start.1 = ((bf16[64,8,128]{2,1,0:T(8,128)(2,1)}), bf16[64,8,128]{2,1,0:T(8,128)(2,1)S(1)}, u32[]{:S(2)}, u32[]{:S(2)}) async-start(bf16[64,8,128]{2,1,0:T(8,128)(2,1)} %add_pieces.1), calls=%async_computation.1 | async-start | bytes 262144 | tf_op jit(solution)/shard_map/all_to_all | solution.py:704

commit v7 on v6

--- a/solution.py
+++ b/solution.py
@@ -114,23 +114,8 @@
         near = blocks[row // tile, pl.ds(base, GROUP), :].astype(F32)
         chosen = jnp.where(place == lax.rem(row, GROUP), near, 0.0)
         rows.append(jnp.sum(chosen, 0, keepdims=True))
-    hub_out[...] = jnp.concatenate(rows, 0)
+    hub_out[...] = jnp.broadcast_to(jnp.concatenate(rows, 0).astype(BF16)[None], hub_out.shape)
     wait(moves)
-
-
-def spread_kernel(hub, _, out):
-    out[...] = jnp.broadcast_to(hub[...].astype(BF16)[None], out.shape)
-
-
-def spread_hubs(hub, after, parts):
-    return pl.pallas_call(
-        spread_kernel,
-        out_shape=jax.ShapeDtypeStruct((parts,) + hub.shape, BF16),
-        in_specs=[VMEM_SPEC, ANY_SPEC],
-        out_specs=VMEM_SPEC,
-        compiler_params=params(),
-        name="spread_hubs",
-    )(hub, after)
 
 
 def gather_sends(send, hubs, blocks, parts):
@@ -140,7 +125,7 @@
         send_kernel,
         out_shape=[pltpu.HBM((per_list, tile, width), BF16)] * lists
         + [
-            pltpu.VMEM((hubs.shape[0], width), F32),
+            jax.ShapeDtypeStruct((parts, hubs.shape[0], width), BF16),
             pltpu.VMEM(blocks.shape, BF16),
         ],
         in_specs=[HBM_SPEC] * 3,
@@ -220,12 +205,9 @@
     lists = len(OFFSETS)
     tiles_hbm, rows_hbm, agg_hbm, d_hbm = refs[:4]
     halos, refs = refs[4 : 4 + lists], refs[4 + lists :]
-    hubs, refs = refs[:QUAD], refs[QUAD:]
-    self_hbm, neigh_hbm, bias_hbm, hidden_hbm, d_pre_out, d_agg_hbm = refs[:6]
-    backs, mine, refs = refs[6 : 6 + lists], refs[6 + lists], refs[7 + lists :]
-    theirs, refs = refs[: QUAD - 1], refs[QUAD - 1 :]
-    hubs_in, hubs_f32, hub_rows = refs[:3]
-    refs = refs[3:]
+    hub, self_hbm, neigh_hbm, bias_hbm, hidden_hbm, d_pre_out, d_agg_hbm = refs[:7]
+    backs, mine, refs = refs[7 : 7 + lists], refs[7 + lists], refs[8 + lists :]
+    theirs, hub_rows, refs = refs[: QUAD - 1], refs[QUAD - 1], refs[QUAD:]
     src, weights, bias, table, rem_grad, backs_out, w_grad, b_grad = refs[:8]
     w_self_grad, w_neigh_grad, b_rows = refs[8:11]
     refs = refs[11:]
@@ -235,19 +217,18 @@
     width = rows.shape[-1]
     per_list = halos[0].shape[0]
     halo_count = lists * per_list
-    hub_blocks = table.shape[0] - halo_count
+    hub_blocks = hub.shape[0]
     place = lax.axis_index("dom") % QUAD
     slots = [j ^ 1 for j in lists_of_ways()]
     pairs = [
         (src_hbm, src),
+        (hub, table.at[pl.ds(halo_count, hub_blocks)]),
         (self_hbm, weights.at[pl.ds(0, width)]),
         (neigh_hbm, weights.at[pl.ds(width, width)]),
         (bias_hbm, bias),
     ]
     for w, s in enumerate(slots):
         pairs.append((halos[w], table.at[pl.ds(s * per_list, per_list)]))
-    for x in range(QUAD):
-        pairs.append((hubs[x], hubs_in.at[place ^ x]))
     moves = [pltpu.make_async_copy(*p, sem_t.at[n]) for n, p in enumerate(pairs)]
     chunks = count // STEP
 
@@ -279,13 +260,6 @@
     parts = QUAD * mine.shape[0]
     owned = hub_blocks * tile // parts
     each = parts // QUAD
-    for c in range(QUAD):
-        hubs_f32[...] = hubs_in[c].astype(F32)
-        for r in range(owned):
-            hub_rows[pl.ds(c * owned + r, each, stride=QUAD * owned), :] = hubs_f32[
-                pl.ds(r, each, stride=owned), :
-            ]
-    table[halo_count:] = hub_rows[...].reshape(hub_blocks, tile, width).astype(BF16)
 
     @pl.loop(0, chunks)
     def _(i):
@@ -295,34 +269,54 @@
         def edges(b):
             return jnp.concatenate([tiles[i * STEP + b, k] for k in range(per_block)], 1)
 
-        sources = [[src[k, i * STEP + b] for k in range(per_block)] for b in range(STEP)]
-        remote = [
-            jnp.dot(
-                edges(b),
-                jnp.concatenate([table[s] for s in sources[b]], 0),
-                preferred_element_type=F32,
-            )
-            for b in range(STEP)
-        ]
-        agg = agg_local[many, :] + jnp.concatenate(remote, 0)
-        both = jnp.concatenate([rows[many, :], agg.astype(BF16)], 1)
-        pre = jnp.dot(both, weights[...], preferred_element_type=F32) + bias[...]
-        sig = jax.nn.sigmoid(pre)
-        hidden[many, :] = (pre * sig).astype(BF16)
-        d_pre = d_hidden[many, :].astype(F32) * (sig * (1.0 + pre * (1.0 - sig)))
-        b_grad[...] += jnp.sum(d_pre.reshape(-1, 8, d_pre.shape[-1]), 0)
-        d_pre_b = d_pre.astype(BF16)
-        d_pre_out[many, :] = d_pre_b
-        d_agg = lax.dot_general(weights[width:, :], d_pre_b, NT, preferred_element_type=F32)
-        d_agg = d_agg.astype(BF16)
-        for b in range(STEP):
-            own = d_agg[:, b * tile : (b + 1) * tile]
-            d_agg_out[i * STEP + b] = own
-            terms = jnp.dot(own, edges(b), preferred_element_type=F32)
-            for k, s in enumerate(sources[b]):
-                rem_grad[s] += terms[:, k * tile : (k + 1) * tile]
+        per = STEP // 2
+        rows_per = per * tile
+
+        def lines(g):
+            return rows_of(i * 2 + g, rows_per)
+
+        def stage_a(g):
+            remote = []
+            for b in range(g * per, (g + 1) * per):
+                taken = [table[src[k, i * STEP + b]] for k in range(per_block)]
+                remote.append(
+                    jnp.dot(edges(b), jnp.concatenate(taken, 0), preferred_element_type=F32)
+                )
+            agg = agg_local[lines(g), :] + jnp.concatenate(remote, 0)
+            both = jnp.concatenate([rows[lines(g), :], agg.astype(BF16)], 1)
+            return both, jnp.dot(both, weights[...], preferred_element_type=F32) + bias[...]
+
+        def stage_b(g, pre):
+            sig = jax.nn.sigmoid(pre)
+            hid = pre * sig
+            hidden[lines(g), :] = hid.astype(BF16)
+            d_pre = d_hidden[lines(g), :].astype(F32) * (sig + hid * (1.0 - sig))
+            b_grad[...] += jnp.sum(d_pre.reshape(-1, 8, d_pre.shape[-1]), 0)
+            d_pre_b = d_pre.astype(BF16)
+            d_pre_out[lines(g), :] = d_pre_b
+            return d_pre_b
+
+        def stage_c(g, both, d_pre_b):
+            d_agg = lax.dot_general(weights[width:, :], d_pre_b, NT, preferred_element_type=F32)
+            d_agg = d_agg.astype(BF16)
+            for n in range(per):
+                b = g * per + n
+                own = d_agg[:, n * tile : (n + 1) * tile]
+                d_agg_out[i * STEP + b] = own
+                terms = jnp.dot(own, edges(b), preferred_element_type=F32)
+                for k in range(per_block):
+                    rem_grad[src[k, i * STEP + b]] += terms[:, k * tile : (k + 1) * tile]
+            w_grad[...] += lax.dot_general(d_pre_b, both, TN, preferred_element_type=F32)
+
+        held = {}
+        for stage, g in [(0, 0), (1, 0), (0, 1), (2, 0), (1, 1), (2, 1)]:
+            if stage == 0:
+                held[g] = stage_a(g)
+            elif stage == 1:
+                held[g] = (held[g][0], stage_b(g, held[g][1]))
+            else:
+                stage_c(g, *held[g])
         start(store(i))
-        w_grad[...] += lax.dot_general(d_pre_b, both, TN, preferred_element_type=F32)
 
     sent = []
     for w, s in enumerate(slots):
@@ -364,13 +358,12 @@
         wait(store(i))
 
 
-def layer(src, tiles, rows, agg_local, halos, hubs, w_self, w_neigh, bias, d_hidden, parts):
+def layer(src, tiles, rows, agg_local, halos, hub, w_self, w_neigh, bias, d_hidden, parts):
     count, per_block, tile, _ = tiles.shape
     nodes, width = rows.shape
     units = d_hidden.shape[-1]
     lists, per_list = len(halos), halos[0].shape[0]
-    hub_total = QUAD * hubs[0].shape[0]
-    table = lists * per_list + hub_total // tile
+    table = lists * per_list + hub.shape[0]
     pieces = (parts // QUAD, CHUNK, width)
     chunks = count // STEP
     return pl.pallas_call(
@@ -383,15 +376,13 @@
         + [pltpu.HBM((per_list, width, tile), BF16)] * lists
         + [pltpu.VMEM(pieces, F32)]
         + [pltpu.HBM(pieces, BF16)] * (QUAD - 1),
-        in_specs=[HBM_SPEC] * 5 + [ANY_SPEC] * (lists + QUAD) + [HBM_SPEC] * 3,
+        in_specs=[HBM_SPEC] * 5 + [ANY_SPEC] * (lists + 1) + [HBM_SPEC] * 3,
         out_specs=[HBM_SPEC, VMEM_SPEC]
         + [HBM_SPEC] * (lists + 1)
         + [VMEM_SPEC]
         + [HBM_SPEC] * (QUAD - 1),
         scratch_shapes=[
-            pltpu.VMEM((QUAD,) + hubs[0].shape, BF16),
-            pltpu.VMEM(hubs[0].shape, F32),
-            pltpu.VMEM((hub_total, width), F32),
+            pltpu.VMEM((hub.shape[0] * tile, width), F32),
             pltpu.SMEM(src.shape, jnp.int32),
             pltpu.VMEM((2 * width, units), BF16),
             pltpu.VMEM((1, units), F32),
@@ -411,7 +402,7 @@
             pltpu.VMEM((nodes, units), BF16),
             pltpu.VMEM((nodes, units), BF16),
             pltpu.VMEM((count, width, tile), BF16),
-            pltpu.SemaphoreType.DMA((lists + 4 + QUAD,)),
+            pltpu.SemaphoreType.DMA((lists + 5,)),
             pltpu.SemaphoreType.DMA((lists + QUAD - 1,)),
             pltpu.SemaphoreType.DMA((chunks, 4)),
             pltpu.SemaphoreType.DMA((chunks, 2)),
@@ -430,7 +421,7 @@
         hbm(agg_local),
         hbm(d_hidden),
         *halos,
-        *hubs,
+        hub,
         hbm(w_self),
         hbm(w_neigh),
         hbm(bias),
@@ -680,11 +671,8 @@
     tile = local_tiles.shape[-1]
     blocks = features.reshape(nodes // tile, tile, width)
     *sends, hub_mine, own = gather_sends(send_blocks, hub_rows, blocks, parts)
+    hub_all = lax.all_to_all(hub_mine, "dom", 0, 0)
     halos = [swapped(b, way) for way, b in enumerate(sends)]
-    groups = same_place(parts)
-    spread = spread_hubs(vmem(hub_mine), halos[0], parts // QUAD)
-    hub_quarter = lax.all_to_all(spread, "dom", 0, 0, axis_index_groups=groups)
-    hub_quarter = hub_quarter.reshape(-1, width)
     agg_local = local_aggregate(local_src.T, local_tiles, own)
     hidden, d_pre, d_agg, *rest = layer(
         remote_src.T,
@@ -692,7 +680,7 @@
         features,
         agg_local,
         halos,
-        [hub_quarter] + [swapped(hub_quarter, way) for way in SHARING],
+        hub_all.reshape(-1, tile, width),
         w_self,
         w_neigh,
         bias[None],
@@ -701,7 +689,7 @@
     )
     backs, mine, theirs = rest[: len(OFFSETS)], rest[len(OFFSETS)], rest[len(OFFSETS) + 1 :]
     packed = add_pieces(mine, [swapped(x, way) for x, way in zip(theirs, SHARING)])
-    pieces = lax.all_to_all(packed, "dom", 0, 0, axis_index_groups=groups)
+    pieces = lax.all_to_all(packed, "dom", 0, 0, axis_index_groups=same_place(parts))
     returned = [swapped(b, way) for way, b in enumerate(backs)]
     grad_t = local_backward(local_src.T, local_tiles, d_pre, d_agg, w_self)
     rough, near = collect(send_blocks, hub_rows, grad_t, returned)

time: 80.5 us -> 79.8 us (level)
  starting transfers between devices: 39.2 us -> 40.5 us
  Pallas kernels: 26.9 us -> 25.8 us
  waiting for transfers between devices: 12.1 us -> 11.2 us
    all_to_all x2, starting transfers between devices: 17.2 us -> 20.3 us  [the longest x1 15.7 us: shards(): hub_all = lax.all_to_all(hub_mine, 'dom', 0, 0)]
    all_to_all x2, waiting for transfers between devices: 8.45 us -> 5.46 us  [the longest x1 5.46 us: shards(): lax.all_to_all(packed, 'dom', 0, 0, axis_index_groups=same_place(parts))]
    ppermute x14 -> x11, waiting for transfers between devices: 3.62 us -> 5.78 us  [swapped(): lax.ppermute(block, 'dom', [(i, partner(i, way, n)) for i in range(n)])]
    ppermute x14 -> x11, starting transfers between devices: 22 us -> 20.2 us  [swapped(): lax.ppermute(block, 'dom', [(i, partner(i, way, n)) for i in range(n)])]
    pallas_call x1, Pallas kernels: 10.8 us -> 9.66 us  [layer(): pl.pallas_call(layer_kernel, out_shape=[pltpu.HBM((nodes, units), BF16),...]
  transfers between devices with their start and end apart: 16 -> 13, of which waited for: 4 -> 3; matrix products, arithmetic and copies ran while one was open for 0% -> 0% of each run, Pallas kernels for 15% -> 14%
where the time goes in v7:
time: 79.8 us; the launch traced here: 78.3 us
  starting transfers between devices  40.5 us (51%)
  Pallas kernels  25.8 us (32%)
  waiting for transfers between devices  11.2 us (14%)
    ppermute x11, starting transfers between devices, swapped(): lax.ppermute(block, 'dom', [(i, partner(i, way, n)) for i in range(n)])  20.2 us
    all_to_all x1, starting transfers between devices, shards(): hub_all = lax.all_to_all(hub_mine, 'dom', 0, 0)  15.7 us
    pallas_call x1, Pallas kernels, layer(): pl.pallas_call(layer_kernel, out_shape=[pltpu.HBM((nodes, units), BF16),...  9.66 us
    ppermute x11, waiting for transfers between devices, swapped(): lax.ppermute(block, 'dom', [(i, partner(i, way, n)) for i in range(n)])  5.78 us
    all_to_all x1, waiting for transfers between devices, shards(): lax.all_to_all(packed, 'dom', 0, 0, axis_index_groups=same_place(parts))  5.46 us
    all_to_all x1, starting transfers between devices, shards(): lax.all_to_all(packed, 'dom', 0, 0, axis_index_groups=same_place(parts))  4.63 us
    pallas_call x1, Pallas kernels, local_backward(): pl.pallas_call(back_kernel, out_shape=pltpu.VMEM((count, width, tile), F3...  4.54 us
    pallas_call x1, Pallas kernels, local_aggregate(): pl.pallas_call(local_kernel, out_shape=pltpu.HBM(agg, F32), in_specs=[HBM...  3.49 us
  transfers between devices with their start and end apart: 13, of which 3 were waited for; matrix products, arithmetic and copies ran while one was open for 0% of the time, Pallas kernels for 14%

profile of v7, /device:TPU:1, one launch (start us, length us, event | category | flops | bytes accessed | tf_op | source)
XLA Modules:
  0.0 78.3 jit_solution(17885465067806128351)
XLA Ops:
  0.6 2.9 %sends.1 = (bf16[4,128,128]{2,1,0:T(8,128)(2,1)}, bf16[4,128,128]{2,1,0:T(8,128)(2,1)}, bf16[4,128,128]{2,1,0:T(8,128)(2,1)}, bf16[4,128,128]{2,1,0:T(8,128)(2,1...) custom-call(s32[4,4]{1,0:T(4,128)} %send_hbm.3, s32[4]{0:T(128)} %hubs_hbm.5, ...), custom_call_target="tpu_custom_call" | custom-call | tf_op jit(solution)/shard_map/sends/pallas_call | solution.py:124
  3.5 15.7 %all-to-all-start = ((bf16[256,4,128]{2,1,0:T(4,128)(2,1)}), bf16[256,4,128]{2,1,0:T(4,128)(2,1)S(1)}, u32[]{:S(2)}, u32[]{:S(2)}) async-start(bf16[256,4,128]{2,1,0:T(4,128)(2,1)} %get-tuple-element.33), calls=%async_computation | async-start | bytes 524288 | tf_op jit(solution)/shard_map/all_to_all | solution.py:674
  19.2 2.2 %collective-permute-start = (bf16[4,128,128]{2,1,0:T(8,128)(2,1)}, bf16[4,128,128]{2,1,0:T(8,128)(2,1)S(1)}, u32[]{:S(2)}, u32[]{:S(2)}) collective-permute-start(bf16[4,128,128]{2,1,0:T(8,128)(2,1)} %get-tuple-element.29), channel_id=1, source_target_pairs={{0,1},{1,0},{2,3},{3,2},{4,5},{5,4},{6,7},{7,6},{8,9},{9,8},{10,11... | collective-permute-start | bytes 393224 | tf_op jit(solution)/shard_map/ppermute | solution.py:36
  21.4 0.0 collective-permute-start.1
  21.4 1.2 %collective-permute-start.2 = (bf16[4,128,128]{2,1,0:T(8,128)(2,1)}, bf16[4,128,128]{2,1,0:T(8,128)(2,1)S(1)}, u32[]{:S(2)}, u32[]{:S(2)}) collective-permute-start(bf16[4,128,128]{2,1,0:T(8,128)(2,1)} %get-tuple-element.31), channel_id=1, source_target_pairs={{0,2},{1,3},{2,0},{3,1},{4,6},{5,7},{6,4},{7,5},{8,10},{9,11},{10,... | collective-permute-start | bytes 393224 | tf_op jit(solution)/shard_map/ppermute | solution.py:36
  22.6 7.3 %collective-permute-start.3 = (bf16[4,128,128]{2,1,0:T(8,128)(2,1)}, bf16[4,128,128]{2,1,0:T(8,128)(2,1)S(1)}, u32[]{:S(2)}, u32[]{:S(2)}) collective-permute-start(bf16[4,128,128]{2,1,0:T(8,128)(2,1)} %get-tuple-element.32), channel_id=1, source_target_pairs={{0,254},{1,255},{2,4},{3,5},{4,2},{5,3},{6,8},{7,9},{8,6},{9,7},{1... | collective-permute-start | bytes 393224 | tf_op jit(solution)/shard_map/ppermute | solution.py:36
  30.0 3.5 %local_aggregate.1.refs_2_ = f32[4096,128]{1,0:T(8,128)} custom-call(s32[3,32]{1,0:T(4,128)} %bitcast.13, bf16[32,3,128,128]{3,2,1,0:T(8,128)(2,1)} %tiles_hbm.3, bf16[32,128,128]{2,1,0:T(8,128)(2,1)S(1)} %get-tuple-element.28.blocks), custom_call_target="tpu_custom_call" | custom-call | flops 10000000000 | bytes 67108864 | tf_op jit(solution)/shard_map/local_aggregate/pallas_call | solution.py:183
  33.5 0.0 collective-permute-done.refs_4_
  33.5 0.0 collective-permute-done.1.refs_5_
  33.5 2.4 %collective-permute-done.3.refs_7_ = bf16[4,128,128]{2,1,0:T(8,128)(2,1)S(1)} collective-permute-done((bf16[4,128,128]{2,1,0:T(8,128)(2,1)}, bf16[4,128,128]{2,1,0:T(8,128)(2,1)S(1)}, u32[]{:S(2)}, u32[]{:S(2)}) %collective-permute-start.3) | collective-permute-done | bytes 131104 | tf_op jit(solution)/shard_map/ppermute | solution.py:36
  35.9 0.0 all-to-all-done
  35.9 9.7 %layer.1 = (bf16[4096,256]{1,0:T(8,128)(2,1)}, bf16[4096,256]{1,0:T(8,128)(2,1)S(1)}, bf16[32,128,128]{2,1,0:T(8,128)(2,1)}, bf16[4,128,128]{2,1,0:T(8,128)(2,1)...) custom-call(s32[3,32]{1,0:T(4,128)} %bitcast.11, ...), custom_call_target="tpu_custom_call" | custom-call | flops 2415919104 | bytes 14680064 | tf_op jit(solution)/shard_map/layer/pallas_call | solution.py:369
  45.6 3.6 %collective-permute-start.4 = (bf16[64,8,128]{2,1,0:T(8,128)(2,1)}, bf16[64,8,128]{2,1,0:T(8,128)(2,1)S(1)}, u32[]{:S(2)}, u32[]{:S(2)}) collective-permute-start(bf16[64,8,128]{2,1,0:T(8,128)(2,1)} %get-tuple-element.36), channel_id=1, source_target_pairs={{0,1},{1,0},{2,3},{3,2},{4,5},{5,4},{6,7},{7,6},{8,9},{9,8},{10,11... | collective-permute-start | bytes 393224 | tf_op jit(solution)/shard_map/ppermute | solution.py:36
  49.2 1.7 %collective-permute-start.6 = (bf16[64,8,128]{2,1,0:T(8,128)(2,1)}, bf16[64,8,128]{2,1,0:T(8,128)(2,1)S(1)}, u32[]{:S(2)}, u32[]{:S(2)}) collective-permute-start(bf16[64,8,128]{2,1,0:T(8,128)(2,1)} %get-tuple-element.38), channel_id=1, source_target_pairs={{0,3},{1,2},{2,1},{3,0},{4,7},{5,6},{6,5},{7,4},{8,11},{9,10},{10,... | collective-permute-start | bytes 393224 | tf_op jit(solution)/shard_map/ppermute | solution.py:36
  51.0 0.1 collective-permute-start.7
  51.1 0.1 collective-permute-start.8
  51.2 3.3 %collective-permute-done.5.refs_1_ = bf16[64,8,128]{2,1,0:T(8,128)(2,1)S(1)} collective-permute-done((bf16[64,8,128]{2,1,0:T(8,128)(2,1)}, bf16[64,8,128]{2,1,0:T(8,128)(2,1)S(1)}, u32[]{:S(2)}, u32[]{:S(2)}) %collective-permute-start.5) | collective-permute-done | bytes 131104 | tf_op jit(solution)/shard_map/ppermute | solution.py:36
  54.5 3.9 %collective-permute-start.10 = (bf16[4,128,128]{2,1,0:T(8,128)(2,1)}, bf16[4,128,128]{2,1,0:T(8,128)(2,1)S(1)}, u32[]{:S(2)}, u32[]{:S(2)}) collective-permute-start(bf16[4,128,128]{2,1,0:T(8,128)(2,1)} %get-tuple-element.44), channel_id=1, source_target_pairs={{0,254},{1,255},{2,4},{3,5},{4,2},{5,3},{6,8},{7,9},{8,6},{9,7},{1... | collective-permute-start | bytes 393224 | tf_op jit(solution)/shard_map/ppermute | solution.py:36
  58.4 1.3 %add_pieces.1 = bf16[64,8,128]{2,1,0:T(8,128)(2,1)} custom-call(f32[64,8,128]{2,1,0:T(8,128)S(1)} %get-tuple-element.35.mine, bf16[64,8,128]{2,1,0:T(8,128)(2,1)S(1)} %collective-permute-done.4.refs_0_, bf16[64,8,128]{2,1,0:T(8,128)(2,1)S(1)} %collective-permute-done.5.refs_1_, bf16[64,8,128]{2,1,0:T(8,128)(2,1)S(1)} %collective-permute-done.6.refs_2_), custom_call_target="tpu_custom_call" | custom-call | tf_op jit(solution)/shard_map/add_pieces/pallas_call | solution.py:448
  59.6 4.6 %all-to-all-start.1 = ((bf16[64,8,128]{2,1,0:T(8,128)(2,1)}), bf16[64,8,128]{2,1,0:T(8,128)(2,1)S(1)}, u32[]{:S(2)}, u32[]{:S(2)}) async-start(bf16[64,8,128]{2,1,0:T(8,128)(2,1)} %add_pieces.1), calls=%async_computation.1 | async-start | bytes 262144 | tf_op jit(solution)/shard_map/all_to_all | solution.py:692
  64.2 4.5 %local_backward.1._ = f32[32,128,128]{2,1,0:T(8,128)S(1)} custom-call(s32[3,32]{1,0:T(4,128)} %bitcast.14, bf16[128,256]{1,0:T(8,128)(2,1)} %weight_hbm.1, bf16[32,3,128,128]{3,2,1,0:T(8,128)(2,1)} %tiles_hbm.3, bf16[32,128,128]{2,1,0:T(8,128)(2,1)} %get-tuple-element.39.d_hbm, bf16[4096,256]{1,0:T(8,128)(2,1)S(1)} %get-tuple-element.40.d_pre), custom_call_target="tpu_custom_call" | custom-call | flops 10000000000 | bytes 67108864 | tf_op jit(solution)/shard_map/local_backward/pallas_call | solution.py:504
  68.8 2.0 %collect.1 = (f32[32,128,128]{2,1,0:T(8,128)S(1)}, bf16[4096,128]{1,0:T(8,128)(2,1)}, f32[4,16,128]{2,1,0:T(8,128)S(1)}) custom-call(s32[4,4]{1,0:T(4,128)} %send_hbm.3, s32[4]{0:T(128)} %hubs_hbm.5, f32[32,128,128]{2,1,0:T(8,128)S(1)} %local_backward.1._, bf16[4,128,128]{2,1,0:T(8,128)(2,1)S(1)} %collective-permute-done.7.refs_0_, ...), custom_call_target="tpu_custom_call", output_to_operand_aliasing={{0}: (2, {})} | custom-call | flops 4194304 | bytes 4194304 | tf_op jit(solution)/shard_map/collect/pallas_call | solution.py:562
  70.9 5.5 %all-to-all-done.1.pieces_hbm = bf16[64,8,128]{2,1,0:T(8,128)(2,1)S(1)} async-done(((bf16[64,8,128]{2,1,0:T(8,128)(2,1)}), bf16[64,8,128]{2,1,0:T(8,128)(2,1)S(1)}, u32[]{:S(2)}, u32[]{:S(2)}) %all-to-all-start.1) | async-done | bytes 131104 | tf_op jit(solution)/shard_map/all_to_all | solution.py:692
  76.3 2.0 %finish.1 = (bf16[4096,128]{1,0:T(8,128)(2,1)}, f32[1,128]{1,0:T(1,128)}, f32[1,128]{1,0:T(1,128)}, f32[1,128]{1,0:T(1,128)}) custom-call(s32[4]{0:T(128)} %hubs_hbm.5, bf16[64,8,128]{2,1,0:T(8,128)(2,1)S(1)} %all-to-all-done.1.pieces_hbm, f32[4,16,128]{2,1,0:T(8,128)S(1)} %get-tuple-element.45.near, ...), custom_call_target="tpu_custom_call", output_to_operand_aliasing={{0}: (3, {})} | custom-call | tf_op jit(solution)/shard_map/finish/pallas_call | solution.py:638
  (9 shorter events, 0.0 us)
Async XLA Ops:
  3.5 32.4 %all-to-all-start = ((bf16[256,4,128]{2,1,0:T(4,128)(2,1)}), bf16[256,4,128]{2,1,0:T(4,128)(2,1)S(1)}, u32[]{:S(2)}, u32[]{:S(2)}) async-start(bf16[256,4,128]{2,1,0:T(4,128)(2,1)} %get-tuple-element.33), calls=%async_computation | async-start | bytes 524288 | tf_op jit(solution)/shard_map/all_to_all | solution.py:674
  19.2 14.3 %collective-permute-start = (bf16[4,128,128]{2,1,0:T(8,128)(2,1)}, bf16[4,128,128]{2,1,0:T(8,128)(2,1)S(1)}, u32[]{:S(2)}, u32[]{:S(2)}) collective-permute-start(bf16[4,128,128]{2,1,0:T(8,128)(2,1)} %get-tuple-element.29), channel_id=1, source_target_pairs={{0,1},{1,0},{2,3},{3,2},{4,5},{5,4},{6,7},{7,6},{8,9},{9,8},{10,11... | collective-permute-start | bytes 393224 | tf_op jit(solution)/shard_map/ppermute | solution.py:36
  21.4 12.0 %collective-permute-start.1 = (bf16[4,128,128]{2,1,0:T(8,128)(2,1)}, bf16[4,128,128]{2,1,0:T(8,128)(2,1)S(1)}, u32[]{:S(2)}, u32[]{:S(2)}) collective-permute-start(bf16[4,128,128]{2,1,0:T(8,128)(2,1)} %get-tuple-element.30), channel_id=1, source_target_pairs={{0,255},{1,2},{2,1},{3,4},{4,3},{5,6},{6,5},{7,8},{8,7},{9,10},{10... | collective-permute-start | bytes 393224 | tf_op jit(solution)/shard_map/ppermute | solution.py:36
  21.4 12.1 %collective-permute-start.2 = (bf16[4,128,128]{2,1,0:T(8,128)(2,1)}, bf16[4,128,128]{2,1,0:T(8,128)(2,1)S(1)}, u32[]{:S(2)}, u32[]{:S(2)}) collective-permute-start(bf16[4,128,128]{2,1,0:T(8,128)(2,1)} %get-tuple-element.31), channel_id=1, source_target_pairs={{0,2},{1,3},{2,0},{3,1},{4,6},{5,7},{6,4},{7,5},{8,10},{9,11},{10,... | collective-permute-start | bytes 393224 | tf_op jit(solution)/shard_map/ppermute | solution.py:36
  22.6 13.3 %collective-permute-start.3 = (bf16[4,128,128]{2,1,0:T(8,128)(2,1)}, bf16[4,128,128]{2,1,0:T(8,128)(2,1)S(1)}, u32[]{:S(2)}, u32[]{:S(2)}) collective-permute-start(bf16[4,128,128]{2,1,0:T(8,128)(2,1)} %get-tuple-element.32), channel_id=1, source_target_pairs={{0,254},{1,255},{2,4},{3,5},{4,2},{5,3},{6,8},{7,9},{8,6},{9,7},{1... | collective-permute-start | bytes 393224 | tf_op jit(solution)/shard_map/ppermute | solution.py:36
  45.6 5.6 %collective-permute-start.4 = (bf16[64,8,128]{2,1,0:T(8,128)(2,1)}, bf16[64,8,128]{2,1,0:T(8,128)(2,1)S(1)}, u32[]{:S(2)}, u32[]{:S(2)}) collective-permute-start(bf16[64,8,128]{2,1,0:T(8,128)(2,1)} %get-tuple-element.36), channel_id=1, source_target_pairs={{0,1},{1,0},{2,3},{3,2},{4,5},{5,4},{6,7},{7,6},{8,9},{9,8},{10,11... | collective-permute-start | bytes 393224 | tf_op jit(solution)/shard_map/ppermute | solution.py:36
  49.2 5.3 %collective-permute-start.5 = (bf16[64,8,128]{2,1,0:T(8,128)(2,1)}, bf16[64,8,128]{2,1,0:T(8,128)(2,1)S(1)}, u32[]{:S(2)}, u32[]{:S(2)}) collective-permute-start(bf16[64,8,128]{2,1,0:T(8,128)(2,1)} %get-tuple-element.37), channel_id=1, source_target_pairs={{0,2},{1,3},{2,0},{3,1},{4,6},{5,7},{6,4},{7,5},{8,10},{9,11},{10,... | collective-permute-start | bytes 393224 | tf_op jit(solution)/shard_map/ppermute | solution.py:36
  49.2 9.1 %collective-permute-start.6 = (bf16[64,8,128]{2,1,0:T(8,128)(2,1)}, bf16[64,8,128]{2,1,0:T(8,128)(2,1)S(1)}, u32[]{:S(2)}, u32[]{:S(2)}) collective-permute-start(bf16[64,8,128]{2,1,0:T(8,128)(2,1)} %get-tuple-element.38), channel_id=1, source_target_pairs={{0,3},{1,2},{2,1},{3,0},{4,7},{5,6},{6,5},{7,4},{8,11},{9,10},{10,... | collective-permute-start | bytes 393224 | tf_op jit(solution)/shard_map/ppermute | solution.py:36
  51.0 17.8 %collective-permute-start.7 = (bf16[4,128,128]{2,1,0:T(8,128)(2,1)}, bf16[4,128,128]{2,1,0:T(8,128)(2,1)S(1)}, u32[]{:S(2)}, u32[]{:S(2)}) collective-permute-start(bf16[4,128,128]{2,1,0:T(8,128)(2,1)} %get-tuple-element.41), channel_id=1, source_target_pairs={{0,1},{1,0},{2,3},{3,2},{4,5},{5,4},{6,7},{7,6},{8,9},{9,8},{10,11... | collective-permute-start | bytes 393224 | tf_op jit(solution)/shard_map/ppermute | solution.py:36
  51.1 17.7 %collective-permute-start.8 = (bf16[4,128,128]{2,1,0:T(8,128)(2,1)}, bf16[4,128,128]{2,1,0:T(8,128)(2,1)S(1)}, u32[]{:S(2)}, u32[]{:S(2)}) collective-permute-start(bf16[4,128,128]{2,1,0:T(8,128)(2,1)} %get-tuple-element.42), channel_id=1, source_target_pairs={{0,255},{1,2},{2,1},{3,4},{4,3},{5,6},{6,5},{7,8},{8,7},{9,10},{10... | collective-permute-start | bytes 393224 | tf_op jit(solution)/shard_map/ppermute | solution.py:36
  51.2 17.6 %collective-permute-start.9 = (bf16[4,128,128]{2,1,0:T(8,128)(2,1)}, bf16[4,128,128]{2,1,0:T(8,128)(2,1)S(1)}, u32[]{:S(2)}, u32[]{:S(2)}) collective-permute-start(bf16[4,128,128]{2,1,0:T(8,128)(2,1)} %get-tuple-element.43), channel_id=1, source_target_pairs={{0,2},{1,3},{2,0},{3,1},{4,6},{5,7},{6,4},{7,5},{8,10},{9,11},{10,... | collective-permute-start | bytes 393224 | tf_op jit(solution)/shard_map/ppermute | solution.py:36
  54.5 14.3 %collective-permute-start.10 = (bf16[4,128,128]{2,1,0:T(8,128)(2,1)}, bf16[4,128,128]{2,1,0:T(8,128)(2,1)S(1)}, u32[]{:S(2)}, u32[]{:S(2)}) collective-permute-start(bf16[4,128,128]{2,1,0:T(8,128)(2,1)} %get-tuple-element.44), channel_id=1, source_target_pairs={{0,254},{1,255},{2,4},{3,5},{4,2},{5,3},{6,8},{7,9},{8,6},{9,7},{1... | collective-permute-start | bytes 393224 | tf_op jit(solution)/shard_map/ppermute | solution.py:36
  59.6 16.7 %all-to-all-start.1 = ((bf16[64,8,128]{2,1,0:T(8,128)(2,1)}), bf16[64,8,128]{2,1,0:T(8,128)(2,1)S(1)}, u32[]{:S(2)}, u32[]{:S(2)}) async-start(bf16[64,8,128]{2,1,0:T(8,128)(2,1)} %add_pieces.1), calls=%async_computation.1 | async-start | bytes 262144 | tf_op jit(solution)/shard_map/all_to_all | solution.py:692

commit v8 on v4

--- a/solution.py
+++ b/solution.py
@@ -193,11 +193,11 @@
     lists = len(OFFSETS)
     tiles_hbm, rows_hbm, agg_hbm, d_hbm = refs[:4]
     halos, refs = refs[4 : 4 + lists], refs[4 + lists :]
-    hub, self_hbm, neigh_hbm, bias_hbm, hidden_hbm, d_pre_out, d_agg_hbm = refs[:7]
+    hub, self_hbm, neigh_hbm, bias_hbm, hidden_hbm, d_pre_hbm, d_agg_hbm = refs[:7]
     backs, refs = refs[7 : 7 + lists], refs[7 + lists :]
     mine, theirs, src, weights, bias, table, rem_grad, backs_out, w_grad, b_grad = refs[:10]
     spread, pack_out, tiles, rows, agg_local, d_hidden, hidden, d_agg_out = refs[10:18]
-    sem_t, sem_back, sem_in, sem_out = refs[18:]
+    d_pre_out, sem_t, sem_back, sem_in, sem_out = refs[18:]
     count, per_block, tile, _ = tiles.shape
     width = rows.shape[-1]
     per_list = halos[0].shape[0]
@@ -231,6 +231,7 @@
         pairs = (
             (hidden.at[many], hidden_hbm.at[many]),
             (d_agg_out.at[few], d_agg_hbm.at[few]),
+            (d_pre_out.at[many], d_pre_hbm.at[many]),
         )
         return [pltpu.make_async_copy(*p, sem_out.at[i, n]) for n, p in enumerate(pairs)]
 
@@ -250,34 +251,54 @@
         def edges(b):
             return jnp.concatenate([tiles[i * STEP + b, k] for k in range(per_block)], 1)
 
-        sources = [[src[k, i * STEP + b] for k in range(per_block)] for b in range(STEP)]
-        remote = [
-            jnp.dot(
-                edges(b),
-                jnp.concatenate([table[s] for s in sources[b]], 0),
-                preferred_element_type=F32,
-            )
-            for b in range(STEP)
-        ]
-        agg = agg_local[many, :] + jnp.concatenate(remote, 0)
-        both = jnp.concatenate([rows[many, :], agg.astype(BF16)], 1)
-        pre = jnp.dot(both, weights[...], preferred_element_type=F32) + bias[...]
-        sig = jax.nn.sigmoid(pre)
-        hidden[many, :] = (pre * sig).astype(BF16)
-        d_pre = d_hidden[many, :].astype(F32) * (sig * (1.0 + pre * (1.0 - sig)))
-        b_grad[...] += jnp.sum(d_pre.reshape(-1, 8, d_pre.shape[-1]), 0)
-        d_pre_b = d_pre.astype(BF16)
-        d_pre_out[many, :] = d_pre_b
-        d_agg = lax.dot_general(weights[width:, :], d_pre_b, NT, preferred_element_type=F32)
-        d_agg = d_agg.astype(BF16)
-        for b in range(STEP):
-            own = d_agg[:, b * tile : (b + 1) * tile]
-            d_agg_out[i * STEP + b] = own
-            terms = jnp.dot(own, edges(b), preferred_element_type=F32)
-            for k, s in enumerate(sources[b]):
-                rem_grad[s] += terms[:, k * tile : (k + 1) * tile]
+        per = STEP // 2
+        rows_per = per * tile
+
+        def lines(g):
+            return rows_of(i * 2 + g, rows_per)
+
+        def stage_a(g):
+            remote = []
+            for b in range(g * per, (g + 1) * per):
+                taken = [table[src[k, i * STEP + b]] for k in range(per_block)]
+                remote.append(
+                    jnp.dot(edges(b), jnp.concatenate(taken, 0), preferred_element_type=F32)
+                )
+            agg = agg_local[lines(g), :] + jnp.concatenate(remote, 0)
+            both = jnp.concatenate([rows[lines(g), :], agg.astype(BF16)], 1)
+            return both, jnp.dot(both, weights[...], preferred_element_type=F32) + bias[...]
+
+        def stage_b(g, pre):
+            sig = jax.nn.sigmoid(pre)
+            hid = pre * sig
+            hidden[lines(g), :] = hid.astype(BF16)
+            d_pre = d_hidden[lines(g), :].astype(F32) * (sig + hid * (1.0 - sig))
+            b_grad[...] += jnp.sum(d_pre.reshape(-1, 8, d_pre.shape[-1]), 0)
+            d_pre_b = d_pre.astype(BF16)
+            d_pre_out[lines(g), :] = d_pre_b
+            return d_pre_b
+
+        def stage_c(g, both, d_pre_b):
+            d_agg = lax.dot_general(weights[width:, :], d_pre_b, NT, preferred_element_type=F32)
+            d_agg = d_agg.astype(BF16)
+            for n in range(per):
+                b = g * per + n
+                own = d_agg[:, n * tile : (n + 1) * tile]
+                d_agg_out[i * STEP + b] = own
+                terms = jnp.dot(own, edges(b), preferred_element_type=F32)
+                for k in range(per_block):
+                    rem_grad[src[k, i * STEP + b]] += terms[:, k * tile : (k + 1) * tile]
+            w_grad[...] += lax.dot_general(d_pre_b, both, TN, preferred_element_type=F32)
+
+        held = {}
+        for stage, g in [(0, 0), (1, 0), (0, 1), (2, 0), (1, 1), (2, 1)]:
+            if stage == 0:
+                held[g] = stage_a(g)
+            elif stage == 1:
+                held[g] = (held[g][0], stage_b(g, held[g][1]))
+            else:
+                stage_c(g, *held[g])
         start(store(i))
-        w_grad[...] += lax.dot_general(d_pre_b, both, TN, preferred_element_type=F32)
 
     sent = []
     for w, s in enumerate(slots):
@@ -326,13 +347,13 @@
         layer_kernel,
         out_shape=[
             pltpu.HBM((nodes, units), BF16),
-            pltpu.VMEM((nodes, units), BF16),
+            pltpu.HBM((nodes, units), BF16),
             pltpu.HBM((count, width, tile), BF16),
         ]
         + [pltpu.HBM((per_list, width, tile), BF16)] * lists
         + [pltpu.VMEM(pieces, F32), pltpu.HBM(pieces, BF16)],
         in_specs=[HBM_SPEC] * 5 + [ANY_SPEC] * (lists + 1) + [HBM_SPEC] * 3,
-        out_specs=[HBM_SPEC, VMEM_SPEC] + [HBM_SPEC] * (lists + 1) + [VMEM_SPEC, HBM_SPEC],
+        out_specs=[HBM_SPEC] * (lists + 3) + [VMEM_SPEC, HBM_SPEC],
         scratch_shapes=[
             pltpu.SMEM(src.shape, jnp.int32),
             pltpu.VMEM((2 * width, units), BF16),
@@ -350,10 +371,11 @@
             pltpu.VMEM((nodes, units), BF16),
             pltpu.VMEM((nodes, units), BF16),
             pltpu.VMEM((count, width, tile), BF16),
+            pltpu.VMEM((nodes, units), BF16),
             pltpu.SemaphoreType.DMA((lists + 5,)),
             pltpu.SemaphoreType.DMA((lists + 1,)),
             pltpu.SemaphoreType.DMA((chunks, 4)),
-            pltpu.SemaphoreType.DMA((chunks, 2)),
+            pltpu.SemaphoreType.DMA((chunks, 3)),
         ],
         compiler_params=params(),
         cost_estimate=pl.CostEstimate(
@@ -403,14 +425,19 @@
 
 
 def back_kernel(
-    src_hbm, weight_hbm, tiles_hbm, d_hbm, d_pre, total, src, weight, tiles, d_agg, sems, sem_in
+    src_hbm, weight_hbm, tiles_hbm, d_hbm, p_hbm, total, src, weight, tiles, d_agg, d_pre, sems, sem_in
 ):
     count, per_block, tile, _ = tiles.shape
     size = STEP * tile
 
     def fetch(i):
         part = pl.ds(i * STEP, STEP)
-        pairs = ((tiles_hbm.at[part], tiles.at[part]), (d_hbm.at[part], d_agg.at[part]))
+        many = rows_of(i, size)
+        pairs = (
+            (p_hbm.at[many], d_pre.at[many]),
+            (tiles_hbm.at[part], tiles.at[part]),
+            (d_hbm.at[part], d_agg.at[part]),
+        )
         return [pltpu.make_async_copy(*p, sem_in.at[i, n]) for n, p in enumerate(pairs)]
 
     loads = [
@@ -445,15 +472,16 @@
     return pl.pallas_call(
         back_kernel,
         out_shape=pltpu.VMEM((count, width, tile), F32),
-        in_specs=[HBM_SPEC] * 4 + [VMEM_SPEC],
+        in_specs=[HBM_SPEC] * 5,
         out_specs=VMEM_SPEC,
         scratch_shapes=[
             pltpu.SMEM(src.shape, jnp.int32),
             pltpu.VMEM(weight.shape, BF16),
             pltpu.VMEM(tiles.shape, BF16),
             pltpu.VMEM(d_agg.shape, BF16),
+            pltpu.VMEM(d_pre.shape, BF16),
             pltpu.SemaphoreType.DMA((2,)),
-            pltpu.SemaphoreType.DMA((count // STEP, 2)),
+            pltpu.SemaphoreType.DMA((count // STEP, 3)),
         ],
         compiler_params=params(),
         cost_estimate=pl.CostEstimate(
@@ -462,22 +490,35 @@
             transcendentals=0,
         ),
         name="local_backward",
-    )(hbm(src), hbm(weight), hbm(tiles), hbm(d_agg), vmem(d_pre))
-
-
-def collect_kernel(send_hbm, hubs_hbm, _, *refs):
+    )(hbm(src), hbm(weight), hbm(tiles), hbm(d_agg), hbm(d_pre))
+
+
+def collect_kernel(send_hbm, hubs_hbm, _, pieces_any, *refs):
     lists, per_list = send_hbm.shape
-    halos_hbm = refs[:lists]
-    total, out, near, send, hubs, halos, turned, sem_in, sem_out = refs[lists:]
+    halos_any, refs = refs[:lists], refs[lists:]
+    total, out, g_self, g_neigh, g_bias = refs[:5]
+    send, hubs, halos, pieces, turned, sem_in, sem_out = refs[5:]
     count, width, tile = total.shape
+    owned = hubs.shape[0]
     pairs = [(send_hbm, send), (hubs_hbm, hubs)]
-    pairs += [(halos_hbm[way], halos.at[way]) for way in range(lists)]
+    pairs += [(halos_any[way], halos.at[way]) for way in range(lists)]
+    pairs.append((pieces_any, pieces))
     loads = [pltpu.make_async_copy(*p, sem_in.at[n]) for n, p in enumerate(pairs)]
     start(loads)
     wait(loads)
     for way, j in enumerate(lists_of_ways()):
         for h in range(per_list):
             total[send[j, h]] += halos[way, h].astype(F32)
+    summed = jnp.sum(pieces[...].astype(F32), 0)
+    g_self[...] = summed[owned : owned + 1, :]
+    g_neigh[...] = summed[owned + 1 : owned + 2, :]
+    last = summed[owned + 2 : owned + 3, :]
+    g_bias[...] = jnp.broadcast_to(last[:, 0:1] + last[:, 1:2], last.shape)
+    lane = lax.broadcasted_iota(jnp.int32, (width, tile), 1)
+    for i in range(owned):
+        row = hubs[i]
+        column = jnp.transpose(jnp.broadcast_to(summed[i : i + 1, :], (tile, width)))
+        total[row // tile] += jnp.where(lane == lax.rem(row, tile), column, 0.0)
     chunks = sem_out.shape[0]
     each = count // chunks
     stores = []
@@ -487,113 +528,32 @@
         part = pl.ds(c * each * tile, each * tile)
         stores.append(pltpu.make_async_copy(turned.at[part], out.at[part], sem_out.at[c]))
         stores[-1].start()
-    for i in range(hubs.shape[0]):
-        row = hubs[i]
-        block = jnp.transpose(total[row // tile])
-        want = lax.rem(row, tile) // GROUP
-        part = jnp.zeros((GROUP, width), F32)
-        for g in range(tile // GROUP):
-            part = jnp.where(want == g, block[g * GROUP : (g + 1) * GROUP], part)
-        near[i] = part
     wait(stores)
 
 
-def collect(send, hubs, grad, halos):
+def collect(send, hubs, grad, pieces, halos):
     count, width, tile = grad.shape
     lists = len(halos)
-    near = (hubs.shape[0], GROUP, width)
+    line = jax.ShapeDtypeStruct((1, width), F32)
     return pl.pallas_call(
         collect_kernel,
-        out_shape=[
-            pltpu.VMEM(grad.shape, F32),
-            pltpu.HBM((count * tile, width), BF16),
-            pltpu.VMEM(near, F32),
-        ],
-        in_specs=[HBM_SPEC] * 2 + [VMEM_SPEC] + [ANY_SPEC] * lists,
-        out_specs=[VMEM_SPEC, HBM_SPEC, VMEM_SPEC],
+        out_shape=[pltpu.VMEM(grad.shape, F32), pltpu.HBM((count * tile, width), BF16)]
+        + [line] * 3,
+        in_specs=[HBM_SPEC] * 2 + [VMEM_SPEC] + [ANY_SPEC] * (1 + lists),
+        out_specs=[VMEM_SPEC, HBM_SPEC] + [VMEM_SPEC] * 3,
         scratch_shapes=[
             pltpu.SMEM(send.shape, jnp.int32),
             pltpu.SMEM(hubs.shape, jnp.int32),
             pltpu.VMEM((lists,) + halos[0].shape, BF16),
+            pltpu.VMEM(pieces.shape, BF16),
             pltpu.VMEM((count * tile, width), BF16),
-            pltpu.SemaphoreType.DMA((2 + lists,)),
+            pltpu.SemaphoreType.DMA((3 + lists,)),
             pltpu.SemaphoreType.DMA((4,)),
         ],
         input_output_aliases={2: 0},
         compiler_params=params(),
-        cost_estimate=pl.CostEstimate(
-            flops=grad.size * 8, bytes_accessed=4 << 20, transcendentals=0
-        ),
         name="collect",
-    )(hbm(send), hbm(hubs), vmem(grad), *halos)[1:]
-
-
-def finish_kernel(
-    hubs_hbm, pieces_hbm, near, _, grad, g_self, g_neigh, g_bias, hubs, pieces, rows, sem_in, sems
-):
-    owned = hubs.shape[0]
-    chunks = sem_in.shape[0] - 1
-    each = pieces.shape[0] // chunks
-    index = pltpu.make_async_copy(hubs_hbm, hubs, sem_in.at[chunks])
-    index.start()
-    loads = []
-    for c in range(chunks):
-        part = pl.ds(c * each, each)
-        loads.append(pltpu.make_async_copy(pieces_hbm.at[part], pieces.at[part], sem_in.at[c]))
-    start(loads)
-    index.wait()
-    total = jnp.zeros(pieces.shape[1:], F32)
-    for c in range(chunks):
-        loads[c].wait()
-        total += jnp.sum(pieces[c * each : (c + 1) * each].astype(F32), 0)
-    g_self[...] = total[owned : owned + 1, :]
-    g_neigh[...] = total[owned + 1 : owned + 2, :]
-    last = total[owned + 2 : owned + 3, :]
-    g_bias[...] = jnp.broadcast_to(last[:, 0:1] + last[:, 1:2], last.shape)
-    place = lax.broadcasted_iota(jnp.int32, (GROUP, total.shape[-1]), 0)
-    for i in range(owned):
-        value = near[i]
-        for m in range(owned):
-            same = hubs[m] // GROUP == hubs[i] // GROUP
-            hit = jnp.logical_and(place == lax.rem(hubs[m], GROUP), same)
-            value = value + jnp.where(hit, total[m : m + 1, :], 0.0)
-        rows[i] = value.astype(BF16)
-
-    def fresh(i):
-        new = hubs[i] >= 0
-        for m in range(i):
-            new = jnp.logical_and(new, hubs[m] // GROUP != hubs[i] // GROUP)
-        return new
-
-    def move(i):
-        base = pl.multiple_of(hubs[i] // GROUP * GROUP, GROUP)
-        return pltpu.make_async_copy(rows.at[i], grad.at[pl.ds(base, GROUP), :], sems.at[i])
-
-    for i in range(owned):
-        pl.when(fresh(i))(lambda i=i: move(i).start())
-    for i in range(owned):
-        pl.when(fresh(i))(lambda i=i: move(i).wait())
-
-
-def finish(hubs, pieces, near, grad):
-    owned, _, width = near.shape
-    line = jax.ShapeDtypeStruct((1, width), F32)
-    return pl.pallas_call(
-        finish_kernel,
-        out_shape=[pltpu.HBM(grad.shape, grad.dtype), line, line, line],
-        in_specs=[HBM_SPEC, ANY_SPEC, VMEM_SPEC, HBM_SPEC],
-        out_specs=[HBM_SPEC, VMEM_SPEC, VMEM_SPEC, VMEM_SPEC],
-        scratch_shapes=[
-            pltpu.SMEM(hubs.shape, jnp.int32),
-            pltpu.VMEM(pieces.shape, BF16),
-            pltpu.VMEM((owned, GROUP, width), BF16),
-            pltpu.SemaphoreType.DMA((5,)),
-            pltpu.SemaphoreType.DMA((owned,)),
-        ],
-        input_output_aliases={3: 0},
-        compiler_params=params(),
-        name="finish",
-    )(hbm(hubs), pieces, vmem(near), hbm(grad))
+    )(hbm(send), hbm(hubs), vmem(grad), pieces, *halos)[1:]
 
 
 def shards(
@@ -637,8 +597,7 @@
     pieces = lax.all_to_all(packed, "dom", 0, 0, axis_index_groups=same_core)
     returned = [swapped(b, way) for way, b in enumerate(backs)]
     grad_t = local_backward(local_src.T, local_tiles, d_pre, d_agg, w_self)
-    rough, near = collect(send_blocks, hub_rows, grad_t, returned)
-    grad, g_self, g_neigh, g_bias = finish(hub_rows, pieces, near, rough)
+    grad, g_self, g_neigh, g_bias = collect(send_blocks, hub_rows, grad_t, pieces, returned)
     return (hidden, grad, g_self.reshape(width, 1), g_neigh.reshape(width, 1), g_bias[0, :1])
 
 

time: 78.4 us -> 76.3 us (0.973)
  Pallas kernels: 26.2 us -> 25 us
  waiting for transfers between devices: 5.84 us -> 5.05 us
    pallas_call x1 -> x0, Pallas kernels: 2.04 us -> none  [finish(): pl.pallas_call(finish_kernel, out_shape=[pltpu.HBM(grad.shape, grad.dtype...]
    pallas_call x1, Pallas kernels: 4.54 us -> 5.34 us  [local_backward(): pl.pallas_call(back_kernel, out_shape=pltpu.VMEM((count, width, tile), F3...]
    ppermute x9, waiting for transfers between devices: 5.84 us -> 5.04 us  [swapped(): lax.ppermute(block, 'dom', [(i, partner(i, way, n)) for i in range(n)])]
  transfers between devices with their start and end apart: 11 -> 11, of which waited for: 3 -> 3; matrix products, arithmetic and copies ran while one was open for 0% -> 0% of each run, Pallas kernels for 13% -> 12%
where the time goes in v8:
time: 76.3 us; the launch traced here: 76.1 us
  starting transfers between devices  45.3 us (59%)
  Pallas kernels  25 us (33%)
  waiting for transfers between devices  5.05 us (7%)
    ppermute x9, starting transfers between devices, swapped(): lax.ppermute(block, 'dom', [(i, partner(i, way, n)) for i in range(n)])  23.5 us
    all_to_all x1, starting transfers between devices, shards(): hub_all = lax.all_to_all(hub_mine, 'dom', 0, 0)  15.7 us
    pallas_call x1, Pallas kernels, layer(): pl.pallas_call(layer_kernel, out_shape=[pltpu.HBM((nodes, units), BF16),...  9.75 us
    all_to_all x1, starting transfers between devices, shards(): pieces = lax.all_to_all(packed, 'dom', 0, 0, axis_index_groups=same_core)  6.17 us
    pallas_call x1, Pallas kernels, local_backward(): pl.pallas_call(back_kernel, out_shape=pltpu.VMEM((count, width, tile), F3...  5.34 us
    ppermute x9, waiting for transfers between devices, swapped(): lax.ppermute(block, 'dom', [(i, partner(i, way, n)) for i in range(n)])  5.04 us
    pallas_call x1, Pallas kernels, local_aggregate(): pl.pallas_call(local_kernel, out_shape=pltpu.HBM(agg, F32), in_specs=[HBM...  3.5 us
    pallas_call x1, Pallas kernels, gather_sends(): pl.pallas_call(send_kernel, out_shape=[pltpu.HBM((per_list, tile, width),...  2.88 us
  transfers between devices with their start and end apart: 11, of which 3 were waited for; matrix products, arithmetic and copies ran while one was open for 0% of the time, Pallas kernels for 12%

profile of v8, /device:TPU:1, one launch (start us, length us, event | category | flops | bytes accessed | tf_op | source)
XLA Modules:
  0.0 76.1 jit_solution(11195993017586234089)
XLA Ops:
  0.6 2.9 %sends.1 = (bf16[4,128,128]{2,1,0:T(8,128)(2,1)}, bf16[4,128,128]{2,1,0:T(8,128)(2,1)}, bf16[4,128,128]{2,1,0:T(8,128)(2,1)}, bf16[4,128,128]{2,1,0:T(8,128)(2,1...) custom-call(s32[4,4]{1,0:T(4,128)} %send_hbm.3, s32[4]{0:T(128)} %hubs_hbm.3, ...), custom_call_target="tpu_custom_call" | custom-call | tf_op jit(solution)/shard_map/sends/pallas_call | solution.py:112
  3.5 15.7 %all-to-all-start = ((bf16[256,4,128]{2,1,0:T(4,128)(2,1)}), bf16[256,4,128]{2,1,0:T(4,128)(2,1)S(1)}, u32[]{:S(2)}, u32[]{:S(2)}) async-start(bf16[256,4,128]{2,1,0:T(4,128)(2,1)} %get-tuple-element.29), calls=%async_computation | async-start | bytes 524288 | tf_op jit(solution)/shard_map/all_to_all | solution.py:578
  19.2 2.2 %collective-permute-start = (bf16[4,128,128]{2,1,0:T(8,128)(2,1)}, bf16[4,128,128]{2,1,0:T(8,128)(2,1)S(1)}, u32[]{:S(2)}, u32[]{:S(2)}) collective-permute-start(bf16[4,128,128]{2,1,0:T(8,128)(2,1)} %get-tuple-element.25), channel_id=1, source_target_pairs={{0,1},{1,0},{2,3},{3,2},{4,5},{5,4},{6,7},{7,6},{8,9},{9,8},{10,11... | collective-permute-start | bytes 393224 | tf_op jit(solution)/shard_map/ppermute | solution.py:31
  21.4 0.0 collective-permute-start.1
  21.4 1.2 %collective-permute-start.2 = (bf16[4,128,128]{2,1,0:T(8,128)(2,1)}, bf16[4,128,128]{2,1,0:T(8,128)(2,1)S(1)}, u32[]{:S(2)}, u32[]{:S(2)}) collective-permute-start(bf16[4,128,128]{2,1,0:T(8,128)(2,1)} %get-tuple-element.27), channel_id=1, source_target_pairs={{0,2},{1,3},{2,0},{3,1},{4,6},{5,7},{6,4},{7,5},{8,10},{9,11},{10,... | collective-permute-start | bytes 393224 | tf_op jit(solution)/shard_map/ppermute | solution.py:31
  22.6 7.3 %collective-permute-start.3 = (bf16[4,128,128]{2,1,0:T(8,128)(2,1)}, bf16[4,128,128]{2,1,0:T(8,128)(2,1)S(1)}, u32[]{:S(2)}, u32[]{:S(2)}) collective-permute-start(bf16[4,128,128]{2,1,0:T(8,128)(2,1)} %get-tuple-element.28), channel_id=1, source_target_pairs={{0,254},{1,255},{2,4},{3,5},{4,2},{5,3},{6,8},{7,9},{8,6},{9,7},{1... | collective-permute-start | bytes 393224 | tf_op jit(solution)/shard_map/ppermute | solution.py:31
  30.0 3.5 %local_aggregate.1.refs_2_ = f32[4096,128]{1,0:T(8,128)} custom-call(s32[3,32]{1,0:T(4,128)} %bitcast.11, bf16[32,3,128,128]{3,2,1,0:T(8,128)(2,1)} %tiles_hbm.3, bf16[32,128,128]{2,1,0:T(8,128)(2,1)S(1)} %get-tuple-element.24.blocks), custom_call_target="tpu_custom_call" | custom-call | flops 402653184 | bytes 8388608 | tf_op jit(solution)/shard_map/local_aggregate/pallas_call | solution.py:171
  33.5 0.0 collective-permute-done.1.refs_5_
  33.5 0.0 collective-permute-done.2.refs_6_
  33.5 2.4 %collective-permute-done.3.refs_7_ = bf16[4,128,128]{2,1,0:T(8,128)(2,1)S(1)} collective-permute-done((bf16[4,128,128]{2,1,0:T(8,128)(2,1)}, bf16[4,128,128]{2,1,0:T(8,128)(2,1)S(1)}, u32[]{:S(2)}, u32[]{:S(2)}) %collective-permute-start.3) | collective-permute-done | bytes 131104 | tf_op jit(solution)/shard_map/ppermute | solution.py:31
  35.9 0.0 all-to-all-done
  35.9 9.8 %layer.1 = (bf16[4096,256]{1,0:T(8,128)(2,1)}, bf16[4096,256]{1,0:T(8,128)(2,1)}, bf16[32,128,128]{2,1,0:T(8,128)(2,1)}, bf16[4,128,128]{2,1,0:T(8,128)(2,1)}, b...) custom-call(s32[3,32]{1,0:T(4,128)} %bitcast.13, ...), custom_call_target="tpu_custom_call" | custom-call | flops 2415919104 | bytes 14680064 | tf_op jit(solution)/shard_map/layer/pallas_call | solution.py:346
  45.7 3.6 %collective-permute-start.4 = (bf16[128,8,128]{2,1,0:T(8,128)(2,1)}, bf16[128,8,128]{2,1,0:T(8,128)(2,1)S(1)}, u32[]{:S(2)}, u32[]{:S(2)}) collective-permute-start(bf16[128,8,128]{2,1,0:T(8,128)(2,1)} %get-tuple-element.34), channel_id=1, source_target_pairs={{0,1},{1,0},{2,3},{3,2},{4,5},{5,4},{6,7},{7,6},{8,9},{9,8},{10,11... | collective-permute-start | bytes 786440 | tf_op jit(solution)/shard_map/ppermute | solution.py:31
  49.3 1.4 %collective-permute-done.4.theirs_any = bf16[128,8,128]{2,1,0:T(8,128)(2,1)S(1)} collective-permute-done((bf16[128,8,128]{2,1,0:T(8,128)(2,1)}, bf16[128,8,128]{2,1,0:T(8,128)(2,1)S(1)}, u32[]{:S(2)}, u32[]{:S(2)}) %collective-permute-start.4) | collective-permute-done | bytes 262176 | tf_op jit(solution)/shard_map/ppermute | solution.py:31
  50.7 0.8 %add_pieces.1 = bf16[128,8,128]{2,1,0:T(8,128)(2,1)} custom-call(f32[128,8,128]{2,1,0:T(8,128)S(1)} %get-tuple-element.33.mine, bf16[128,8,128]{2,1,0:T(8,128)(2,1)S(1)} %collective-permute-done.4.theirs_any), custom_call_target="tpu_custom_call" | custom-call | tf_op jit(solution)/shard_map/add_pieces/pallas_call | solution.py:412
  51.5 6.2 %all-to-all-start.1 = ((bf16[128,8,128]{2,1,0:T(8,128)(2,1)}), bf16[128,8,128]{2,1,0:T(8,128)(2,1)S(1)}, u32[]{:S(2)}, u32[]{:S(2)}) async-start(bf16[128,8,128]{2,1,0:T(8,128)(2,1)} %add_pieces.1), calls=%async_computation.1 | async-start | bytes 524288 | tf_op jit(solution)/shard_map/all_to_all | solution.py:597
  57.6 0.6 collective-permute-start.5
  58.3 0.8 %collective-permute-start.6 = (bf16[4,128,128]{2,1,0:T(8,128)(2,1)}, bf16[4,128,128]{2,1,0:T(8,128)(2,1)S(1)}, u32[]{:S(2)}, u32[]{:S(2)}) collective-permute-start(bf16[4,128,128]{2,1,0:T(8,128)(2,1)} %get-tuple-element.36), channel_id=1, source_target_pairs={{0,255},{1,2},{2,1},{3,4},{4,3},{5,6},{6,5},{7,8},{8,7},{9,10},{10... | collective-permute-start | bytes 393224 | tf_op jit(solution)/shard_map/ppermute | solution.py:31
  59.1 1.2 %collective-permute-start.7 = (bf16[4,128,128]{2,1,0:T(8,128)(2,1)}, bf16[4,128,128]{2,1,0:T(8,128)(2,1)S(1)}, u32[]{:S(2)}, u32[]{:S(2)}) collective-permute-start(bf16[4,128,128]{2,1,0:T(8,128)(2,1)} %get-tuple-element.37), channel_id=1, source_target_pairs={{0,2},{1,3},{2,0},{3,1},{4,6},{5,7},{6,4},{7,5},{8,10},{9,11},{10,... | collective-permute-start | bytes 393224 | tf_op jit(solution)/shard_map/ppermute | solution.py:31
  60.3 6.5 %collective-permute-start.8 = (bf16[4,128,128]{2,1,0:T(8,128)(2,1)}, bf16[4,128,128]{2,1,0:T(8,128)(2,1)S(1)}, u32[]{:S(2)}, u32[]{:S(2)}) collective-permute-start(bf16[4,128,128]{2,1,0:T(8,128)(2,1)} %get-tuple-element.38), channel_id=1, source_target_pairs={{0,254},{1,255},{2,4},{3,5},{4,2},{5,3},{6,8},{7,9},{8,6},{9,7},{1... | collective-permute-start | bytes 393224 | tf_op jit(solution)/shard_map/ppermute | solution.py:31
  66.7 5.3 %local_backward.1._ = f32[32,128,128]{2,1,0:T(8,128)S(1)} custom-call(s32[3,32]{1,0:T(4,128)} %bitcast.12, bf16[128,256]{1,0:T(8,128)(2,1)} %weight_hbm.1, bf16[32,3,128,128]{3,2,1,0:T(8,128)(2,1)} %tiles_hbm.3, bf16[32,128,128]{2,1,0:T(8,128)(2,1)} %get-tuple-element.31.d_hbm, bf16[4096,256]{1,0:T(8,128)(2,1)} %get-tuple-element.32.p_hbm), custom_call_target="tpu_custom_call" | custom-call | flops 671088640 | bytes 8388608 | tf_op jit(solution)/shard_map/local_backward/pallas_call | solution.py:472
  72.1 0.0 collective-permute-done.5.refs_0_
  72.1 1.2 %collective-permute-done.8.refs_3_ = bf16[4,128,128]{2,1,0:T(8,128)(2,1)S(1)} collective-permute-done((bf16[4,128,128]{2,1,0:T(8,128)(2,1)}, bf16[4,128,128]{2,1,0:T(8,128)(2,1)S(1)}, u32[]{:S(2)}, u32[]{:S(2)}) %collective-permute-start.8) | collective-permute-done | bytes 131104 | tf_op jit(solution)/shard_map/ppermute | solution.py:31
  73.3 2.7 %collect.1 = (f32[32,128,128]{2,1,0:T(8,128)S(1)}, bf16[4096,128]{1,0:T(8,128)(2,1)}, f32[1,128]{1,0:T(1,128)}, f32[1,128]{1,0:T(1,128)}, f32[1,128]{1,0:T(1,128)}) custom-call(s32[4,4]{1,0:T(4,128)} %send_hbm.3, s32[4]{0:T(128)} %hubs_hbm.3, f32[32,128,128]{2,1,0:T(8,128)S(1)} %local_backward.1._, ...), custom_call_target="tpu_custom_call", output_to_operand_aliasing={{0}: (2, {})} | custom-call | tf_op jit(solution)/shard_map/collect/pallas_call | solution.py:538
  (4 shorter events, 0.0 us)
Async XLA Ops:
  3.5 32.4 %all-to-all-start = ((bf16[256,4,128]{2,1,0:T(4,128)(2,1)}), bf16[256,4,128]{2,1,0:T(4,128)(2,1)S(1)}, u32[]{:S(2)}, u32[]{:S(2)}) async-start(bf16[256,4,128]{2,1,0:T(4,128)(2,1)} %get-tuple-element.29), calls=%async_computation | async-start | bytes 524288 | tf_op jit(solution)/shard_map/all_to_all | solution.py:578
  19.2 14.3 %collective-permute-start = (bf16[4,128,128]{2,1,0:T(8,128)(2,1)}, bf16[4,128,128]{2,1,0:T(8,128)(2,1)S(1)}, u32[]{:S(2)}, u32[]{:S(2)}) collective-permute-start(bf16[4,128,128]{2,1,0:T(8,128)(2,1)} %get-tuple-element.25), channel_id=1, source_target_pairs={{0,1},{1,0},{2,3},{3,2},{4,5},{5,4},{6,7},{7,6},{8,9},{9,8},{10,11... | collective-permute-start | bytes 393224 | tf_op jit(solution)/shard_map/ppermute | solution.py:31
  21.4 12.1 %collective-permute-start.1 = (bf16[4,128,128]{2,1,0:T(8,128)(2,1)}, bf16[4,128,128]{2,1,0:T(8,128)(2,1)S(1)}, u32[]{:S(2)}, u32[]{:S(2)}) collective-permute-start(bf16[4,128,128]{2,1,0:T(8,128)(2,1)} %get-tuple-element.26), channel_id=1, source_target_pairs={{0,255},{1,2},{2,1},{3,4},{4,3},{5,6},{6,5},{7,8},{8,7},{9,10},{10... | collective-permute-start | bytes 393224 | tf_op jit(solution)/shard_map/ppermute | solution.py:31
  21.4 12.1 %collective-permute-start.2 = (bf16[4,128,128]{2,1,0:T(8,128)(2,1)}, bf16[4,128,128]{2,1,0:T(8,128)(2,1)S(1)}, u32[]{:S(2)}, u32[]{:S(2)}) collective-permute-start(bf16[4,128,128]{2,1,0:T(8,128)(2,1)} %get-tuple-element.27), channel_id=1, source_target_pairs={{0,2},{1,3},{2,0},{3,1},{4,6},{5,7},{6,4},{7,5},{8,10},{9,11},{10,... | collective-permute-start | bytes 393224 | tf_op jit(solution)/shard_map/ppermute | solution.py:31
  22.6 13.3 %collective-permute-start.3 = (bf16[4,128,128]{2,1,0:T(8,128)(2,1)}, bf16[4,128,128]{2,1,0:T(8,128)(2,1)S(1)}, u32[]{:S(2)}, u32[]{:S(2)}) collective-permute-start(bf16[4,128,128]{2,1,0:T(8,128)(2,1)} %get-tuple-element.28), channel_id=1, source_target_pairs={{0,254},{1,255},{2,4},{3,5},{4,2},{5,3},{6,8},{7,9},{8,6},{9,7},{1... | collective-permute-start | bytes 393224 | tf_op jit(solution)/shard_map/ppermute | solution.py:31
  45.7 5.0 %collective-permute-start.4 = (bf16[128,8,128]{2,1,0:T(8,128)(2,1)}, bf16[128,8,128]{2,1,0:T(8,128)(2,1)S(1)}, u32[]{:S(2)}, u32[]{:S(2)}) collective-permute-start(bf16[128,8,128]{2,1,0:T(8,128)(2,1)} %get-tuple-element.34), channel_id=1, source_target_pairs={{0,1},{1,0},{2,3},{3,2},{4,5},{5,4},{6,7},{7,6},{8,9},{9,8},{10,11... | collective-permute-start | bytes 786440 | tf_op jit(solution)/shard_map/ppermute | solution.py:31
  51.5 21.9 %all-to-all-start.1 = ((bf16[128,8,128]{2,1,0:T(8,128)(2,1)}), bf16[128,8,128]{2,1,0:T(8,128)(2,1)S(1)}, u32[]{:S(2)}, u32[]{:S(2)}) async-start(bf16[128,8,128]{2,1,0:T(8,128)(2,1)} %add_pieces.1), calls=%async_computation.1 | async-start | bytes 524288 | tf_op jit(solution)/shard_map/all_to_all | solution.py:597
  57.6 14.4 %collective-permute-start.5 = (bf16[4,128,128]{2,1,0:T(8,128)(2,1)}, bf16[4,128,128]{2,1,0:T(8,128)(2,1)S(1)}, u32[]{:S(2)}, u32[]{:S(2)}) collective-permute-start(bf16[4,128,128]{2,1,0:T(8,128)(2,1)} %get-tuple-element.35), channel_id=1, source_target_pairs={{0,1},{1,0},{2,3},{3,2},{4,5},{5,4},{6,7},{7,6},{8,9},{9,8},{10,11... | collective-permute-start | bytes 393224 | tf_op jit(solution)/shard_map/ppermute | solution.py:31
  58.3 13.8 %collective-permute-start.6 = (bf16[4,128,128]{2,1,0:T(8,128)(2,1)}, bf16[4,128,128]{2,1,0:T(8,128)(2,1)S(1)}, u32[]{:S(2)}, u32[]{:S(2)}) collective-permute-start(bf16[4,128,128]{2,1,0:T(8,128)(2,1)} %get-tuple-element.36), channel_id=1, source_target_pairs={{0,255},{1,2},{2,1},{3,4},{4,3},{5,6},{6,5},{7,8},{8,7},{9,10},{10... | collective-permute-start | bytes 393224 | tf_op jit(solution)/shard_map/ppermute | solution.py:31
  59.1 13.0 %collective-permute-start.7 = (bf16[4,128,128]{2,1,0:T(8,128)(2,1)}, bf16[4,128,128]{2,1,0:T(8,128)(2,1)S(1)}, u32[]{:S(2)}, u32[]{:S(2)}) collective-permute-start(bf16[4,128,128]{2,1,0:T(8,128)(2,1)} %get-tuple-element.37), channel_id=1, source_target_pairs={{0,2},{1,3},{2,0},{3,1},{4,6},{5,7},{6,4},{7,5},{8,10},{9,11},{10,... | collective-permute-start | bytes 393224 | tf_op jit(solution)/shard_map/ppermute | solution.py:31
  60.3 13.1 %collective-permute-start.8 = (bf16[4,128,128]{2,1,0:T(8,128)(2,1)}, bf16[4,128,128]{2,1,0:T(8,128)(2,1)S(1)}, u32[]{:S(2)}, u32[]{:S(2)}) collective-permute-start(bf16[4,128,128]{2,1,0:T(8,128)(2,1)} %get-tuple-element.38), channel_id=1, source_target_pairs={{0,254},{1,255},{2,4},{3,5},{4,2},{5,3},{6,8},{7,9},{8,6},{9,7},{1... | collective-permute-start | bytes 393224 | tf_op jit(solution)/shard_map/ppermute | solution.py:31

commit v9 on v8

--- a/solution.py
+++ b/solution.py
@@ -75,7 +75,7 @@
 def send_kernel(send_hbm, hubs_hbm, blocks_hbm, *refs):
     lists, per_list = send_hbm.shape
     outs, refs = refs[:lists], refs[lists:]
-    hub_out, blocks, send, hubs, sem_in, sems = refs
+    hub_out, blocks, send, hubs, spread, sem_in, sems = refs
     owned = hubs.shape[0]
     count, tile, width = blocks.shape
     pairs = [(send_hbm, send), (hubs_hbm, hubs)]
@@ -85,6 +85,7 @@
     loads = [pltpu.make_async_copy(*p, sem_in.at[n]) for n, p in enumerate(pairs)]
     start(loads)
     wait(loads)
+    place = lax.broadcasted_iota(jnp.int32, (GROUP, width), 0)
     moves = []
     for way, j in enumerate(lists_of_ways()):
         for h in range(per_list):
@@ -94,7 +95,6 @@
                 )
             )
     start(moves)
-    place = lax.broadcasted_iota(jnp.int32, (GROUP, width), 0)
     rows = []
     for i in range(owned):
         row = hubs[i]
@@ -102,8 +102,11 @@
         near = blocks[row // tile, pl.ds(base, GROUP), :].astype(F32)
         chosen = jnp.where(place == lax.rem(row, GROUP), near, 0.0)
         rows.append(jnp.sum(chosen, 0, keepdims=True))
-    hub_out[...] = jnp.broadcast_to(jnp.concatenate(rows, 0).astype(BF16)[None], hub_out.shape)
+    spread[...] = jnp.broadcast_to(jnp.concatenate(rows, 0).astype(BF16)[None], spread.shape)
+    last = pltpu.make_async_copy(spread, hub_out, sems.at[lists * per_list])
+    last.start()
     wait(moves)
+    last.wait()
 
 
 def gather_sends(send, hubs, blocks, parts):
@@ -113,16 +116,17 @@
         send_kernel,
         out_shape=[pltpu.HBM((per_list, tile, width), BF16)] * lists
         + [
-            jax.ShapeDtypeStruct((parts, hubs.shape[0], width), BF16),
+            pltpu.HBM((parts, hubs.shape[0], width), BF16),
             pltpu.VMEM(blocks.shape, BF16),
         ],
         in_specs=[HBM_SPEC] * 3,
-        out_specs=[HBM_SPEC] * lists + [VMEM_SPEC, VMEM_SPEC],
+        out_specs=[HBM_SPEC] * lists + [HBM_SPEC, VMEM_SPEC],
         scratch_shapes=[
             pltpu.SMEM(send.shape, jnp.int32),
             pltpu.SMEM(hubs.shape, jnp.int32),
+            pltpu.VMEM((parts, hubs.shape[0], width), BF16),
             pltpu.SemaphoreType.DMA((4,)),
-            pltpu.SemaphoreType.DMA((lists * per_list,)),
+            pltpu.SemaphoreType.DMA((lists * per_list + 1,)),
         ],
         compiler_params=params(),
         name="sends",
@@ -398,30 +402,44 @@
     )
 
 
-def add_kernel(mine, theirs_any, out_hbm, theirs, out, sems):
-    load = pltpu.make_async_copy(theirs_any, theirs, sems.at[0])
-    load.start()
-    load.wait()
+def add_kernel(mine, theirs_any, relay, *refs):
+    backs, (out_hbm, *joined), refs = refs[:2], refs[2:5], refs[5:]
+    theirs, out, both, sem_in, sem_out = refs
+    per_list = relay.shape[0]
+    first, second = pl.ds(0, per_list), pl.ds(per_list, per_list)
+    pairs = [(theirs_any, theirs)]
+    for n in range(2):
+        pairs += [(backs[n], both.at[n, first]), (relay, both.at[n, second])]
+    loads = [pltpu.make_async_copy(*p, sem_in.at[n]) for n, p in enumerate(pairs)]
+    start(loads)
+    loads[0].wait()
     out[...] = (mine[...] + theirs[...].astype(F32)).astype(BF16)
-    save = pltpu.make_async_copy(out, out_hbm, sems.at[1])
-    save.start()
-    save.wait()
-
-
-def add_pieces(mine, theirs):
+    saves = [pltpu.make_async_copy(out, out_hbm, sem_out.at[0])]
+    saves[0].start()
+    wait(loads[1:])
+    for n in range(2):
+        saves.append(pltpu.make_async_copy(both.at[n], joined[n], sem_out.at[1 + n]))
+        saves[-1].start()
+    wait(saves)
+
+
+def add_pieces(mine, theirs, relay, backs):
+    joined = (2 * relay.shape[0],) + relay.shape[1:]
     return pl.pallas_call(
         add_kernel,
-        out_shape=pltpu.HBM(theirs.shape, BF16),
-        in_specs=[VMEM_SPEC, ANY_SPEC],
-        out_specs=HBM_SPEC,
+        out_shape=[pltpu.HBM(theirs.shape, BF16)] + [pltpu.HBM(joined, BF16)] * 2,
+        in_specs=[VMEM_SPEC] + [ANY_SPEC] * 4,
+        out_specs=[HBM_SPEC] * 3,
         scratch_shapes=[
             pltpu.VMEM(theirs.shape, BF16),
             pltpu.VMEM(theirs.shape, BF16),
-            pltpu.SemaphoreType.DMA((2,)),
+            pltpu.VMEM((2,) + joined, BF16),
+            pltpu.SemaphoreType.DMA((5,)),
+            pltpu.SemaphoreType.DMA((3,)),
         ],
         compiler_params=params(),
         name="add_pieces",
-    )(vmem(mine), theirs)
+    )(vmem(mine), theirs, relay, *[hbm(b) for b in backs])
 
 
 def back_kernel(
@@ -495,20 +513,26 @@
 
 def collect_kernel(send_hbm, hubs_hbm, _, pieces_any, *refs):
     lists, per_list = send_hbm.shape
-    halos_any, refs = refs[:lists], refs[lists:]
+    near_any, *chips_any = refs[:3]
+    refs = refs[3:]
     total, out, g_self, g_neigh, g_bias = refs[:5]
     send, hubs, halos, pieces, turned, sem_in, sem_out = refs[5:]
     count, width, tile = total.shape
     owned = hubs.shape[0]
     pairs = [(send_hbm, send), (hubs_hbm, hubs)]
-    pairs += [(halos_any[way], halos.at[way]) for way in range(lists)]
-    pairs.append((pieces_any, pieces))
+    first, second = pl.ds(0, per_list), pl.ds(per_list, per_list)
+    pairs += [(pieces_any, pieces), (near_any, halos.at[0])]
+    for n in range(2):
+        pairs.append((chips_any[n].at[first], halos.at[2 + n]))
+        pairs.append((chips_any[n].at[second], halos.at[4 + n]))
     loads = [pltpu.make_async_copy(*p, sem_in.at[n]) for n, p in enumerate(pairs)]
     start(loads)
     wait(loads)
-    for way, j in enumerate(lists_of_ways()):
+    ways = lists_of_ways()
+    relayed = jnp.where((ways[0] + ways[2]) % 2 == 1, 4, 5)
+    for n, j in zip((0, relayed, 2, 3), ways):
         for h in range(per_list):
-            total[send[j, h]] += halos[way, h].astype(F32)
+            total[send[j, h]] += halos[n, h].astype(F32)
     summed = jnp.sum(pieces[...].astype(F32), 0)
     g_self[...] = summed[owned : owned + 1, :]
     g_neigh[...] = summed[owned + 1 : owned + 2, :]
@@ -533,21 +557,20 @@
 
 def collect(send, hubs, grad, pieces, halos):
     count, width, tile = grad.shape
-    lists = len(halos)
     line = jax.ShapeDtypeStruct((1, width), F32)
     return pl.pallas_call(
         collect_kernel,
         out_shape=[pltpu.VMEM(grad.shape, F32), pltpu.HBM((count * tile, width), BF16)]
         + [line] * 3,
-        in_specs=[HBM_SPEC] * 2 + [VMEM_SPEC] + [ANY_SPEC] * (1 + lists),
+        in_specs=[HBM_SPEC] * 2 + [VMEM_SPEC] + [ANY_SPEC] * 4,
         out_specs=[VMEM_SPEC, HBM_SPEC] + [VMEM_SPEC] * 3,
         scratch_shapes=[
             pltpu.SMEM(send.shape, jnp.int32),
             pltpu.SMEM(hubs.shape, jnp.int32),
-            pltpu.VMEM((lists,) + halos[0].shape, BF16),
+            pltpu.VMEM((6,) + halos[0].shape, BF16),
             pltpu.VMEM(pieces.shape, BF16),
             pltpu.VMEM((count * tile, width), BF16),
-            pltpu.SemaphoreType.DMA((3 + lists,)),
+            pltpu.SemaphoreType.DMA((8,)),
             pltpu.SemaphoreType.DMA((4,)),
         ],
         input_output_aliases={2: 0},
@@ -592,10 +615,10 @@
         parts,
     )
     *backs, mine, theirs = rest
-    packed = add_pieces(mine, swapped(theirs, 0))
+    packed, *joined = add_pieces(mine, swapped(theirs, 0), swapped(backs[1], 0), backs[2:])
     same_core = [list(range(c, parts, 2)) for c in range(2)]
     pieces = lax.all_to_all(packed, "dom", 0, 0, axis_index_groups=same_core)
-    returned = [swapped(b, way) for way, b in enumerate(backs)]
+    returned = [swapped(x, way) for x, way in zip([backs[0]] + joined, (0, 2, 3))]
     grad_t = local_backward(local_src.T, local_tiles, d_pre, d_agg, w_self)
     grad, g_self, g_neigh, g_bias = collect(send_blocks, hub_rows, grad_t, pieces, returned)
     return (hidden, grad, g_self.reshape(width, 1), g_neigh.reshape(width, 1), g_bias[0, :1])

time: 76.3 us -> 79.4 us (1.041)
  waiting for transfers between devices: 5.05 us -> 6.89 us
  Pallas kernels: 25 us -> 25.8 us
    ppermute x9, waiting for transfers between devices: 5.04 us -> 6.88 us  [swapped(): lax.ppermute(block, 'dom', [(i, partner(i, way, n)) for i in range(n)])]
    pallas_call x1, Pallas kernels: 0.78 us -> 1.98 us  [add_pieces(): pl.pallas_call(add_kernel, out_shape=[pltpu.HBM(theirs.shape, BF16)] + [p...]
  transfers between devices with their start and end apart: 11 -> 11, of which waited for: 3 -> 3; matrix products, arithmetic and copies ran while one was open for 0% -> 0% of each run, Pallas kernels for 12% -> 11%
where the time goes in v9:
time: 79.4 us; the launch traced here: 79.1 us
  starting transfers between devices  45.7 us (58%)
  Pallas kernels  25.8 us (32%)
  waiting for transfers between devices  6.89 us (9%)
    ppermute x9, starting transfers between devices, swapped(): lax.ppermute(block, 'dom', [(i, partner(i, way, n)) for i in range(n)])  23.9 us
    all_to_all x1, starting transfers between devices, shards(): hub_all = lax.all_to_all(hub_mine, 'dom', 0, 0)  15.7 us
    pallas_call x1, Pallas kernels, layer(): pl.pallas_call(layer_kernel, out_shape=[pltpu.HBM((nodes, units), BF16),...  9.75 us
    ppermute x9, waiting for transfers between devices, swapped(): lax.ppermute(block, 'dom', [(i, partner(i, way, n)) for i in range(n)])  6.88 us
    all_to_all x1, starting transfers between devices, shards(): pieces = lax.all_to_all(packed, 'dom', 0, 0, axis_index_groups=same_core)  6.17 us
    pallas_call x1, Pallas kernels, local_backward(): pl.pallas_call(back_kernel, out_shape=pltpu.VMEM((count, width, tile), F3...  5.35 us
    pallas_call x1, Pallas kernels, local_aggregate(): pl.pallas_call(local_kernel, out_shape=pltpu.HBM(agg, F32), in_specs=[HBM...  3.51 us
    pallas_call x1, Pallas kernels, collect(): pl.pallas_call(collect_kernel, out_shape=[pltpu.VMEM(grad.shape, F32), pl...  2.91 us
  transfers between devices with their start and end apart: 11, of which 3 were waited for; matrix products, arithmetic and copies ran while one was open for 0% of the time, Pallas kernels for 11%

profile of v9, /device:TPU:1, one launch (start us, length us, event | category | flops | bytes accessed | tf_op | source)
XLA Modules:
  0.0 79.1 jit_solution(16138326148894925089)
XLA Ops:
  0.6 2.3 %sends.1 = (bf16[4,128,128]{2,1,0:T(8,128)(2,1)}, bf16[4,128,128]{2,1,0:T(8,128)(2,1)}, bf16[4,128,128]{2,1,0:T(8,128)(2,1)}, bf16[4,128,128]{2,1,0:T(8,128)(2,1...) custom-call(s32[4,4]{1,0:T(4,128)} %send_hbm.3, s32[4]{0:T(128)} %hubs_hbm.3, ...), custom_call_target="tpu_custom_call" | custom-call | tf_op jit(solution)/shard_map/sends/pallas_call | solution.py:115
  2.9 15.7 %all-to-all-start = ((bf16[256,4,128]{2,1,0:T(4,128)(2,1)}), bf16[256,4,128]{2,1,0:T(4,128)(2,1)S(1)}, u32[]{:S(2)}, u32[]{:S(2)}) async-start(bf16[256,4,128]{2,1,0:T(4,128)(2,1)} %get-tuple-element.32), calls=%async_computation | async-start | bytes 524288 | tf_op jit(solution)/shard_map/all_to_all | solution.py:601
  18.6 2.2 %collective-permute-start = (bf16[4,128,128]{2,1,0:T(8,128)(2,1)}, bf16[4,128,128]{2,1,0:T(8,128)(2,1)S(1)}, u32[]{:S(2)}, u32[]{:S(2)}) collective-permute-start(bf16[4,128,128]{2,1,0:T(8,128)(2,1)} %get-tuple-element.28), channel_id=1, source_target_pairs={{0,1},{1,0},{2,3},{3,2},{4,5},{5,4},{6,7},{7,6},{8,9},{9,8},{10,11... | collective-permute-start | bytes 393224 | tf_op jit(solution)/shard_map/ppermute | solution.py:31
  20.8 1.2 %collective-permute-start.2 = (bf16[4,128,128]{2,1,0:T(8,128)(2,1)}, bf16[4,128,128]{2,1,0:T(8,128)(2,1)S(1)}, u32[]{:S(2)}, u32[]{:S(2)}) collective-permute-start(bf16[4,128,128]{2,1,0:T(8,128)(2,1)} %get-tuple-element.30), channel_id=1, source_target_pairs={{0,2},{1,3},{2,0},{3,1},{4,6},{5,7},{6,4},{7,5},{8,10},{9,11},{10,... | collective-permute-start | bytes 393224 | tf_op jit(solution)/shard_map/ppermute | solution.py:31
  22.1 7.3 %collective-permute-start.3 = (bf16[4,128,128]{2,1,0:T(8,128)(2,1)}, bf16[4,128,128]{2,1,0:T(8,128)(2,1)S(1)}, u32[]{:S(2)}, u32[]{:S(2)}) collective-permute-start(bf16[4,128,128]{2,1,0:T(8,128)(2,1)} %get-tuple-element.31), channel_id=1, source_target_pairs={{0,254},{1,255},{2,4},{3,5},{4,2},{5,3},{6,8},{7,9},{8,6},{9,7},{1... | collective-permute-start | bytes 393224 | tf_op jit(solution)/shard_map/ppermute | solution.py:31
  29.4 3.5 %local_aggregate.1.refs_2_ = f32[4096,128]{1,0:T(8,128)} custom-call(s32[3,32]{1,0:T(4,128)} %bitcast.11, bf16[32,3,128,128]{3,2,1,0:T(8,128)(2,1)} %tiles_hbm.3, bf16[32,128,128]{2,1,0:T(8,128)(2,1)S(1)} %get-tuple-element.27.blocks), custom_call_target="tpu_custom_call" | custom-call | flops 402653184 | bytes 8388608 | tf_op jit(solution)/shard_map/local_aggregate/pallas_call | solution.py:175
  32.9 0.0 collective-permute-done.refs_4_
  32.9 0.0 collective-permute-done.1.refs_5_
  32.9 2.4 %collective-permute-done.3.refs_7_ = bf16[4,128,128]{2,1,0:T(8,128)(2,1)S(1)} collective-permute-done((bf16[4,128,128]{2,1,0:T(8,128)(2,1)}, bf16[4,128,128]{2,1,0:T(8,128)(2,1)S(1)}, u32[]{:S(2)}, u32[]{:S(2)}) %collective-permute-start.3) | collective-permute-done | bytes 131104 | tf_op jit(solution)/shard_map/ppermute | solution.py:31
  35.4 0.0 all-to-all-done
  35.4 9.8 %layer.1 = (bf16[4096,256]{1,0:T(8,128)(2,1)}, bf16[4096,256]{1,0:T(8,128)(2,1)}, bf16[32,128,128]{2,1,0:T(8,128)(2,1)}, bf16[4,128,128]{2,1,0:T(8,128)(2,1)}, b...) custom-call(s32[3,32]{1,0:T(4,128)} %bitcast.13, ...), custom_call_target="tpu_custom_call" | custom-call | flops 2415919104 | bytes 14680064 | tf_op jit(solution)/shard_map/layer/pallas_call | solution.py:350
  45.1 3.6 %collective-permute-start.4 = (bf16[128,8,128]{2,1,0:T(8,128)(2,1)}, bf16[128,8,128]{2,1,0:T(8,128)(2,1)S(1)}, u32[]{:S(2)}, u32[]{:S(2)}) collective-permute-start(bf16[128,8,128]{2,1,0:T(8,128)(2,1)} %get-tuple-element.37), channel_id=1, source_target_pairs={{0,1},{1,0},{2,3},{3,2},{4,5},{5,4},{6,7},{7,6},{8,9},{9,8},{10,11... | collective-permute-start | bytes 786440 | tf_op jit(solution)/shard_map/ppermute | solution.py:31
  48.7 0.1 collective-permute-start.5
  48.8 1.5 %collective-permute-done.5.relay = bf16[4,128,128]{2,1,0:T(8,128)(2,1)S(1)} collective-permute-done((bf16[4,128,128]{2,1,0:T(8,128)(2,1)}, bf16[4,128,128]{2,1,0:T(8,128)(2,1)S(1)}, u32[]{:S(2)}, u32[]{:S(2)}) %collective-permute-start.5) | collective-permute-done | bytes 131104 | tf_op jit(solution)/shard_map/ppermute | solution.py:31
  50.3 0.0 collective-permute-done.4.theirs_any
  50.3 2.0 %add_pieces.1 = (bf16[128,8,128]{2,1,0:T(8,128)(2,1)}, bf16[8,128,128]{2,1,0:T(8,128)(2,1)}, bf16[8,128,128]{2,1,0:T(8,128)(2,1)}) custom-call(f32[128,8,128]{2,1,0:T(8,128)S(1)} %get-tuple-element.36.mine, bf16[128,8,128]{2,1,0:T(8,128)(2,1)S(1)} %collective-permute-done.4.theirs_any, bf16[4,128,128]{2,1,0:T(8,128)(2,1)S(1)} %collective-permute-done.5.relay, ...), custom_call_target="tpu_custom_call" | custom-call | tf_op jit(solution)/shard_map/add_pieces/pallas_call | solution.py:428
  52.3 6.2 %all-to-all-start.1 = ((bf16[128,8,128]{2,1,0:T(8,128)(2,1)}), bf16[128,8,128]{2,1,0:T(8,128)(2,1)S(1)}, u32[]{:S(2)}, u32[]{:S(2)}) async-start(bf16[128,8,128]{2,1,0:T(8,128)(2,1)} %get-tuple-element.41), calls=%async_computation.1 | async-start | bytes 524288 | tf_op jit(solution)/shard_map/all_to_all | solution.py:620
  58.5 0.5 collective-permute-start.7
  59.0 7.5 %collective-permute-start.8 = (bf16[8,128,128]{2,1,0:T(8,128)(2,1)}, bf16[8,128,128]{2,1,0:T(8,128)(2,1)S(1)}, u32[]{:S(2)}, u32[]{:S(2)}) collective-permute-start(bf16[8,128,128]{2,1,0:T(8,128)(2,1)} %get-tuple-element.44), channel_id=1, source_target_pairs={{0,254},{1,255},{2,4},{3,5},{4,2},{5,3},{6,8},{7,9},{8,6},{9,7},{1... | collective-permute-start | bytes 786440 | tf_op jit(solution)/shard_map/ppermute | solution.py:31
  66.5 1.4 %collective-permute-start.6 = (bf16[4,128,128]{2,1,0:T(8,128)(2,1)}, bf16[4,128,128]{2,1,0:T(8,128)(2,1)S(1)}, u32[]{:S(2)}, u32[]{:S(2)}) collective-permute-start(bf16[4,128,128]{2,1,0:T(8,128)(2,1)} %get-tuple-element.42), channel_id=1, source_target_pairs={{0,1},{1,0},{2,3},{3,2},{4,5},{5,4},{6,7},{7,6},{8,9},{9,8},{10,11... | collective-permute-start | bytes 393224 | tf_op jit(solution)/shard_map/ppermute | solution.py:31
  67.8 5.4 %local_backward.1._ = f32[32,128,128]{2,1,0:T(8,128)S(1)} custom-call(s32[3,32]{1,0:T(4,128)} %bitcast.12, bf16[128,256]{1,0:T(8,128)(2,1)} %weight_hbm.1, bf16[32,3,128,128]{3,2,1,0:T(8,128)(2,1)} %tiles_hbm.3, bf16[32,128,128]{2,1,0:T(8,128)(2,1)} %get-tuple-element.34.d_hbm, bf16[4096,256]{1,0:T(8,128)(2,1)} %get-tuple-element.35.p_hbm), custom_call_target="tpu_custom_call" | custom-call | flops 671088640 | bytes 8388608 | tf_op jit(solution)/shard_map/local_backward/pallas_call | solution.py:490
  73.2 0.0 collective-permute-done.7.refs_1_
  73.2 3.0 %collective-permute-done.8.refs_2_ = bf16[8,128,128]{2,1,0:T(8,128)(2,1)S(1)} collective-permute-done((bf16[8,128,128]{2,1,0:T(8,128)(2,1)}, bf16[8,128,128]{2,1,0:T(8,128)(2,1)S(1)}, u32[]{:S(2)}, u32[]{:S(2)}) %collective-permute-start.8) | collective-permute-done | bytes 262176 | tf_op jit(solution)/shard_map/ppermute | solution.py:31
  76.2 2.9 %collect.1 = (f32[32,128,128]{2,1,0:T(8,128)S(1)}, bf16[4096,128]{1,0:T(8,128)(2,1)}, f32[1,128]{1,0:T(1,128)}, f32[1,128]{1,0:T(1,128)}, f32[1,128]{1,0:T(1,128)}) custom-call(s32[4,4]{1,0:T(4,128)} %send_hbm.3, s32[4]{0:T(128)} %hubs_hbm.3, f32[32,128,128]{2,1,0:T(8,128)S(1)} %local_backward.1._, ...), custom_call_target="tpu_custom_call", output_to_operand_aliasing={{0}: (2, {})} | custom-call | tf_op jit(solution)/shard_map/collect/pallas_call | solution.py:561
  (4 shorter events, 0.0 us)
Async XLA Ops:
  2.9 32.4 %all-to-all-start = ((bf16[256,4,128]{2,1,0:T(4,128)(2,1)}), bf16[256,4,128]{2,1,0:T(4,128)(2,1)S(1)}, u32[]{:S(2)}, u32[]{:S(2)}) async-start(bf16[256,4,128]{2,1,0:T(4,128)(2,1)} %get-tuple-element.32), calls=%async_computation | async-start | bytes 524288 | tf_op jit(solution)/shard_map/all_to_all | solution.py:601
  18.6 14.3 %collective-permute-start = (bf16[4,128,128]{2,1,0:T(8,128)(2,1)}, bf16[4,128,128]{2,1,0:T(8,128)(2,1)S(1)}, u32[]{:S(2)}, u32[]{:S(2)}) collective-permute-start(bf16[4,128,128]{2,1,0:T(8,128)(2,1)} %get-tuple-element.28), channel_id=1, source_target_pairs={{0,1},{1,0},{2,3},{3,2},{4,5},{5,4},{6,7},{7,6},{8,9},{9,8},{10,11... | collective-permute-start | bytes 393224 | tf_op jit(solution)/shard_map/ppermute | solution.py:31
  20.8 12.1 %collective-permute-start.1 = (bf16[4,128,128]{2,1,0:T(8,128)(2,1)}, bf16[4,128,128]{2,1,0:T(8,128)(2,1)S(1)}, u32[]{:S(2)}, u32[]{:S(2)}) collective-permute-start(bf16[4,128,128]{2,1,0:T(8,128)(2,1)} %get-tuple-element.29), channel_id=1, source_target_pairs={{0,255},{1,2},{2,1},{3,4},{4,3},{5,6},{6,5},{7,8},{8,7},{9,10},{10... | collective-permute-start | bytes 393224 | tf_op jit(solution)/shard_map/ppermute | solution.py:31
  20.8 12.1 %collective-permute-start.2 = (bf16[4,128,128]{2,1,0:T(8,128)(2,1)}, bf16[4,128,128]{2,1,0:T(8,128)(2,1)S(1)}, u32[]{:S(2)}, u32[]{:S(2)}) collective-permute-start(bf16[4,128,128]{2,1,0:T(8,128)(2,1)} %get-tuple-element.30), channel_id=1, source_target_pairs={{0,2},{1,3},{2,0},{3,1},{4,6},{5,7},{6,4},{7,5},{8,10},{9,11},{10,... | collective-permute-start | bytes 393224 | tf_op jit(solution)/shard_map/ppermute | solution.py:31
  22.1 13.3 %collective-permute-start.3 = (bf16[4,128,128]{2,1,0:T(8,128)(2,1)}, bf16[4,128,128]{2,1,0:T(8,128)(2,1)S(1)}, u32[]{:S(2)}, u32[]{:S(2)}) collective-permute-start(bf16[4,128,128]{2,1,0:T(8,128)(2,1)} %get-tuple-element.31), channel_id=1, source_target_pairs={{0,254},{1,255},{2,4},{3,5},{4,2},{5,3},{6,8},{7,9},{8,6},{9,7},{1... | collective-permute-start | bytes 393224 | tf_op jit(solution)/shard_map/ppermute | solution.py:31
  45.1 5.2 %collective-permute-start.4 = (bf16[128,8,128]{2,1,0:T(8,128)(2,1)}, bf16[128,8,128]{2,1,0:T(8,128)(2,1)S(1)}, u32[]{:S(2)}, u32[]{:S(2)}) collective-permute-start(bf16[128,8,128]{2,1,0:T(8,128)(2,1)} %get-tuple-element.37), channel_id=1, source_target_pairs={{0,1},{1,0},{2,3},{3,2},{4,5},{5,4},{6,7},{7,6},{8,9},{9,8},{10,11... | collective-permute-start | bytes 786440 | tf_op jit(solution)/shard_map/ppermute | solution.py:31
  48.7 1.6 %collective-permute-start.5 = (bf16[4,128,128]{2,1,0:T(8,128)(2,1)}, bf16[4,128,128]{2,1,0:T(8,128)(2,1)S(1)}, u32[]{:S(2)}, u32[]{:S(2)}) collective-permute-start(bf16[4,128,128]{2,1,0:T(8,128)(2,1)} %get-tuple-element.38), channel_id=1, source_target_pairs={{0,1},{1,0},{2,3},{3,2},{4,5},{5,4},{6,7},{7,6},{8,9},{9,8},{10,11... | collective-permute-start | bytes 393224 | tf_op jit(solution)/shard_map/ppermute | solution.py:31
  52.3 23.9 %all-to-all-start.1 = ((bf16[128,8,128]{2,1,0:T(8,128)(2,1)}), bf16[128,8,128]{2,1,0:T(8,128)(2,1)S(1)}, u32[]{:S(2)}, u32[]{:S(2)}) async-start(bf16[128,8,128]{2,1,0:T(8,128)(2,1)} %get-tuple-element.41), calls=%async_computation.1 | async-start | bytes 524288 | tf_op jit(solution)/shard_map/all_to_all | solution.py:620
  58.5 14.8 %collective-permute-start.7 = (bf16[8,128,128]{2,1,0:T(8,128)(2,1)}, bf16[8,128,128]{2,1,0:T(8,128)(2,1)S(1)}, u32[]{:S(2)}, u32[]{:S(2)}) collective-permute-start(bf16[8,128,128]{2,1,0:T(8,128)(2,1)} %get-tuple-element.43), channel_id=1, source_target_pairs={{0,2},{1,3},{2,0},{3,1},{4,6},{5,7},{6,4},{7,5},{8,10},{9,11},{10,... | collective-permute-start | bytes 786440 | tf_op jit(solution)/shard_map/ppermute | solution.py:31
  59.0 17.2 %collective-permute-start.8 = (bf16[8,128,128]{2,1,0:T(8,128)(2,1)}, bf16[8,128,128]{2,1,0:T(8,128)(2,1)S(1)}, u32[]{:S(2)}, u32[]{:S(2)}) collective-permute-start(bf16[8,128,128]{2,1,0:T(8,128)(2,1)} %get-tuple-element.44), channel_id=1, source_target_pairs={{0,254},{1,255},{2,4},{3,5},{4,2},{5,3},{6,8},{7,9},{8,6},{9,7},{1... | collective-permute-start | bytes 786440 | tf_op jit(solution)/shard_map/ppermute | solution.py:31
  66.5 6.7 %collective-permute-start.6 = (bf16[4,128,128]{2,1,0:T(8,128)(2,1)}, bf16[4,128,128]{2,1,0:T(8,128)(2,1)S(1)}, u32[]{:S(2)}, u32[]{:S(2)}) collective-permute-start(bf16[4,128,128]{2,1,0:T(8,128)(2,1)} %get-tuple-element.42), channel_id=1, source_target_pairs={{0,1},{1,0},{2,3},{3,2},{4,5},{5,4},{6,7},{7,6},{8,9},{9,8},{10,11... | collective-permute-start | bytes 393224 | tf_op jit(solution)/shard_map/ppermute | solution.py:31
